TPU v7x, 32 devices: a whole 2x2x4 slice. The times are simulated.
32 devices in a mesh: segment: 4 (over y, x), ctx: 4 (over z), tp: 2 (over core).
Axes of the slice: x: 2, y: 2, z: 4, core: 2. Of those that a mesh axis runs over, the one named last changes fastest.
Arguments:
- mamba_input: bfloat16 [4, 512, 8192], P('segment', 'ctx', 'tp'), may hold values from -13 to 13
- mamba_gate: bfloat16 [4, 512, 8192], P('segment', 'ctx', 'tp'), may hold values from -6 to 6
- step_size: bfloat16 [4, 512, 128], P('segment', 'ctx', 'tp'), may hold values from 0 to 2, as said below
- state_maps: bfloat16 [4, 512, 256], P('segment', 'ctx'), may hold values from -3 to 3
- decay_rate: float32 [128], P('tp'), may hold values from 0.5 to 2
- skip_gain: float32 [128], P('tp'), may hold values from 0.5 to 1.5
- norm_gain: float32 [8192], P('tp'), may hold values from 0.1 to 1.9
- queries: bfloat16 [4, 512, 8192], P('segment', 'ctx', 'tp'), may hold values from -155 to 154
- keys: bfloat16 [4, 512, 1024], P('segment', 'ctx', 'tp'), may hold values from -5 to 5
- values: bfloat16 [4, 512, 1024], P('segment', 'ctx', 'tp'), may hold values from -6 to 6
- source_len: int32 [4], P('segment'), may hold values from 204 to 459
Outputs:
- mamba_handed: bfloat16 [4, 512, 8192], P('segment', 'ctx', 'tp')
- attention_handed: bfloat16 [4, 512, 8192], P('segment', 'ctx', 'tp')
Inputs may be any that keep to these rules, and one draw needn't show every extreme that they name: `step_size`: positive.
All inputs are finite; a program needn't handle non-finite values.
Results may differ from a plain program's by a relative error of at most 0.0095.
Values may be sent and summed in bfloat16 or wider, within the bound.
No kernel may reach another device: no remote copies, remote signals or barrier semaphores. Data moves between devices by JAX's collectives and lax.ppermute only.
A program may use at most 320 MiB of HBM per device.

v0:
```python
import math

import jax
import jax.numpy as jnp
from jax import lax
from jax.sharding import PartitionSpec as P

QUERY_HEADS = 64
KEY_VALUE_HEADS = 8
HEAD_WIDTH = 128
NST = 128
EM = 8192
HP = 64
BLOCK_LEN = 128


precise = lax.Precision.HIGHEST


def from_behind(array, axis, by):
    size = lax.axis_size(axis)
    return lax.ppermute(array, axis, [(i, (i + by) % size) for i in range(size)])


def join_states(earlier, later):
    return (earlier[0] + later[0], jnp.exp(later[0])[..., None, None] * earlier[1] + later[1])


def scan_blocks(mixer_in, step_in, maps_in, speed_collection, skips):
    tok_rows = mixer_in.shape[0]
    head_count = step_in.shape[1]
    block_len = min(BLOCK_LEN, tok_rows)
    blocks = tok_rows // block_len
    step_float = step_in.astype(jnp.float32).reshape(blocks, block_len, head_count)
    log_decay = -speed_collection[None, None, :] * step_float
    cum_log = jnp.cumsum(log_decay, axis=1)
    x_float = mixer_in.astype(jnp.float32).reshape(blocks, block_len, head_count, HP)
    b_float = maps_in[:, :NST].astype(jnp.float32).reshape(blocks, block_len, NST)
    c_float = maps_in[:, NST:].astype(jnp.float32).reshape(blocks, block_len, NST)
    gram = jnp.einsum("cin,cjn->cij", c_float, b_float, precision=precise)
    lower_tri = (jnp.arange(block_len)[:, None] >= jnp.arange(block_len)[None, :])[None, :, :, None]
    differ = cum_log[:, :, None, :] - cum_log[:, None, :, :]
    decay = jnp.where(lower_tri, jnp.exp(jnp.where(lower_tri, differ, 0.0)), 0.0)
    weights = gram[..., None] * decay * step_float[:, None, :, :]
    inner_out = jnp.einsum("cijh,cjhp->cihp", weights, x_float, precision=precise)
    tail_decay = jnp.exp(cum_log[:, -1:, :] - cum_log) * step_float
    block_states = jnp.einsum("cjh,cjn,cjhp->chnp", tail_decay, b_float, x_float, precision=precise)
    block_logs = cum_log[:, -1, :]
    inc_logs, inc_states = lax.associative_scan(join_states, (block_logs, block_states), axis=0)
    entering = jnp.concatenate([jnp.zeros_like(block_states[:1]), inc_states[:-1]], axis=0)
    enter_logs = jnp.concatenate([jnp.zeros_like(block_logs[:1]), inc_logs[:-1]], axis=0)
    outer_out = jnp.exp(cum_log)[..., None] * jnp.einsum(
        "cin,chnp->cihp", c_float, entering, precision=precise
    )
    mixed = inner_out + outer_out + skips[None, None, :, None] * x_float
    cum_block = (cum_log + enter_logs[:, None, :]).reshape(tok_rows, head_count)
    return (mixed.reshape(tok_rows, head_count, HP), inc_states[-1], inc_logs[-1], cum_block)


def on_device(
    mamba_input,
    mamba_gate,
    step_size,
    state_maps,
    decay_rate,
    skip_gain,
    norm_gain,
    queries,
    keys,
    values,
    source_len,
):
    mixer_in = mamba_input[0]
    gate_in = mamba_gate[0]
    step_in = step_size[0]
    maps_in = state_maps[0]
    tok_rows = mixer_in.shape[0]
    ctx_index = lax.axis_index("ctx")
    chan_rows, chan_steps = (
        lax.all_to_all(mixer_in, "ctx", split_axis=1, concat_axis=0, tiled=True),
        lax.all_to_all(step_in, "ctx", split_axis=1, concat_axis=0, tiled=True),
    )
    all_maps = lax.all_gather(maps_in, "ctx", axis=0, tiled=True)
    sub_heads = chan_steps.shape[1]
    rate_sub = lax.dynamic_slice_in_dim(decay_rate, ctx_index * sub_heads, sub_heads)
    skip_sub = lax.dynamic_slice_in_dim(skip_gain, ctx_index * sub_heads, sub_heads)
    chan_out, _, _, _ = scan_blocks(chan_rows, chan_steps, all_maps, rate_sub, skip_sub)
    chan_out = chan_out.reshape(chan_rows.shape[0], sub_heads * HP).astype(jnp.bfloat16)
    raw = lax.all_to_all(chan_out, "ctx", split_axis=0, concat_axis=1, tiled=True)
    gated = raw.astype(jnp.float32) * jax.nn.silu(gate_in.astype(jnp.float32))
    square_sums = lax.psum(jnp.sum(gated * gated, axis=-1), "tp")
    mean_sq = square_sums / EM
    mamba_out = (gated * lax.rsqrt(mean_sq + 1e-05)[:, None] * norm_gain[None, :]).astype(
        jnp.bfloat16
    )
    query_in = queries[0]
    kv_local = keys.shape[2] // HEAD_WIDTH
    group_width = QUERY_HEADS // KEY_VALUE_HEADS
    query_head_rows = query_in.reshape(tok_rows, kv_local, group_width, HEAD_WIDTH)
    source = source_len[0]
    query_pos = ctx_index * tok_rows + jnp.arange(tok_rows, dtype=jnp.int32)
    scale = 1.0 / math.sqrt(HEAD_WIDTH)
    start_max = jnp.full((kv_local, group_width, tok_rows), -1e30, jnp.float32)
    key_piece = lax.all_gather(keys[0], "ctx", axis=0, tiled=True)
    value_piece = lax.all_gather(values[0], "ctx", axis=0, tiled=True)
    piece_rows = key_piece.shape[0]
    key_head_rows = key_piece.reshape(piece_rows, kv_local, HEAD_WIDTH)
    value_head_rows = value_piece.reshape(piece_rows, kv_local, HEAD_WIDTH)
    key_pos = jnp.arange(piece_rows, dtype=jnp.int32)
    visible = (key_pos[None, :] <= query_pos[:, None]) | (key_pos[None, :] < source)
    scores = (
        jnp.einsum(
            "tkgd,skd->kgts", query_head_rows, key_head_rows, preferred_element_type=jnp.float32
        )
        * scale
    )
    scores = jnp.where(visible[None, None], scores, -jnp.inf)
    new_max = jnp.maximum(start_max, jnp.max(scores, axis=-1))
    weights = jnp.exp(scores - new_max[..., None])
    new_total = jnp.sum(weights, axis=-1)
    product = jnp.einsum(
        "kgts,skd->kgtd",
        weights.astype(jnp.bfloat16),
        value_head_rows,
        preferred_element_type=jnp.float32,
    )
    attention_out = (
        (product / new_total[..., None])
        .transpose(2, 0, 1, 3)
        .reshape(tok_rows, kv_local * group_width * HEAD_WIDTH)
        .astype(jnp.bfloat16)
    )
    mamba_next, attention_next = from_behind((mamba_out, attention_out), "segment", 1)
    return (mamba_next[None], attention_next[None])


def solution(mesh):
    placed = (
        P("segment", "ctx", "tp"),
        P("segment", "ctx", "tp"),
        P("segment", "ctx", "tp"),
        P("segment", "ctx", None),
        P("tp"),
        P("tp"),
        P("tp"),
        P("segment", "ctx", "tp"),
        P("segment", "ctx", "tp"),
        P("segment", "ctx", "tp"),
        P("segment"),
    )
    return jax.shard_map(
        on_device,
        mesh=mesh,
        in_specs=placed,
        out_specs=(P("segment", "ctx", "tp"), P("segment", "ctx", "tp")),
        check_vma=False,
    )
```

profile of v0, /device:TPU:0, one launch (start us, length us, event | category | flops | bytes accessed | tf_op | source)
XLA Modules:
  0.0 210.7 jit_solution(2879283660547346659)
XLA Ops:
  0.6 6.5 %all-to-all-start = ((bf16[128,4,16]{0,2,1:T(8,128)(2,1)}), bf16[128,4,16]{0,2,1:T(8,128)(2,1)S(1)}, u32[]{:S(2)}, u32[]{:S(2)}) async-start(bf16[128,4,16]{0,2,1:T(8,128)(2,1)} %bitcast.128), calls=%async_computation | async-start | bytes 32768 | tf_op jit(solution)/shard_map/all_to_all | solution.py:81
  7.7 14.7 %all-gather = bf16[1,512,256]{2,1,0:T(8,128)(2,1)S(1)} all-gather(bf16[1,128,256]{2,1,0:T(8,128)(2,1)} %param.14), channel_id=2, replica_groups=mesh['segment'=4,'ctx'=4,'tp'=2] {'ctx'}, dimensions={1}, use_global_device_ids=true | all-gather | bytes 327680 | tf_op jit(solution)/shard_map/all_gather | solution.py:83
  23.1 1.4 copy.69
  24.7 14.7 %all-gather.1 = bf16[1,512,512]{1,2,0:T(8,128)(2,1)S(1)} all-gather(bf16[1,128,512]{1,2,0:T(8,128)(2,1)S(1)} %copy.52), channel_id=3, replica_groups=mesh['segment'=4,'ctx'=4,'tp'=2] {'ctx'}, dimensions={1}, use_global_device_ids=true | all-gather | bytes 655360 | tf_op jit(solution)/shard_map/all_gather | solution.py:104
  40.5 4.9 %fusion.2 = (f32[4,8,128]{2,1,0:T(8,128)S(1)}, f32[4,512,128,8]{2,1,3,0:T(8,128)}) fusion(pred[128,512]{0,1:T(8,128)(4,1)S(1)} %fusion.46, bf16[512,4,128,1]{0,2,3,1:T(8,128)(2,1)S(1)} %bitcast.114, bf16[128,4,8,128]{3,2,1,0:T(8,128)(2,1)S(1)} %bitcast.112), kind=kOutput, calls=%fused_computation.4 | convolution fusion | flops 543158272 | bytes 10043392 | tf_op jit(solution)/shard_map/tkgd,skd->kgts/dot_general | solution.py:112
  45.5 1.3 copy.64
  47.4 4.2 %all-to-all-start.1 = ((bf16[128,4,1024]{0,2,1:T(8,128)(2,1)}), bf16[128,4,1024]{0,2,1:T(8,128)(2,1)S(1)}, u32[]{:S(2)}, u32[]{:S(2)}) async-start(bf16[128,4,1024]{0,2,1:T(8,128)(2,1)} %bitcast.6), calls=%async_computation.1 | async-start | bytes 2097152 | tf_op jit(solution)/shard_map/all_to_all | solution.py:80
  55.3 16.3 %all-to-all-done.1 = bf16[128,4,1024]{0,2,1:T(8,128)(2,1)S(1)} async-done(((bf16[128,4,1024]{0,2,1:T(8,128)(2,1)}), bf16[128,4,1024]{0,2,1:T(8,128)(2,1)S(1)}, u32[]{:S(2)}, u32[]{:S(2)}) %all-to-all-start.1) | async-done | bytes 1048608 | tf_op jit(solution)/shard_map/all_to_all | solution.py:80
  71.5 1.2 fusion.36
  74.4 1.1 pad_add_fusion
  75.5 16.7 %pad.37 = f32[4,16,128,64]{2,3,1,0:T(8,128)} pad(f32[2,16,128,64]{2,3,1,0:T(8,128)} %pad_add_fusion, f32[]{:T(128)} %constant.9.clone.1), padding=1_0_1x0_0_0x0_0_0x0_0_0 | pad | bytes 3145732
  92.2 1.2 fusion.51
  93.4 1.1 pad_maximum_fusion
  94.5 12.3 %pad.21 = f32[3,16,128,64]{2,3,1,0:T(8,128)S(1)} pad(f32[2,16,128,64]{2,3,1,0:T(8,128)} %pad_maximum_fusion, f32[]{:T(128)} %constant.9.clone.1), padding=0_0_1x0_0_0x0_0_0x0_0_0 | pad | bytes 2621444 | tf_op jit(solution)/shard_map/slice | solution.py:50
  106.9 5.0 %fusion.8 = f32[4,16,128,64]{2,3,1,0:T(8,128)S(1)} fusion(bf16[4,128,16,64]{1,3,2,0:T(8,128)(2,1)S(1)} %bitcast.108, f32[4,128,16]{1,2,0:T(8,128)S(1)} %copy-done.8, f32[4,128,16]{1,2,0:T(8,128)S(1)} %copy-done.7, f32[4,128,128]{2,1,0:T(8,128)S(1)} %copy-done.4, pred[128,128]{1,0:T(8,128)(4,1)S(1)} %copy-done.10), kind=kOutput, calls=%fused_computation.9 | convolution fusion | flops 810549248 | bytes 3489792 | tf_op jit(solution)/shard_map/cijh,cjhp->cihp/dot_general | solution.py:45
  111.9 2.3 %fusion.18 = bf16[4,128,16,64]{1,3,2,0:T(8,128)(2,1)} fusion(bf16[4,128,16,64]{1,3,2,0:T(8,128)(2,1)S(1)} %bitcast.109, f32[4,16,128,64]{2,3,1,0:T(8,128)S(1)} %fusion.8, bf16[4,128,128,1]{2,1,3,0:T(8,128)(2,1)S(1)} %bitcast.116, f32[3,16,128,64]{2,3,1,0:T(8,128)S(1)} %pad.21, f32[16]{0:T(128)S(1)} %copy-done.11, f32[4,128,16]{1,2,0:T(8,128)S(1)} %copy.47, ...), kind=kOutput, calls=%fused_computation.21 | convolution fusion | flops 607518720 | bytes 7504384 | tf_op jit(solution)/shard_map/cin,chnp->cihp/dot_general | solution.py:52
  114.1 3.6 %all-to-all-start.2 = ((bf16[4,128,1024]{1,2,0:T(8,128)(2,1)}), bf16[4,128,1024]{1,2,0:T(8,128)(2,1)S(1)}, u32[]{:S(2)}, u32[]{:S(2)}) async-start(bf16[4,128,1024]{1,2,0:T(8,128)(2,1)} %bitcast.113), calls=%async_computation.2 | async-start | bytes 2097152 | tf_op jit(solution)/shard_map/all_to_all | solution.py:89
  117.8 32.9 %all-gather.2 = bf16[1,512,512]{2,1,0:T(8,128)(2,1)S(1)} all-gather(bf16[1,128,512]{2,1,0:T(8,128)(2,1)S(1)} %copy-done.5), channel_id=4, replica_groups=mesh['segment'=4,'ctx'=4,'tp'=2] {'ctx'}, dimensions={1}, use_global_device_ids=true | all-gather | bytes 655360 | tf_op jit(solution)/shard_map/all_gather | solution.py:105
  150.9 5.1 %fusion = f32[4,8,128]{2,1,0:T(8,128)S(1)} fusion(f32[4,512,128,8]{2,1,3,0:T(8,128)} %get-tuple-element.13, f32[4,8,128]{2,1,0:T(8,128)S(1)} %broadcast_maximum_fusion, pred[128,512]{0,1:T(8,128)(4,1)S(1)} %fusion.46), kind=kLoop, calls=%fused_computation.2 | loop fusion | flops 8384512 | bytes 8486912 | tf_op jit(solution)/shard_map/reduce_sum | solution.py:120
  156.0 5.5 %fusion.19 = bf16[128,4,8,128]{0,3,2,1:T(8,128)(2,1)S(1)} fusion(bf16[512,4,128,1]{0,2,3,1:T(8,128)(2,1)S(1)} %bitcast.123, f32[4,512,128,8]{2,1,3,0:T(8,128)} %get-tuple-element.13, f32[4,8,128]{2,1,0:T(8,128)S(1)} %broadcast_maximum_fusion, pred[128,512]{0,1:T(8,128)(4,1)S(1)} %fusion.46, f32[128,4,8]{0,2,1:T(8,128)S(1)} %bitcast.127), kind=kOutput, calls=%fused_computation.23 | convolution fusion | flops 546308096 | bytes 10059776 | tf_op jit(solution)/shard_map/kgts,skd->kgtd/dot_general | solution.py:121
  161.5 1.3 copy.57
  162.8 1.5 collective-permute-start.1
  164.3 1.5 copy.68
  165.8 1.5 convert_element_type.78
  167.3 2.9 %copy.65 = f32[128,4096]{1,0:T(8,128)} copy(f32[128,4096]{0,1:T(8,128)} %bitcast.111) | data formatting | bytes 4194304 | tf_op jit(solution)/shard_map/convert_element_type | solution.py:90
  170.9 2.5 %psum.7 = f32[128]{0:T(128)S(1)} all-reduce(f32[128]{0:T(128)S(1)} %fusion.27), channel_id=1, replica_groups=mesh['segment'=4,'ctx'=4,'tp'=2] {'tp'}, use_global_device_ids=true, to_apply=%region_2.3 | all-reduce | flops 128 | bytes 1024 | tf_op jit(solution)/shard_map/psum | solution.py:91
  173.4 2.6 %fusion.34 = bf16[128,4096]{1,0:T(8,128)(2,1)S(1)} fusion(f32[128,4096]{1,0:T(8,128)} %copy.65, f32[4096]{0:T(1024)S(1)} %copy-done.9, f32[128]{0:T(128)S(1)} %add_rsqrt_fusion, bf16[1,128,4096]{2,1,0:T(8,128)(2,1)} %param.12), kind=kLoop, calls=%fused_computation.42 | loop fusion | flops 4718592 | bytes 4211200 | tf_op jit(solution)/shard_map/convert_element_type | solution.py:93
  176.0 1.5 collective-permute-start
  177.5 12.6 %collective-permute-done.1 = bf16[128,4096]{1,0:T(8,128)(2,1)} collective-permute-done((bf16[128,4096]{1,0:T(8,128)(2,1)}, bf16[128,4096]{1,0:T(8,128)(2,1)}, u32[]{:S(2)}, u32[]{:S(2)}) %collective-permute-start.1) | collective-permute-done | bytes 1048608 | tf_op jit(solution)/shard_map/ppermute | solution.py:22
  190.1 17.4 %collective-permute-done = bf16[128,4096]{1,0:T(8,128)(2,1)S(1)} collective-permute-done((bf16[128,4096]{1,0:T(8,128)(2,1)S(1)}, bf16[128,4096]{1,0:T(8,128)(2,1)S(1)}, u32[]{:S(2)}, u32[]{:S(2)}) %collective-permute-start) | collective-permute-done | bytes 1048608 | tf_op jit(solution)/shard_map/ppermute | solution.py:22
  207.5 1.0 copy.77
  208.4 2.3 %copy.78 = bf16[1,128,4096]{2,1,0:T(8,128)(2,1)} copy(bf16[1,128,4096]{2,1,0:T(8,128)(2,1)} %bitcast.35) | data formatting | bytes 2097152
  (65 shorter events, 8.8 us)
Async XLA Ops:
  0.6 23.9 %copy-start.6 = (bf16[1,128,512]{2,1,0:T(8,128)(2,1)S(1)}, bf16[1,128,512]{2,1,0:T(8,128)(2,1)}, u32[]{:S(2)}) copy-start(bf16[1,128,512]{2,1,0:T(8,128)(2,1)} %param.19) | copy-start | bytes 393220
  0.6 46.7 %all-to-all-start = ((bf16[128,4,16]{0,2,1:T(8,128)(2,1)}), bf16[128,4,16]{0,2,1:T(8,128)(2,1)S(1)}, u32[]{:S(2)}, u32[]{:S(2)}) async-start(bf16[128,4,16]{0,2,1:T(8,128)(2,1)} %bitcast.128), calls=%async_computation | async-start | bytes 32768 | tf_op jit(solution)/shard_map/all_to_all | solution.py:81
  40.5 4.9 %copy-start.15 = (f32[64]{0:T(128)S(1)}, f32[64]{0:T(128)}, u32[]{:S(2)}) copy-start(f32[64]{0:T(128)} %param.15) | copy-start | bytes 772
  40.5 5.0 %copy-start.3 = (bf16[1,128,4096]{2,1,0:T(8,128)(2,1)S(1)}, bf16[1,128,4096]{2,1,0:T(8,128)(2,1)}, u32[]{:S(2)}) copy-start(bf16[1,128,4096]{2,1,0:T(8,128)(2,1)} %param.11) | copy-start | bytes 3145732
  45.4 1.4 copy-start.16
  47.4 24.2 %all-to-all-start.1 = ((bf16[128,4,1024]{0,2,1:T(8,128)(2,1)}), bf16[128,4,1024]{0,2,1:T(8,128)(2,1)S(1)}, u32[]{:S(2)}, u32[]{:S(2)}) async-start(bf16[128,4,1024]{0,2,1:T(8,128)(2,1)} %bitcast.6), calls=%async_computation.1 | async-start | bytes 2097152 | tf_op jit(solution)/shard_map/all_to_all | solution.py:80
  71.5 1.2 copy-start.12
  72.7 0.6 copy-start.13
  73.4 0.8 copy-start.1
  73.4 1.0 copy-start.2
  75.5 16.7 %copy-start.14 = (f32[16]{0:T(128)S(1)}, f32[16]{0:T(128)}, u32[]{:S(2)}) copy-start(f32[16]{0:T(128)} %fusion.47) | copy-start | bytes 196
  93.3 13.5 %copy-start.4 = (f32[4,128,128]{2,1,0:T(8,128)S(1)}, f32[4,128,128]{2,1,0:T(8,128)}, u32[]{:S(2)}) copy-start(f32[4,128,128]{2,1,0:T(8,128)} %fusion.57) | copy-start | bytes 786436
  93.4 13.5 %copy-start.7 = (f32[4,128,16]{1,2,0:T(8,128)S(1)}, f32[4,128,16]{1,2,0:T(8,128)}, u32[]{:S(2)}) copy-start(f32[4,128,16]{1,2,0:T(8,128)} %copy.43) | copy-start | bytes 98308
  93.4 13.5 %copy-start.8 = (f32[4,128,16]{1,2,0:T(8,128)S(1)}, f32[4,128,16]{1,2,0:T(8,128)}, u32[]{:S(2)}) copy-start(f32[4,128,16]{1,2,0:T(8,128)} %convert_bitcast_fusion) | copy-start | bytes 98308
  93.4 13.5 %copy-start.10 = (pred[128,128]{1,0:T(8,128)(4,1)S(1)}, pred[128,128]{1,0:T(8,128)(4,1)}, u32[]{:S(2)}) copy-start(pred[128,128]{1,0:T(8,128)(4,1)} %iota_compare_fusion.1) | copy-start | bytes 49156
  106.8 5.0 %copy-start = (f32[4,16,128,64]{2,3,1,0:T(8,128)S(1)}, f32[4,16,128,64]{2,3,1,0:T(8,128)}, u32[]{:S(2)}) copy-start(f32[4,16,128,64]{2,3,1,0:T(8,128)} %pad.37) | copy-start | bytes 6291460
  106.8 5.0 %copy-start.11 = (f32[16]{0:T(128)S(1)}, f32[16]{0:T(128)}, u32[]{:S(2)}) copy-start(f32[16]{0:T(128)} %dynamic_slice.7) | copy-start | bytes 196
  114.1 3.7 %copy-start.5 = (bf16[1,128,512]{2,1,0:T(8,128)(2,1)S(1)}, bf16[1,128,512]{2,1,0:T(8,128)(2,1)}, u32[]{:S(2)}) copy-start(bf16[1,128,512]{2,1,0:T(8,128)(2,1)} %param.20) | copy-start | bytes 393220
  114.1 51.6 %all-to-all-start.2 = ((bf16[4,128,1024]{1,2,0:T(8,128)(2,1)}), bf16[4,128,1024]{1,2,0:T(8,128)(2,1)S(1)}, u32[]{:S(2)}, u32[]{:S(2)}) async-start(bf16[4,128,1024]{1,2,0:T(8,128)(2,1)} %bitcast.113), calls=%async_computation.2 | async-start | bytes 2097152 | tf_op jit(solution)/shard_map/all_to_all | solution.py:89
  162.8 27.3 %collective-permute-start.1 = (bf16[128,4096]{1,0:T(8,128)(2,1)}, bf16[128,4096]{1,0:T(8,128)(2,1)}, u32[]{:S(2)}, u32[]{:S(2)}) collective-permute-start(bf16[128,4096]{1,0:T(8,128)(2,1)} %copy.57), channel_id=1, source_target_pairs={{0,8},{8,16},{16,24},{24,0},{1,9},{9,17},{17,25},{25,1},{2,10},{10... | collective-permute-start | bytes 3145736 | tf_op jit(solution)/shard_map/ppermute | solution.py:22
  170.2 3.2 %copy-start.9 = (f32[4096]{0:T(1024)S(1)}, f32[4096]{0:T(1024)}, u32[]{:S(2)}) copy-start(f32[4096]{0:T(1024)} %param.17) | copy-start | bytes 49156
  176.0 31.5 %collective-permute-start = (bf16[128,4096]{1,0:T(8,128)(2,1)S(1)}, bf16[128,4096]{1,0:T(8,128)(2,1)S(1)}, u32[]{:S(2)}, u32[]{:S(2)}) collective-permute-start(bf16[128,4096]{1,0:T(8,128)(2,1)S(1)} %fusion.34), channel_id=1, source_target_pairs={{0,8},{8,16},{16,24},{24,0},{1,9},{9,17},{17,25},{25,1},{2,10},{10... | collective-permute-start | bytes 3145736 | tf_op jit(solution)/shard_map/ppermute | solution.py:22
where the time goes:
time: 214 us; the launch traced here: 211 us
  blocking collectives  64.8 us (30%)
  waiting for transfers between devices  46.2 us (22%)
  local copies, waits for them, and re-layouts  45.2 us (21%)
  matrix products  19.8 us (9%)
  starting transfers between devices  17.3 us (8%)
  other arithmetic  15.9 us (7%)
    all_gather x1, blocking collectives, on_device(): value_piece = lax.all_gather(values[0], 'ctx', axis=0, tiled=True)  32.9 us
    ppermute x2, waiting for transfers between devices, from_behind(): lax.ppermute(array, axis, [(i, (i + by) % size) for i in range(size)])  29.9 us
    unnamed x39, local copies, waits for them, and re-layouts  22.9 us
    all_to_all x1, waiting for transfers between devices, on_device(): lax.all_to_all(mixer_in, 'ctx', split_axis=1, concat_axis=0, tiled=True)  16.3 us
    all_gather x1, blocking collectives, on_device(): key_piece = lax.all_gather(keys[0], 'ctx', axis=0, tiled=True)  14.7 us
    all_gather x1, blocking collectives, on_device(): all_maps = lax.all_gather(maps_in, 'ctx', axis=0, tiled=True)  14.7 us
    slice x1, local copies, waits for them, and re-layouts, scan_blocks(): inc_states[:-1]  12.3 us
    all_to_all x1, starting transfers between devices, on_device(): lax.all_to_all(step_in, 'ctx', split_axis=1, concat_axis=0, tiled=True)  6.46 us
  transfers between devices with their start and end apart: 5, of which 3 were waited for; matrix products, arithmetic and copies ran while one was open for 17% of the time, Pallas kernels for 0%

commit v1 on v0

v1 whole, which is shorter than its diff:
```python
import functools
import math

import jax
import jax.numpy as jnp
from jax import lax
from jax.experimental import pallas as pl
from jax.experimental.pallas import tpu as pltpu
from jax.sharding import PartitionSpec as P

QUERY_HEADS = 64
KEY_VALUE_HEADS = 8
HEAD_WIDTH = 128
NST = 128
HP = 64
GROUP = QUERY_HEADS // KEY_VALUE_HEADS
CHUNKS = 4
VMEM = 40 * 1024 * 1024
HIGH = lax.Precision.HIGHEST


def dot(a, b, dims, precision=None):
    return lax.dot_general(
        a, b, (dims, ((), ())), precision=precision, preferred_element_type=jnp.float32
    )


def call(kernel, out_shape, flops, nbytes, **kw):
    return pl.pallas_call(
        kernel,
        out_shape=out_shape,
        compiler_params=pltpu.CompilerParams(vmem_limit_bytes=VMEM),
        cost_estimate=pl.CostEstimate(flops=flops, bytes_accessed=nbytes, transcendentals=0),
        **kw,
    )


def lower_mask(rows):
    return lax.broadcasted_iota(jnp.int32, (rows, rows), 0) >= lax.broadcasted_iota(
        jnp.int32, (rows, rows), 1
    )


def pair_columns(table, pair, rows):
    lane = lax.broadcasted_iota(jnp.int32, (rows, 2 * HP), 1)
    first = jnp.broadcast_to(table[:, 2 * pair : 2 * pair + 1], (rows, 2 * HP))
    second = jnp.broadcast_to(table[:, 2 * pair + 1 : 2 * pair + 2], (rows, 2 * HP))
    return jnp.where(lane < HP, first, second)


def state_kernel(x_ref, dt_ref, rate_ref, b_ref, state_ref, decay_ref, cum_ref, cum_t_ref, dt_t_ref):
    rows, heads = dt_ref.shape
    width = x_ref.shape[1] // CHUNKS
    lower = lower_mask(rows)
    ones = jnp.where(lower, 1.0, 0.0).astype(jnp.bfloat16)
    eye = jnp.where(
        lax.broadcasted_iota(jnp.int32, (rows, rows), 0)
        == lax.broadcasted_iota(jnp.int32, (rows, rows), 1),
        1.0,
        0.0,
    ).astype(jnp.bfloat16)
    dt = dt_ref[...]
    rate = rate_ref[...]
    cum = -rate * dot(ones, dt, ((1,), (0,)))
    cum_ref[...] = cum
    rate_col = jnp.transpose(jnp.broadcast_to(rate, (8, heads)))[:, :1]
    cum_t_ref[...] = -rate_col * dot(dt, ones, ((0,), (1,)))
    dt_t_ref[...] = dot(dt, eye, ((0,), (0,)))
    total = cum[rows - 1 : rows, :]
    tail = jnp.exp(total - cum) * dt.astype(jnp.float32)
    whole = jnp.exp(total)
    b = b_ref[...]
    for chunk in range(CHUNKS):
        for tile in range(width // 128):
            pair = chunk * (width // 128) + tile
            xs = x_ref[:, pair * 128 : pair * 128 + 128].astype(jnp.float32)
            xw = (xs * pair_columns(tail, pair, rows)).astype(jnp.bfloat16)
            state = dot(b, xw, ((0,), (0,)))
            state_ref[chunk, :, tile * 128 : tile * 128 + 128] = state.astype(state_ref.dtype)
            decay_ref[chunk, :, tile * 128 : tile * 128 + 128] = pair_columns(whole, pair, 1)


def inner_kernel(chunk, x_ref, skip_ref, maps_ref, cum_ref, cum_t_ref, dt_t_ref, out_ref):
    rows = x_ref.shape[0]
    width = x_ref.shape[1]
    gram = dot(maps_ref[:, NST:], maps_ref[:, :NST], ((1,), (1,)))
    gram = jnp.where(lower_mask(rows), gram, 0.0)
    lane = lax.broadcasted_iota(jnp.int32, (rows, 128), 1)
    cum = cum_ref[...]
    skip = skip_ref[...]
    for tile in range(width // 128):
        pair = chunk * (width // 128) + tile
        mixes = []
        for head in (2 * pair, 2 * pair + 1):
            mine = jnp.broadcast_to(cum[:, head : head + 1], (rows, rows))
            theirs = cum_t_ref[head : head + 1, :]
            decay = jnp.exp(jnp.minimum(mine - theirs, 0.0))
            mixes.append((gram * decay * dt_t_ref[head : head + 1, :]).astype(jnp.bfloat16))
        xs = x_ref[:, tile * 128 : tile * 128 + 128]
        zero = jnp.zeros_like(xs)
        stacked = jnp.concatenate(
            [jnp.where(lane < HP, xs, zero), jnp.where(lane < HP, zero, xs)], axis=0
        )
        mixed = dot(jnp.concatenate(mixes, axis=1), stacked, ((1,), (0,)))
        out_ref[:, tile * 128 : tile * 128 + 128] = mixed + pair_columns(
            skip, pair, 1
        ) * xs.astype(jnp.float32)


def gate_kernel(chunk, sources, index_ref, inner_ref, gate_ref, maps_ref, cum_ref, *refs):
    states, (out_ref, sums_ref, enter) = refs[:sources], refs[sources:]
    rows, width = out_ref.shape
    index = index_ref[0]

    @pl.when(index == 0)
    def _():
        enter[...] = jnp.zeros_like(enter)

    for source in range(sources):

        @pl.when(index == source + 1)
        def _(source=source):
            enter[...] = states[source][...].astype(jnp.bfloat16)

    grow = jnp.exp(cum_ref[...])
    outer = dot(maps_ref[:, NST:], enter[...], ((1,), (0,)))
    total = jnp.zeros((rows, 128), jnp.float32)
    for tile in range(width // 128):
        at = slice(tile * 128, tile * 128 + 128)
        pair = chunk * (width // 128) + tile
        raw = inner_ref[:, at] + pair_columns(grow, pair, rows) * outer[:, at]
        raw = raw.astype(jnp.bfloat16).astype(jnp.float32)
        gate = gate_ref[:, at].astype(jnp.float32)
        gated = raw * (gate / (1.0 + jnp.exp(-gate)))
        out_ref[:, at] = gated.astype(jnp.bfloat16)
        total = total + gated * gated
    sums_ref[...] = dot(jnp.ones((8, 128), jnp.float32), total, ((1,), (1,)), HIGH)


def norm_kernel(channels, *refs):
    *chunk_refs, sums_ref, gain_ref, out_ref = refs
    rows = out_ref.shape[0]
    mean = sums_ref[0:1, :] / channels
    scale = jnp.broadcast_to(lax.rsqrt(mean + 1e-05), (rows, rows))
    eye = lax.broadcasted_iota(jnp.int32, (rows, rows), 0) == lax.broadcasted_iota(
        jnp.int32, (rows, rows), 1
    )
    scale = jnp.sum(jnp.where(eye, scale, 0.0), axis=1, keepdims=True)
    at = 0
    for ref in chunk_refs:
        width = ref.shape[1]
        out_ref[:, at : at + width] = (
            ref[...].astype(jnp.float32) * scale * gain_ref[:, at : at + width]
        ).astype(jnp.bfloat16)
        at += width


def attention_kernel(ctx, index_ref, source_ref, q_ref, k_ref, v_ref, out_ref):
    rows = q_ref.shape[0]
    keys = k_ref.shape[0]
    index = index_ref[0]
    source = source_ref[0]
    lane = lax.broadcasted_iota(jnp.int32, (rows, keys), 1)
    owner = index - lane // rows
    owner = jnp.where(owner < 0, owner + ctx, owner)
    key_pos = owner * rows + lane % rows
    query_pos = index * rows + lax.broadcasted_iota(jnp.int32, (rows, keys), 0)
    visible = (key_pos <= query_pos) | (key_pos < source)
    factor = math.log2(math.e) / math.sqrt(HEAD_WIDTH)
    k = k_ref[...]
    v = v_ref[...]
    for head in range(GROUP):
        at = slice(head * HEAD_WIDTH, (head + 1) * HEAD_WIDTH)
        scores = dot(q_ref[:, at], k, ((1,), (1,))) * factor
        scores = jnp.where(visible, scores, -jnp.inf)
        top = jnp.max(scores, axis=1, keepdims=True)
        weights = jnp.exp2(scores - top)
        total = jnp.sum(weights, axis=1, keepdims=True)
        mixed = dot(weights.astype(jnp.bfloat16), v, ((1,), (0,)))
        out_ref[:, at] = (mixed / total).astype(jnp.bfloat16)


def on_device(
    mamba_input,
    mamba_gate,
    step_size,
    state_maps,
    decay_rate,
    skip_gain,
    norm_gain,
    queries,
    keys,
    values,
    source_len,
):
    segments = lax.axis_size("segment")
    ctx = lax.axis_size("ctx")
    tps = lax.axis_size("tp")
    index = lax.axis_index("ctx")
    index_in = index.astype(jnp.int32).reshape(1)
    onward = [(i, (i + 1) % segments) for i in range(segments)]

    def hand(array):
        return lax.ppermute(array, "segment", onward)

    x, gate, dt, maps = mamba_input[0], mamba_gate[0], step_size[0], state_maps[0]
    rows, channels = x.shape
    heads = dt.shape[1]
    width = channels // CHUNKS
    wire = jnp.bfloat16 if ctx <= 8 else jnp.float32
    f32 = jnp.float32

    source = hand(source_len)
    key_values = hand(jnp.concatenate([keys[0], values[0]], axis=1))
    query = hand(queries[0])

    rate = decay_rate.reshape(1, heads)
    skip = skip_gain.reshape(1, heads)
    shape = jax.ShapeDtypeStruct
    states, decays, cum, cum_t, dt_t = call(
        state_kernel,
        (
            shape((CHUNKS, NST, width), wire),
            shape((CHUNKS, 1, width), f32),
            shape((rows, heads), f32),
            shape((heads, rows), f32),
            shape((heads, rows), f32),
        ),
        2 * rows * NST * channels,
        4 * rows * channels,
    )(x, dt, rate, maps[:, :NST])

    chain = [(i, i + 1) for i in range(ctx - 1)]
    arrived = []
    for step in range(CHUNKS + ctx - 2):
        which = jnp.clip(step - index, 0, CHUNKS - 1)
        state = lax.dynamic_index_in_dim(states, which, 0, keepdims=False)
        if step > 0:
            decay = lax.dynamic_index_in_dim(decays, which, 0, keepdims=False)
            state = (arrived[-1].astype(f32) * decay + state.astype(f32)).astype(wire)
        arrived.append(lax.ppermute(state, "ctx", chain))

    pieces = [key_values]
    for distance in range(1, ctx):
        pieces.append(
            lax.ppermute(key_values, "ctx", [(i, (i + distance) % ctx) for i in range(ctx)])
        )
    all_key_values = jnp.concatenate(pieces, axis=0)
    all_rows = ctx * rows
    groups = keys.shape[2] // HEAD_WIDTH
    wide = GROUP * HEAD_WIDTH
    attention = call(
        functools.partial(attention_kernel, ctx),
        shape((rows, groups * wide), jnp.bfloat16),
        4 * rows * groups * wide * all_rows,
        4 * rows * groups * wide,
        grid=(groups,),
        in_specs=[
            pl.BlockSpec(memory_space=pltpu.SMEM),
            pl.BlockSpec(memory_space=pltpu.SMEM),
            pl.BlockSpec((rows, wide), lambda g: (0, g)),
            pl.BlockSpec((all_rows, HEAD_WIDTH), lambda g: (0, g)),
            pl.BlockSpec((all_rows, HEAD_WIDTH), lambda g: (0, g + groups)),
        ],
        out_specs=pl.BlockSpec((rows, wide), lambda g: (0, g)),
    )(index_in, source, query, all_key_values, all_key_values)

    handed = []
    sums = None
    whole = lambda *dims: pl.BlockSpec(dims, lambda i: (0,) * len(dims))
    for chunk in range(CHUNKS):
        block = pl.BlockSpec((rows, width), lambda i, chunk=chunk: (0, chunk))
        inner = call(
            functools.partial(inner_kernel, chunk),
            shape((rows, width), f32),
            2 * rows * rows * width,
            6 * rows * width,
            grid=(1,),
            in_specs=[block, whole(1, heads), whole(rows, 2 * NST), whole(rows, heads)]
            + [whole(heads, rows)] * 2,
            out_specs=whole(rows, width),
        )(x, skip, maps, cum, cum_t, dt_t)
        gated, part = call(
            functools.partial(gate_kernel, chunk, ctx - 1),
            (shape((rows, width), jnp.bfloat16), shape((8, rows), f32)),
            2 * rows * rows * width,
            8 * rows * width,
            grid=(1,),
            in_specs=[
                pl.BlockSpec(memory_space=pltpu.SMEM),
                whole(rows, width),
                block,
                whole(rows, 2 * NST),
                whole(rows, heads),
            ]
            + [whole(NST, width)] * (ctx - 1),
            out_specs=(whole(rows, width), whole(8, rows)),
            scratch_shapes=[pltpu.VMEM((NST, width), jnp.bfloat16)],
        )(index_in, inner, gate, maps, cum, *arrived[chunk : chunk + ctx - 1])
        handed.append(hand(gated))
        sums = part if sums is None else sums + part
    sums = hand(lax.psum(sums, "tp"))
    mamba = call(
        functools.partial(norm_kernel, channels * tps),
        shape((rows, channels), jnp.bfloat16),
        rows * channels,
        4 * rows * channels,
    )(*handed, sums, norm_gain.reshape(1, channels))
    return (mamba[None], attention[None])


def solution(mesh):
    placed = (
        P("segment", "ctx", "tp"),
        P("segment", "ctx", "tp"),
        P("segment", "ctx", "tp"),
        P("segment", "ctx", None),
        P("tp"),
        P("tp"),
        P("tp"),
        P("segment", "ctx", "tp"),
        P("segment", "ctx", "tp"),
        P("segment", "ctx", "tp"),
        P("segment"),
    )
    return jax.shard_map(
        on_device,
        mesh=mesh,
        in_specs=placed,
        out_specs=(P("segment", "ctx", "tp"), P("segment", "ctx", "tp")),
        check_vma=False,
    )
```

time: 214 us -> 99.3 us (0.46)
  the two profiles are of different devices: /device:TPU:0 before, /device:TPU:19 now
where the time goes in v1:
time: 99.3 us; the launch traced here: 98.9 us
  waiting for transfers between devices  33.5 us (34%)
  starting transfers between devices  31.3 us (32%)
  Pallas kernels  20.8 us (21%)
  blocking collectives  8.39 us (8%)
  local copies, waits for them, and re-layouts  3.55 us (4%)
    ppermute x6, waiting for transfers between devices, on_device(): arrived.append(lax.ppermute(state, 'ctx', chain))  21.3 us
    ppermute x6, starting transfers between devices, on_device(): arrived.append(lax.ppermute(state, 'ctx', chain))  19.9 us
    ppermute x3, waiting for transfers between devices, on_device(): lax.ppermute(key_values, 'ctx', [(i, (i + distance) % ctx) for i in range...  12.2 us
    pallas_call x1, Pallas kernels, on_device(): call(functools.partial(attention_kernel, ctx), shape((rows, groups * wide...  10.8 us
    ppermute x8, starting transfers between devices, hand(): return lax.ppermute(array, 'segment', onward)  9.8 us
    psum x1, blocking collectives, on_device(): sums = hand(lax.psum(sums, 'tp'))  8.39 us
    pallas_call x4, Pallas kernels, on_device(): call(functools.partial(gate_kernel, chunk, ctx - 1), (shape((rows, width)...  4.36 us
    unnamed x19, local copies, waits for them, and re-layouts  2.74 us
  transfers between devices with their start and end apart: 17, of which 8 were waited for; matrix products, arithmetic and copies ran while one was open for 0% of the time, Pallas kernels for 18%

profile of v1, /device:TPU:19, one launch (start us, length us, event | category | flops | bytes accessed | tf_op | source)
XLA Modules:
  0.0 98.9 jit_solution(8007677321081871361)
XLA Ops:
  0.6 0.8 copy.13
  1.5 0.8 slice.4.b_ref
  2.2 1.2 %copy-done = bf16[1,128,4096]{2,1,0:T(8,128)(2,1)S(1)} copy-done((bf16[1,128,4096]{2,1,0:T(8,128)(2,1)S(1)}, bf16[1,128,4096]{2,1,0:T(8,128)(2,1)}, u32[]{:S(2)}) %copy-start) | copy-done | bytes 1048600
  4.1 1.8 %shard_map.122 = (bf16[4,128,1024]{2,1,0:T(8,128)(2,1)S(1)}, f32[4,1,1024]{2,1,0:T(1,128)S(1)}, f32[128,64]{1,0:T(8,128)S(1)}, f32[64,128]{1,0:T(8,128)S(1)}, f32[64,128]{1,0:T(8,128)S(1)}) custom-call(bf16[128,4096]{1,0:T(8,128)(2,1)S(1)} %bitcast.35, bf16[128,64]{1,0:T(8,128)(2,1)S(1)} %bitcast.53, f32[1,64]{1,0:T(1,128)S(1)} %bitcast.59, ...), custom_call_target="tpu_custom_call" | custom-call | flops 134217728 | bytes 2097152 | tf_op jit(solution)/shard_map/pallas_call | solution.py:220
  6.0 3.2 %collective-permute-start = (bf16[128,1024]{1,0:T(8,128)(2,1)S(1)}, bf16[128,1024]{1,0:T(8,128)(2,1)S(1)}, u32[]{:S(2)}, u32[]{:S(2)}) collective-permute-start(bf16[128,1024]{1,0:T(8,128)(2,1)S(1)} %dynamic-slice_bitcast_fusion), channel_id=1, source_target_pairs={{0,2},{2,4},{4,6},{1,3},{3,5},{5,7},{8,10},{10,12},{12,14},{9,11},... | collective-permute-start | bytes 786440 | tf_op jit(solution)/shard_map/ppermute | solution.py:241
  9.2 5.8 %collective-permute-done.refs_0_ = bf16[128,1024]{1,0:T(8,128)(2,1)S(1)} collective-permute-done((bf16[128,1024]{1,0:T(8,128)(2,1)S(1)}, bf16[128,1024]{1,0:T(8,128)(2,1)S(1)}, u32[]{:S(2)}, u32[]{:S(2)}) %collective-permute-start) | collective-permute-done | bytes 262176 | tf_op jit(solution)/shard_map/ppermute | solution.py:241
  15.1 3.3 %collective-permute-start.1 = (bf16[128,1024]{1,0:T(8,128)(2,1)S(1)}, bf16[128,1024]{1,0:T(8,128)(2,1)S(1)}, u32[]{:S(2)}, u32[]{:S(2)}) collective-permute-start(bf16[128,1024]{1,0:T(8,128)(2,1)S(1)} %fusion.4), channel_id=1, source_target_pairs={{0,2},{2,4},{4,6},{1,3},{3,5},{5,7},{8,10},{10,12},{12,14},{9,11},... | collective-permute-start | bytes 786440 | tf_op jit(solution)/shard_map/ppermute | solution.py:241
  18.5 4.9 %collective-permute-done.1.refs_1_.refs_0_ = bf16[128,1024]{1,0:T(8,128)(2,1)S(1)} collective-permute-done((bf16[128,1024]{1,0:T(8,128)(2,1)S(1)}, bf16[128,1024]{1,0:T(8,128)(2,1)S(1)}, u32[]{:S(2)}, u32[]{:S(2)}) %collective-permute-start.1) | collective-permute-done | bytes 262176 | tf_op jit(solution)/shard_map/ppermute | solution.py:241
  23.5 3.2 %collective-permute-start.2 = (bf16[128,1024]{1,0:T(8,128)(2,1)S(1)}, bf16[128,1024]{1,0:T(8,128)(2,1)S(1)}, u32[]{:S(2)}, u32[]{:S(2)}) collective-permute-start(bf16[128,1024]{1,0:T(8,128)(2,1)S(1)} %fusion.3), channel_id=1, source_target_pairs={{0,2},{2,4},{4,6},{1,3},{3,5},{5,7},{8,10},{10,12},{12,14},{9,11},... | collective-permute-start | bytes 786440 | tf_op jit(solution)/shard_map/ppermute | solution.py:241
  26.7 3.9 %collective-permute-done.2.refs_2_.refs_1_.refs_0_ = bf16[128,1024]{1,0:T(8,128)(2,1)S(1)} collective-permute-done((bf16[128,1024]{1,0:T(8,128)(2,1)S(1)}, bf16[128,1024]{1,0:T(8,128)(2,1)S(1)}, u32[]{:S(2)}, u32[]{:S(2)}) %collective-permute-start.2) | collective-permute-done | bytes 262176 | tf_op jit(solution)/shard_map/ppermute | solution.py:241
  30.7 3.2 %collective-permute-start.4 = (bf16[128,1024]{1,0:T(8,128)(2,1)S(1)}, bf16[128,1024]{1,0:T(8,128)(2,1)S(1)}, u32[]{:S(2)}, u32[]{:S(2)}) collective-permute-start(bf16[128,1024]{1,0:T(8,128)(2,1)S(1)} %fusion.2), channel_id=1, source_target_pairs={{0,2},{2,4},{4,6},{1,3},{3,5},{5,7},{8,10},{10,12},{12,14},{9,11},... | collective-permute-start | bytes 786440 | tf_op jit(solution)/shard_map/ppermute | solution.py:241
  34.0 1.3 %collective-permute-start.13 = (bf16[128,1024]{1,0:T(8,128)(2,1)S(1)}, bf16[128,1024]{1,0:T(8,128)(2,1)S(1)}, u32[]{:S(2)}, u32[]{:S(2)}) collective-permute-start(bf16[128,1024]{1,0:T(8,128)(2,1)S(1)} %pad_maximum_fusion.1), channel_id=1, source_target_pairs={{0,8},{8,16},{16,24},{24,0},{1,9},{9,17},{17,25},{25,1},{2,10},{10... | collective-permute-start | bytes 786440 | tf_op jit(solution)/shard_map/ppermute | solution.py:204
  35.2 1.2 %collective-permute-start.12 = (bf16[128,4096]{1,0:T(8,128)(2,1)}, bf16[128,4096]{1,0:T(8,128)(2,1)S(1)}, u32[]{:S(2)}, u32[]{:S(2)}) collective-permute-start(bf16[128,4096]{1,0:T(8,128)(2,1)} %bitcast.20), channel_id=1, source_target_pairs={{0,8},{8,16},{16,24},{24,0},{1,9},{9,17},{17,25},{25,1},{2,10},{10... | collective-permute-start | bytes 3145736 | tf_op jit(solution)/shard_map/ppermute | solution.py:204
  36.4 1.3 %collective-permute-done.4.refs_2_.refs_1_.refs_0_ = bf16[128,1024]{1,0:T(8,128)(2,1)S(1)} collective-permute-done((bf16[128,1024]{1,0:T(8,128)(2,1)S(1)}, bf16[128,1024]{1,0:T(8,128)(2,1)S(1)}, u32[]{:S(2)}, u32[]{:S(2)}) %collective-permute-start.4) | collective-permute-done | bytes 262176 | tf_op jit(solution)/shard_map/ppermute | solution.py:241
  37.9 3.2 %collective-permute-start.6 = (bf16[128,1024]{1,0:T(8,128)(2,1)S(1)}, bf16[128,1024]{1,0:T(8,128)(2,1)S(1)}, u32[]{:S(2)}, u32[]{:S(2)}) collective-permute-start(bf16[128,1024]{1,0:T(8,128)(2,1)S(1)} %fusion.1), channel_id=1, source_target_pairs={{0,2},{2,4},{4,6},{1,3},{3,5},{5,7},{8,10},{10,12},{12,14},{9,11},... | collective-permute-start | bytes 786440 | tf_op jit(solution)/shard_map/ppermute | solution.py:241
  41.3 1.3 %collective-permute-start.15 = (bf16[128,1024]{1,0:T(8,128)(2,1)S(1)}, bf16[128,1024]{1,0:T(8,128)(2,1)S(1)}, u32[]{:S(2)}, u32[]{:S(2)}) collective-permute-start(bf16[128,1024]{1,0:T(8,128)(2,1)S(1)} %collective-permute-done.13), channel_id=1, source_target_pairs={{0,4},{2,6},{4,0},{6,2},{1,5},{3,7},{5,1},{7,3},{8,12},{10,14},{12... | collective-permute-start | bytes 786440 | tf_op jit(solution)/shard_map/ppermute | solution.py:246
  42.7 5.1 %collective-permute-done.6.refs_2_.refs_1_ = bf16[128,1024]{1,0:T(8,128)(2,1)S(1)} collective-permute-done((bf16[128,1024]{1,0:T(8,128)(2,1)S(1)}, bf16[128,1024]{1,0:T(8,128)(2,1)S(1)}, u32[]{:S(2)}, u32[]{:S(2)}) %collective-permute-start.6) | collective-permute-done | bytes 262176 | tf_op jit(solution)/shard_map/ppermute | solution.py:241
  47.9 3.7 %collective-permute-start.8 = (bf16[128,1024]{1,0:T(8,128)(2,1)S(1)}, bf16[128,1024]{1,0:T(8,128)(2,1)S(1)}, u32[]{:S(2)}, u32[]{:S(2)}) collective-permute-start(bf16[128,1024]{1,0:T(8,128)(2,1)S(1)} %fusion), channel_id=1, source_target_pairs={{0,2},{2,4},{4,6},{1,3},{3,5},{5,7},{8,10},{10,12},{12,14},{9,11},... | collective-permute-start | bytes 786440 | tf_op jit(solution)/shard_map/ppermute | solution.py:241
  54.0 1.2 %collective-permute-start.11 = (s32[1]{0:T(128)}, s32[1]{0:T(128)}, u32[]{:S(2)}, u32[]{:S(2)}) collective-permute-start(s32[1]{0:T(128)} %param.21), channel_id=1, source_target_pairs={{0,8},{8,16},{16,24},{24,0},{1,9},{9,17},{17,25},{25,1},{2,10},{10... | collective-permute-start | bytes 20 | tf_op jit(solution)/shard_map/ppermute | solution.py:204
  55.2 5.0 %collective-permute-done.15 = bf16[128,1024]{1,0:T(8,128)(2,1)S(1)} collective-permute-done((bf16[128,1024]{1,0:T(8,128)(2,1)S(1)}, bf16[128,1024]{1,0:T(8,128)(2,1)S(1)}, u32[]{:S(2)}, u32[]{:S(2)}) %collective-permute-start.15) | collective-permute-done | bytes 262176 | tf_op jit(solution)/shard_map/ppermute | solution.py:246
  60.2 7.2 %collective-permute-done.14 = bf16[128,1024]{1,0:T(8,128)(2,1)S(1)} collective-permute-done((bf16[128,1024]{1,0:T(8,128)(2,1)S(1)}, bf16[128,1024]{1,0:T(8,128)(2,1)S(1)}, u32[]{:S(2)}, u32[]{:S(2)}) %collective-permute-start.14) | collective-permute-done | bytes 262176 | tf_op jit(solution)/shard_map/ppermute | solution.py:246
  68.2 1.3 %collective-permute-start.3 = (bf16[128,1024]{1,0:T(8,128)(2,1)S(1)}, bf16[128,1024]{1,0:T(8,128)(2,1)S(1)}, u32[]{:S(2)}, u32[]{:S(2)}) collective-permute-start(bf16[128,1024]{1,0:T(8,128)(2,1)S(1)} %get-tuple-element.20), channel_id=1, source_target_pairs={{0,8},{8,16},{16,24},{24,0},{1,9},{9,17},{17,25},{25,1},{2,10},{10... | collective-permute-start | bytes 786440 | tf_op jit(solution)/shard_map/ppermute | solution.py:204
  69.5 1.2 %shard_map.126 = (bf16[128,1024]{1,0:T(8,128)(2,1)}, f32[8,128]{1,0:T(8,128)S(1)}) custom-call(s32[1]{0:T(128)} %bitcast.index_ref, f32[128,1024]{1,0:T(8,128)S(1)} %shard_map.125.inner_ref, bf16[128,4096]{1,0:T(8,128)(2,1)S(1)} %bitcast.41, bf16[128,256]{1,0:T(8,128)(2,1)S(1)} %bitcast.50, f32[128,64]{1,0:T(8,128)S(1)} %get-tuple-element.15.cum_ref, ...), custom_call_target="tpu_custom_call" | custom-call | flops 33554432 | bytes 1048576 | tf_op jit(solution)/shard_map/pallas_call | solution.py:283
  70.7 1.2 %collective-permute-start.5 = (bf16[128,1024]{1,0:T(8,128)(2,1)}, bf16[128,1024]{1,0:T(8,128)(2,1)S(1)}, u32[]{:S(2)}, u32[]{:S(2)}) collective-permute-start(bf16[128,1024]{1,0:T(8,128)(2,1)} %get-tuple-element.21), channel_id=1, source_target_pairs={{0,8},{8,16},{16,24},{24,0},{1,9},{9,17},{17,25},{25,1},{2,10},{10... | collective-permute-start | bytes 786440 | tf_op jit(solution)/shard_map/ppermute | solution.py:204
  71.9 1.2 %shard_map.128 = (bf16[128,1024]{1,0:T(8,128)(2,1)}, f32[8,128]{1,0:T(8,128)S(1)}) custom-call(s32[1]{0:T(128)} %bitcast.index_ref, f32[128,1024]{1,0:T(8,128)S(1)} %shard_map.127.inner_ref, bf16[128,4096]{1,0:T(8,128)(2,1)S(1)} %bitcast.42, bf16[128,256]{1,0:T(8,128)(2,1)S(1)} %bitcast.51, f32[128,64]{1,0:T(8,128)S(1)} %get-tuple-element.15.cum_ref, ...), custom_call_target="tpu_custom_call" | custom-call | flops 33554432 | bytes 1048576 | tf_op jit(solution)/shard_map/pallas_call | solution.py:283
  73.3 1.2 %collective-permute-start.7 = (bf16[128,1024]{1,0:T(8,128)(2,1)}, bf16[128,1024]{1,0:T(8,128)(2,1)S(1)}, u32[]{:S(2)}, u32[]{:S(2)}) collective-permute-start(bf16[128,1024]{1,0:T(8,128)(2,1)} %get-tuple-element.22), channel_id=1, source_target_pairs={{0,8},{8,16},{16,24},{24,0},{1,9},{9,17},{17,25},{25,1},{2,10},{10... | collective-permute-start | bytes 786440 | tf_op jit(solution)/shard_map/ppermute | solution.py:204
  74.5 1.2 %shard_map.130 = (bf16[128,1024]{1,0:T(8,128)(2,1)}, f32[8,128]{1,0:T(8,128)S(1)}) custom-call(s32[1]{0:T(128)} %bitcast.index_ref, f32[128,1024]{1,0:T(8,128)S(1)} %shard_map.129.inner_ref, bf16[128,4096]{1,0:T(8,128)(2,1)S(1)} %bitcast.43, bf16[128,256]{1,0:T(8,128)(2,1)S(1)} %bitcast.52, f32[128,64]{1,0:T(8,128)S(1)} %get-tuple-element.15.cum_ref, ...), custom_call_target="tpu_custom_call" | custom-call | flops 33554432 | bytes 1048576 | tf_op jit(solution)/shard_map/pallas_call | solution.py:283
  75.8 1.2 %collective-permute-start.9 = (bf16[128,1024]{1,0:T(8,128)(2,1)}, bf16[128,1024]{1,0:T(8,128)(2,1)S(1)}, u32[]{:S(2)}, u32[]{:S(2)}) collective-permute-start(bf16[128,1024]{1,0:T(8,128)(2,1)} %get-tuple-element.23), channel_id=1, source_target_pairs={{0,8},{8,16},{16,24},{24,0},{1,9},{9,17},{17,25},{25,1},{2,10},{10... | collective-permute-start | bytes 786440 | tf_op jit(solution)/shard_map/ppermute | solution.py:204
  77.0 8.4 %psum.7 = f32[8,128]{1,0:T(8,128)S(1)} all-reduce(f32[8,128]{1,0:T(8,128)S(1)} %add_add_fusion), channel_id=1, replica_groups=mesh['segment'=4,'ctx'=4,'tp'=2] {'tp'}, use_global_device_ids=true, to_apply=%region_0.1 | all-reduce | flops 1024 | bytes 8192 | tf_op jit(solution)/shard_map/psum | solution.py:302
  85.4 1.2 %collective-permute-start.10 = (f32[8,128]{1,0:T(8,128)S(1)}, f32[8,128]{1,0:T(8,128)S(1)}, u32[]{:S(2)}, u32[]{:S(2)}) collective-permute-start(f32[8,128]{1,0:T(8,128)S(1)} %psum.7), channel_id=1, source_target_pairs={{0,8},{8,16},{16,24},{24,0},{1,9},{9,17},{17,25},{25,1},{2,10},{10... | collective-permute-start | bytes 12296 | tf_op jit(solution)/shard_map/ppermute | solution.py:204
  86.6 10.8 %shard_map.132 = bf16[128,4096]{1,0:T(8,128)(2,1)} custom-call(s32[1]{0:T(128)} %bitcast.index_ref, s32[1]{0:T(128)} %collective-permute-done.11.source_ref, bf16[128,4096]{1,0:T(8,128)(2,1)S(1)} %collective-permute-done.12.q_ref, bf16[512,1024]{1,0:T(8,128)(2,1)S(1)} %pad_maximum_fusion.k_ref.v_ref, bf16[512,1024]{1,0:T(8,128)(2,1)S(1)} %pad_maximum_fusion.k_ref.v_ref), custom_call_target="tpu_custom_call" | custom-call | flops 1073741824 | bytes 2097152 | tf_op jit(solution)/shard_map/pallas_call | solution.py:252
  97.4 1.4 %shard_map.131 = bf16[128,4096]{1,0:T(8,128)(2,1)} custom-call(bf16[128,1024]{1,0:T(8,128)(2,1)S(1)} %collective-permute-done.3.refs_0_, bf16[128,1024]{1,0:T(8,128)(2,1)S(1)} %collective-permute-done.5.refs_1_, bf16[128,1024]{1,0:T(8,128)(2,1)S(1)} %collective-permute-done.7.refs_2_, bf16[128,1024]{1,0:T(8,128)(2,1)S(1)} %collective-permute-done.9.refs_3_, ...), custom_call_target="tpu_custom_call" | custom-call | flops 524288 | bytes 2097152 | tf_op jit(solution)/shard_map/pallas_call | solution.py:303
  (44 shorter events, 4.8 us)
Async XLA Ops:
  2.2 1.2 %copy-start = (bf16[1,128,4096]{2,1,0:T(8,128)(2,1)S(1)}, bf16[1,128,4096]{2,1,0:T(8,128)(2,1)}, u32[]{:S(2)}) copy-start(bf16[1,128,4096]{2,1,0:T(8,128)(2,1)} %param.11) | copy-start | bytes 3145732
  3.5 0.7 copy-start.6
  6.0 9.1 %collective-permute-start = (bf16[128,1024]{1,0:T(8,128)(2,1)S(1)}, bf16[128,1024]{1,0:T(8,128)(2,1)S(1)}, u32[]{:S(2)}, u32[]{:S(2)}) collective-permute-start(bf16[128,1024]{1,0:T(8,128)(2,1)S(1)} %dynamic-slice_bitcast_fusion), channel_id=1, source_target_pairs={{0,2},{2,4},{4,6},{1,3},{3,5},{5,7},{8,10},{10,12},{12,14},{9,11},... | collective-permute-start | bytes 786440 | tf_op jit(solution)/shard_map/ppermute | solution.py:241
  15.0 18.9 %copy-start.7 = (bf16[1,128,512]{2,1,0:T(8,128)(2,1)S(1)}, bf16[1,128,512]{2,1,0:T(8,128)(2,1)}, u32[]{:S(2)}) copy-start(bf16[1,128,512]{2,1,0:T(8,128)(2,1)} %param.20) | copy-start | bytes 393220
  15.0 18.9 %copy-start.8 = (bf16[1,128,512]{2,1,0:T(8,128)(2,1)S(1)}, bf16[1,128,512]{2,1,0:T(8,128)(2,1)}, u32[]{:S(2)}) copy-start(bf16[1,128,512]{2,1,0:T(8,128)(2,1)} %param.19) | copy-start | bytes 393220
  15.1 8.3 %collective-permute-start.1 = (bf16[128,1024]{1,0:T(8,128)(2,1)S(1)}, bf16[128,1024]{1,0:T(8,128)(2,1)S(1)}, u32[]{:S(2)}, u32[]{:S(2)}) collective-permute-start(bf16[128,1024]{1,0:T(8,128)(2,1)S(1)} %fusion.4), channel_id=1, source_target_pairs={{0,2},{2,4},{4,6},{1,3},{3,5},{5,7},{8,10},{10,12},{12,14},{9,11},... | collective-permute-start | bytes 786440 | tf_op jit(solution)/shard_map/ppermute | solution.py:241
  23.5 7.1 %collective-permute-start.2 = (bf16[128,1024]{1,0:T(8,128)(2,1)S(1)}, bf16[128,1024]{1,0:T(8,128)(2,1)S(1)}, u32[]{:S(2)}, u32[]{:S(2)}) collective-permute-start(bf16[128,1024]{1,0:T(8,128)(2,1)S(1)} %fusion.3), channel_id=1, source_target_pairs={{0,2},{2,4},{4,6},{1,3},{3,5},{5,7},{8,10},{10,12},{12,14},{9,11},... | collective-permute-start | bytes 786440 | tf_op jit(solution)/shard_map/ppermute | solution.py:241
  30.7 7.1 %collective-permute-start.4 = (bf16[128,1024]{1,0:T(8,128)(2,1)S(1)}, bf16[128,1024]{1,0:T(8,128)(2,1)S(1)}, u32[]{:S(2)}, u32[]{:S(2)}) collective-permute-start(bf16[128,1024]{1,0:T(8,128)(2,1)S(1)} %fusion.2), channel_id=1, source_target_pairs={{0,2},{2,4},{4,6},{1,3},{3,5},{5,7},{8,10},{10,12},{12,14},{9,11},... | collective-permute-start | bytes 786440 | tf_op jit(solution)/shard_map/ppermute | solution.py:241
  33.9 17.7 %copy-start.1 = (bf16[1,128,4096]{2,1,0:T(8,128)(2,1)S(1)}, bf16[1,128,4096]{2,1,0:T(8,128)(2,1)}, u32[]{:S(2)}) copy-start(bf16[1,128,4096]{2,1,0:T(8,128)(2,1)} %param.11) | copy-start | bytes 3145732
  33.9 17.7 %copy-start.3 = (bf16[1,128,256]{2,1,0:T(8,128)(2,1)S(1)}, bf16[1,128,256]{2,1,0:T(8,128)(2,1)}, u32[]{:S(2)}) copy-start(bf16[1,128,256]{2,1,0:T(8,128)(2,1)} %param.14) | copy-start | bytes 196612
  33.9 17.7 %copy-start.5 = (f32[64]{0:T(128)S(1)}, f32[64]{0:T(128)}, u32[]{:S(2)}) copy-start(f32[64]{0:T(128)} %param.16) | copy-start | bytes 772
  34.0 7.1 %collective-permute-start.13 = (bf16[128,1024]{1,0:T(8,128)(2,1)S(1)}, bf16[128,1024]{1,0:T(8,128)(2,1)S(1)}, u32[]{:S(2)}, u32[]{:S(2)}) collective-permute-start(bf16[128,1024]{1,0:T(8,128)(2,1)S(1)} %pad_maximum_fusion.1), channel_id=1, source_target_pairs={{0,8},{8,16},{16,24},{24,0},{1,9},{9,17},{17,25},{25,1},{2,10},{10... | collective-permute-start | bytes 786440 | tf_op jit(solution)/shard_map/ppermute | solution.py:204
  35.2 50.1 %collective-permute-start.12 = (bf16[128,4096]{1,0:T(8,128)(2,1)}, bf16[128,4096]{1,0:T(8,128)(2,1)S(1)}, u32[]{:S(2)}, u32[]{:S(2)}) collective-permute-start(bf16[128,4096]{1,0:T(8,128)(2,1)} %bitcast.20), channel_id=1, source_target_pairs={{0,8},{8,16},{16,24},{24,0},{1,9},{9,17},{17,25},{25,1},{2,10},{10... | collective-permute-start | bytes 3145736 | tf_op jit(solution)/shard_map/ppermute | solution.py:204
  37.9 9.9 %collective-permute-start.6 = (bf16[128,1024]{1,0:T(8,128)(2,1)S(1)}, bf16[128,1024]{1,0:T(8,128)(2,1)S(1)}, u32[]{:S(2)}, u32[]{:S(2)}) collective-permute-start(bf16[128,1024]{1,0:T(8,128)(2,1)S(1)} %fusion.1), channel_id=1, source_target_pairs={{0,2},{2,4},{4,6},{1,3},{3,5},{5,7},{8,10},{10,12},{12,14},{9,11},... | collective-permute-start | bytes 786440 | tf_op jit(solution)/shard_map/ppermute | solution.py:241
  41.1 12.9 %collective-permute-start.16 = (bf16[128,1024]{1,0:T(8,128)(2,1)S(1)}, bf16[128,1024]{1,0:T(8,128)(2,1)S(1)}, u32[]{:S(2)}, u32[]{:S(2)}) collective-permute-start(bf16[128,1024]{1,0:T(8,128)(2,1)S(1)} %collective-permute-done.13), channel_id=1, source_target_pairs={{0,6},{2,0},{4,2},{6,4},{1,7},{3,1},{5,3},{7,5},{8,14},{10,8},{12,... | collective-permute-start | bytes 786440 | tf_op jit(solution)/shard_map/ppermute | solution.py:246
  41.3 18.9 %collective-permute-start.15 = (bf16[128,1024]{1,0:T(8,128)(2,1)S(1)}, bf16[128,1024]{1,0:T(8,128)(2,1)S(1)}, u32[]{:S(2)}, u32[]{:S(2)}) collective-permute-start(bf16[128,1024]{1,0:T(8,128)(2,1)S(1)} %collective-permute-done.13), channel_id=1, source_target_pairs={{0,4},{2,6},{4,0},{6,2},{1,5},{3,7},{5,1},{7,3},{8,12},{10,14},{12... | collective-permute-start | bytes 786440 | tf_op jit(solution)/shard_map/ppermute | solution.py:246
  42.6 24.8 %collective-permute-start.14 = (bf16[128,1024]{1,0:T(8,128)(2,1)S(1)}, bf16[128,1024]{1,0:T(8,128)(2,1)S(1)}, u32[]{:S(2)}, u32[]{:S(2)}) collective-permute-start(bf16[128,1024]{1,0:T(8,128)(2,1)S(1)} %collective-permute-done.13), channel_id=1, source_target_pairs={{0,2},{2,4},{4,6},{6,0},{1,3},{3,5},{5,7},{7,1},{8,10},{10,12},{12... | collective-permute-start | bytes 786440 | tf_op jit(solution)/shard_map/ppermute | solution.py:246
  47.9 25.5 %collective-permute-start.8 = (bf16[128,1024]{1,0:T(8,128)(2,1)S(1)}, bf16[128,1024]{1,0:T(8,128)(2,1)S(1)}, u32[]{:S(2)}, u32[]{:S(2)}) collective-permute-start(bf16[128,1024]{1,0:T(8,128)(2,1)S(1)} %fusion), channel_id=1, source_target_pairs={{0,2},{2,4},{4,6},{1,3},{3,5},{5,7},{8,10},{10,12},{12,14},{9,11},... | collective-permute-start | bytes 786440 | tf_op jit(solution)/shard_map/ppermute | solution.py:241
  54.0 13.5 %copy-start.2 = (bf16[1,128,4096]{2,1,0:T(8,128)(2,1)S(1)}, bf16[1,128,4096]{2,1,0:T(8,128)(2,1)}, u32[]{:S(2)}) copy-start(bf16[1,128,4096]{2,1,0:T(8,128)(2,1)} %param.12) | copy-start | bytes 3145732
  54.0 21.8 %collective-permute-start.11 = (s32[1]{0:T(128)}, s32[1]{0:T(128)}, u32[]{:S(2)}, u32[]{:S(2)}) collective-permute-start(s32[1]{0:T(128)} %param.21), channel_id=1, source_target_pairs={{0,8},{8,16},{16,24},{24,0},{1,9},{9,17},{17,25},{25,1},{2,10},{10... | collective-permute-start | bytes 20 | tf_op jit(solution)/shard_map/ppermute | solution.py:204
  68.2 29.2 %collective-permute-start.3 = (bf16[128,1024]{1,0:T(8,128)(2,1)S(1)}, bf16[128,1024]{1,0:T(8,128)(2,1)S(1)}, u32[]{:S(2)}, u32[]{:S(2)}) collective-permute-start(bf16[128,1024]{1,0:T(8,128)(2,1)S(1)} %get-tuple-element.20), channel_id=1, source_target_pairs={{0,8},{8,16},{16,24},{24,0},{1,9},{9,17},{17,25},{25,1},{2,10},{10... | collective-permute-start | bytes 786440 | tf_op jit(solution)/shard_map/ppermute | solution.py:204
  70.7 26.7 %collective-permute-start.5 = (bf16[128,1024]{1,0:T(8,128)(2,1)}, bf16[128,1024]{1,0:T(8,128)(2,1)S(1)}, u32[]{:S(2)}, u32[]{:S(2)}) collective-permute-start(bf16[128,1024]{1,0:T(8,128)(2,1)} %get-tuple-element.21), channel_id=1, source_target_pairs={{0,8},{8,16},{16,24},{24,0},{1,9},{9,17},{17,25},{25,1},{2,10},{10... | collective-permute-start | bytes 786440 | tf_op jit(solution)/shard_map/ppermute | solution.py:204
  73.3 24.1 %collective-permute-start.7 = (bf16[128,1024]{1,0:T(8,128)(2,1)}, bf16[128,1024]{1,0:T(8,128)(2,1)S(1)}, u32[]{:S(2)}, u32[]{:S(2)}) collective-permute-start(bf16[128,1024]{1,0:T(8,128)(2,1)} %get-tuple-element.22), channel_id=1, source_target_pairs={{0,8},{8,16},{16,24},{24,0},{1,9},{9,17},{17,25},{25,1},{2,10},{10... | collective-permute-start | bytes 786440 | tf_op jit(solution)/shard_map/ppermute | solution.py:204
  75.8 21.6 %collective-permute-start.9 = (bf16[128,1024]{1,0:T(8,128)(2,1)}, bf16[128,1024]{1,0:T(8,128)(2,1)S(1)}, u32[]{:S(2)}, u32[]{:S(2)}) collective-permute-start(bf16[128,1024]{1,0:T(8,128)(2,1)} %get-tuple-element.23), channel_id=1, source_target_pairs={{0,8},{8,16},{16,24},{24,0},{1,9},{9,17},{17,25},{25,1},{2,10},{10... | collective-permute-start | bytes 786440 | tf_op jit(solution)/shard_map/ppermute | solution.py:204
  85.4 12.1 %copy-start.4 = (f32[4096]{0:T(1024)S(1)}, f32[4096]{0:T(1024)}, u32[]{:S(2)}) copy-start(f32[4096]{0:T(1024)} %param.17) | copy-start | bytes 49156
  85.4 12.0 %collective-permute-start.10 = (f32[8,128]{1,0:T(8,128)S(1)}, f32[8,128]{1,0:T(8,128)S(1)}, u32[]{:S(2)}, u32[]{:S(2)}) collective-permute-start(f32[8,128]{1,0:T(8,128)S(1)} %psum.7), channel_id=1, source_target_pairs={{0,8},{8,16},{16,24},{24,0},{1,9},{9,17},{17,25},{25,1},{2,10},{10... | collective-permute-start | bytes 12296 | tf_op jit(solution)/shard_map/ppermute | solution.py:204

commit v2 on v0

v2 whole, which is shorter than its diff:
```python
import functools
import math

import jax
import jax.numpy as jnp
from jax import lax
from jax.experimental import pallas as pl
from jax.experimental.pallas import tpu as pltpu
from jax.sharding import PartitionSpec as P

QUERY_HEADS = 64
KEY_VALUE_HEADS = 8
HEAD_WIDTH = 128
NST = 128
HP = 64
GROUP = QUERY_HEADS // KEY_VALUE_HEADS
CHUNKS = 2
VMEM = 40 * 1024 * 1024
PARCEL_VMEM = 60 * 1024 * 1024
HIGH = lax.Precision.HIGHEST


def dot(a, b, dims, precision=None):
    return lax.dot_general(
        a, b, (dims, ((), ())), precision=precision, preferred_element_type=jnp.float32
    )


def call(kernel, out_shape, flops, nbytes, **kw):
    return pl.pallas_call(
        kernel,
        out_shape=out_shape,
        compiler_params=pltpu.CompilerParams(vmem_limit_bytes=VMEM),
        cost_estimate=pl.CostEstimate(flops=flops, bytes_accessed=nbytes, transcendentals=0),
        **kw,
    )


def lower_mask(rows):
    return lax.broadcasted_iota(jnp.int32, (rows, rows), 0) >= lax.broadcasted_iota(
        jnp.int32, (rows, rows), 1
    )


def pair_columns(table, pair, rows):
    lane = lax.broadcasted_iota(jnp.int32, (rows, 2 * HP), 1)
    first = jnp.broadcast_to(table[:, 2 * pair : 2 * pair + 1], (rows, 2 * HP))
    second = jnp.broadcast_to(table[:, 2 * pair + 1 : 2 * pair + 2], (rows, 2 * HP))
    return jnp.where(lane < HP, first, second)


def spread(row, first, width):
    return jnp.concatenate(
        [pair_columns(row, first // 2 + pair, 1) for pair in range(width // (2 * HP))], axis=1
    )


def parcel_kernel(index_ref, x_ref, maps_ref, dt_ref, key_ref, value_ref, *refs):
    *parcel_refs, packed_ref, sem = refs
    rows = x_ref.shape[0]
    side, half = x_ref.shape[1] // 2, dt_ref.shape[0] // 2
    width, kv = side // CHUNKS, key_ref.shape[1]
    away = 1 - index_ref[0] % 2
    first = parcel_refs[0]
    moves = [
        (
            x_ref.at[:, pl.ds(pl.multiple_of(away * side + chunk * width, 128), width)],
            out_ref.at[:, pl.ds(0, width)],
        )
        for chunk, out_ref in enumerate(parcel_refs)
    ]
    moves.append((maps_ref, first.at[:, pl.ds(width, 2 * NST)]))
    moves.append(
        (
            dt_ref.at[pl.ds(pl.multiple_of(away * half, half), half), :],
            first.at[pl.ds(0, half), pl.ds(width + 2 * NST, rows)],
        )
    )
    moves.append((key_ref, packed_ref.at[:, pl.ds(0, kv)]))
    moves.append((value_ref, packed_ref.at[:, pl.ds(kv, kv)]))
    copies = [
        pltpu.make_async_copy(src, dst, sem.at[number]) for number, (src, dst) in enumerate(moves)
    ]
    for copy in copies:
        copy.start()
    for copy in copies:
        copy.wait()


def decays(dt, rate, heads):
    rows = dt.shape[1]
    ones = jnp.where(lower_mask(rows), 1.0, 0.0).astype(jnp.bfloat16)
    rate_col = jnp.transpose(jnp.broadcast_to(rate, (8, heads)))[:, :1]
    cum = -rate * dot(ones, dt, ((1,), (1,)))
    cum_t = -rate_col * dot(dt, ones, ((1,), (1,)))
    return cum, cum_t


def state_kernel(
    chunk, index_ref, x_ref, x2_ref, dt_ref, dt2_ref, rate_ref, b_ref, b2_ref,
    out_ref, first_ref, lead_ref, both_ref,
):
    rows, width = x_ref.shape
    count = width // HP
    at = slice(chunk * count, chunk * count + count)
    early = index_ref[0] % 2 == 0
    rate = rate_ref[0][:, at]
    halves = []
    for x, dt, b in ((x_ref, dt_ref, b_ref), (x2_ref, dt2_ref, b2_ref)):
        step = dt[at, :]
        cum, _ = decays(step, rate, count)
        total = cum[rows - 1 : rows, :]
        tail = jnp.exp(total - cum) * jnp.transpose(step.astype(jnp.float32))
        xw = jnp.concatenate(
            [
                (
                    x[:, pair * 128 : pair * 128 + 128].astype(jnp.float32)
                    * pair_columns(tail, pair, rows)
                ).astype(jnp.bfloat16)
                for pair in range(width // 128)
            ],
            axis=1,
        )
        halves.append((dot(b[...], xw, ((0,), (0,))), spread(jnp.exp(total), 0, width)))
    (mine, mine_decay), (theirs, theirs_decay) = halves
    first = jnp.where(early, mine, theirs)
    second = jnp.where(early, theirs, mine)
    lead = jnp.where(early, mine_decay, theirs_decay)
    trail = jnp.where(early, theirs_decay, mine_decay)
    out_ref[...] = (first * trail + second).astype(out_ref.dtype)
    first_ref[...] = first
    lead_ref[...] = lead
    both_ref[...] = lead * trail


def inner_kernel(
    chunk, index_ref, x_ref, x2_ref, dt_ref, dt2_ref, rate_ref, skip_ref, maps_ref, maps2_ref,
    out_ref, grow_ref, out2_ref, grow2_ref,
):
    del index_ref
    rows, width = x_ref.shape
    count = width // HP
    at = slice(chunk * count, chunk * count + count)
    lane = lax.broadcasted_iota(jnp.int32, (rows, 128), 1)
    rate, skip = rate_ref[0][:, at], skip_ref[0][:, at]
    for x, dt, maps, out, spread_out in (
        (x_ref, dt_ref, maps_ref, out_ref, grow_ref),
        (x2_ref, dt2_ref, maps2_ref, out2_ref, grow2_ref),
    ):
        gram = dot(maps[:, NST:], maps[:, :NST], ((1,), (1,)))
        gram = jnp.where(lower_mask(rows), gram, 0.0)
        step = dt[at, :]
        cum, cum_t = decays(step, rate, count)
        step = step.astype(jnp.float32)
        grow = jnp.exp(cum)
        for pair in range(width // 128):
            mixes = []
            for head in (2 * pair, 2 * pair + 1):
                mine = jnp.broadcast_to(cum[:, head : head + 1], (rows, rows))
                decay = jnp.exp(jnp.minimum(mine - cum_t[head : head + 1, :], 0.0))
                mixes.append((gram * decay * step[head : head + 1, :]).astype(jnp.bfloat16))
            xs = x[:, pair * 128 : pair * 128 + 128]
            zero = jnp.zeros_like(xs)
            stacked = jnp.concatenate(
                [jnp.where(lane < HP, xs, zero), jnp.where(lane < HP, zero, xs)], axis=0
            )
            mixed = dot(jnp.concatenate(mixes, axis=1), stacked, ((1,), (0,)))
            mixed = mixed + pair_columns(skip, pair, 1) * xs.astype(jnp.float32)
            out[:, pair * 128 : pair * 128 + 128] = mixed
            spread_out[:, pair * 128 : pair * 128 + 128] = pair_columns(grow, pair, rows)


def gate_and_sum(raw, gate, out_ref, sums_ref):
    rows, width = raw.shape
    gate = gate.astype(jnp.float32)
    gated = raw.astype(jnp.float32) * (gate / (1.0 + jnp.exp(-gate)))
    out_ref[...] = gated.astype(jnp.bfloat16)
    squares = gated * gated
    total = squares[:, :128]
    for tile in range(1, width // 128):
        total = total + squares[:, tile * 128 : tile * 128 + 128]
    sums_ref[...] = dot(jnp.ones((8, 128), jnp.float32), total, ((1,), (1,)), HIGH)


def outer_kernel(
    index_ref, enter_ref, first_ref, lead_ref, local_ref, grow_ref, local2_ref, grow2_ref,
    c_ref, c2_ref, gate_ref, out_ref, sums_ref, back_ref,
):
    early = index_ref[0] % 2 == 0
    enter = jnp.where(index_ref[0] < 2, 0.0, enter_ref[...].astype(jnp.float32))
    later = lead_ref[...] * enter + first_ref[...]
    mine = jnp.where(early, enter, later).astype(jnp.bfloat16)
    theirs = jnp.where(early, later, enter).astype(jnp.bfloat16)
    back = local2_ref[...] + grow2_ref[...] * dot(c2_ref[...], theirs, ((1,), (0,)))
    back_ref[...] = back.astype(jnp.bfloat16)
    raw = local_ref[...] + grow_ref[...] * dot(c_ref[...], mine, ((1,), (0,)))
    gate_and_sum(raw.astype(jnp.bfloat16), gate_ref[...], out_ref, sums_ref)


def gate_kernel(index_ref, raw_ref, gate_ref, out_ref, sums_ref):
    del index_ref
    gate_and_sum(raw_ref[...], gate_ref[...], out_ref, sums_ref)


def norm_kernel(channels, index_ref, *refs):
    *chunk_refs, sums_ref, gain_ref, out_ref = refs
    rows = out_ref.shape[0]
    half = out_ref.shape[1] // 2
    mean = sums_ref[0:1, :] / channels
    scale = jnp.broadcast_to(lax.rsqrt(mean + 1e-05), (rows, rows))
    eye = lax.broadcasted_iota(jnp.int32, (rows, rows), 0) == lax.broadcasted_iota(
        jnp.int32, (rows, rows), 1
    )
    scale = jnp.sum(jnp.where(eye, scale, 0.0), axis=1, keepdims=True)
    parity = index_ref[0] % 2
    for number, ref in enumerate(chunk_refs):
        width = ref.shape[1]
        side, chunk = divmod(number, CHUNKS)
        start = (parity if side == 0 else 1 - parity) * half + chunk * width
        at = pl.ds(pl.multiple_of(start, 128), width)
        out_ref[:, at] = (ref[...].astype(jnp.float32) * scale * gain_ref[:, at]).astype(
            jnp.bfloat16
        )


def attention_kernel(ctx, index_ref, source_ref, q_ref, *refs):
    out_ref, bias_ref = refs[-2:]
    key = jnp.concatenate([ref[...] for ref in refs[:ctx]], axis=0)
    value = jnp.concatenate([ref[...] for ref in refs[ctx : 2 * ctx]], axis=0)
    rows = q_ref.shape[0]
    keys = key.shape[0]
    index = index_ref[0]
    source = source_ref[0]
    place = lax.broadcasted_iota(jnp.int32, (keys, rows), 0)
    away = place // rows
    owner = jnp.zeros_like(place)
    step, bit = ctx // 2, 1
    while step >= 1:
        owner = owner + jnp.where((away & bit) != 0, step, 0)
        step, bit = step // 2, bit * 2
    key_pos = (owner ^ index) * rows + place % rows
    query_pos = index * rows + lax.broadcasted_iota(jnp.int32, (keys, rows), 1)
    bias_ref[...] = jnp.where((key_pos <= query_pos) | (key_pos < source), 0.0, -jnp.inf)
    factor = math.log2(math.e) / math.sqrt(HEAD_WIDTH)
    span = lambda head: slice(head * HEAD_WIDTH, (head + 1) * HEAD_WIDTH)
    query = jnp.concatenate([q_ref[:, span(head)] for head in range(GROUP)], axis=0)
    value = jnp.transpose(value.astype(jnp.float32)).astype(jnp.bfloat16)
    scores = dot(key, query, ((1,), (1,)))
    weights, totals = [], []
    for head in range(GROUP):
        kept = scores[:, head * rows : (head + 1) * rows] + bias_ref[...]
        top = jnp.max(kept, axis=0, keepdims=True)
        weight = jnp.exp2((kept - top) * factor)
        totals.append(jnp.sum(weight, axis=0, keepdims=True))
        weights.append(weight.astype(jnp.bfloat16))
    mixed = dot(value, jnp.concatenate(weights, axis=1), ((1,), (0,)))
    mixed = mixed / jnp.concatenate(totals, axis=1)
    for head in range(GROUP):
        out_ref[:, span(head)] = jnp.transpose(
            mixed[:, head * rows : (head + 1) * rows]
        ).astype(jnp.bfloat16)


def on_device(
    mamba_input,
    mamba_gate,
    step_size,
    state_maps,
    decay_rate,
    skip_gain,
    norm_gain,
    queries,
    keys,
    values,
    source_len,
):
    segments = lax.axis_size("segment")
    ctx = lax.axis_size("ctx")
    tps = lax.axis_size("tp")
    index = lax.axis_index("ctx")
    index_in = index.astype(jnp.int32).reshape(1)
    onward = [(i, (i + 1) % segments) for i in range(segments)]
    partner = [(i, i + 1 - 2 * (i % 2)) for i in range(ctx)]
    further = [(i, (i + 2) % ctx) for i in range(ctx)]
    bf16, f32 = jnp.bfloat16, jnp.float32
    shape = jax.ShapeDtypeStruct

    def hand(array):
        return lax.ppermute(array, "segment", onward)

    def after(value, *others):
        return lax.optimization_barrier((value, *others))[0]

    x, gate, maps = mamba_input[0], mamba_gate[0], state_maps[0]
    dt = step_size[0].T
    heads, rows = dt.shape
    channels = x.shape[1]
    half = heads // 2
    side = channels // 2
    width = side // CHUNKS
    wire = bf16 if ctx <= 8 else f32
    rate = decay_rate.reshape(2, 1, half)
    skip = skip_gain.reshape(2, 1, half)
    groups = keys.shape[2] // HEAD_WIDTH
    wide = GROUP * HEAD_WIDTH

    whole = lambda *dims: pl.BlockSpec(dims, lambda i, s: (0,) * len(dims))
    fixed = lambda dims, *at: pl.BlockSpec(dims, lambda i, s: at)
    mine = lambda dims: pl.BlockSpec(dims, lambda i, s: (s[0] % 2,) + (0,) * (len(dims) - 1))
    columns = lambda chunk: pl.BlockSpec(
        (rows, width), lambda i, s: (0, (s[0] % 2) * CHUNKS + chunk)
    )
    others = lambda chunk: pl.BlockSpec(
        (rows, width), lambda i, s: (0, (1 - s[0] % 2) * CHUNKS + chunk)
    )

    def indexed(kernel, out_shape, flops, nbytes, in_specs, out_specs, scratch=(), vmem=VMEM):
        return pl.pallas_call(
            kernel,
            out_shape=out_shape,
            grid_spec=pltpu.PrefetchScalarGridSpec(
                num_scalar_prefetch=1,
                grid=(1,),
                in_specs=in_specs,
                out_specs=out_specs,
                scratch_shapes=scratch,
            ),
            compiler_params=pltpu.CompilerParams(vmem_limit_bytes=vmem),
            cost_estimate=pl.CostEstimate(flops=flops, bytes_accessed=nbytes, transcendentals=0),
        )

    parcel_width = width + 2 * NST + rows
    hbm = pl.BlockSpec(memory_space=pltpu.HBM)
    kv_width = 2 * groups * HEAD_WIDTH
    *parcels, packed = indexed(
        parcel_kernel,
        (shape((rows, parcel_width), bf16),)
        + (shape((rows, width), bf16),) * (CHUNKS - 1)
        + (shape((rows, kv_width), bf16),),
        0,
        4 * rows * side,
        [hbm] * 5,
        (whole(rows, parcel_width),)
        + (whole(rows, width),) * (CHUNKS - 1)
        + (whole(rows, kv_width),),
        [pltpu.SemaphoreType.DMA((CHUNKS + 4,))],
        PARCEL_VMEM,
    )(index_in, x, maps, dt, keys[0], values[0])
    got = [lax.ppermute(parcel, "ctx", partner) for parcel in parcels]
    key_values = hand(packed)
    query = hand(queries[0])
    source = hand(source_len)
    pairs = [
        columns,
        lambda chunk: whole(rows, width),
        lambda chunk: mine((half, rows)),
        lambda chunk: fixed((half, rows), 0, (width + 2 * NST) // rows),
        lambda chunk: mine((1, 1, half)),
    ]
    places = lambda chunk: [spec(chunk) for spec in pairs]
    states, firsts, leads, inner = [], [], [], []
    for chunk in range(CHUNKS):
        state, first, lead, both = indexed(
            functools.partial(state_kernel, chunk),
            (shape((NST, width), wire), shape((NST, width), f32)) + (shape((1, width), f32),) * 2,
            4 * rows * NST * width,
            4 * rows * width,
            places(chunk) + [whole(rows, NST), fixed((rows, NST), 0, width // NST)],
            (whole(NST, width),) * 2 + (whole(1, width),) * 2,
        )(index_in, x, got[chunk], dt, got[0], rate, maps, got[0])
        enter = lax.ppermute(state, "ctx", further)
        for _ in range(ctx // 2 - 2):
            enter = jnp.where(index < 2, 0.0, enter.astype(f32))
            enter = lax.ppermute((state.astype(f32) + both * enter).astype(wire), "ctx", further)
        states.append(enter)
        firsts.append(first)
        leads.append(lead)
    for chunk in range(CHUNKS):
        inner.append(
            indexed(
                functools.partial(inner_kernel, chunk),
                (shape((rows, width), f32),) * 4,
                8 * rows * rows * width,
                6 * rows * width,
                places(chunk)
                + [
                    mine((1, 1, half)),
                    whole(rows, 2 * NST),
                    fixed((rows, 2 * NST), 0, width // (2 * NST)),
                ],
                (whole(rows, width),) * 4,
            )(index_in, x, got[chunk], dt, got[0], rate, skip, maps, got[0])
        )
    scalar = pl.BlockSpec(memory_space=pltpu.SMEM)

    def attend(group, query, pieces, out):
        more = [] if out is None else [out]
        spot = lambda at: pl.BlockSpec((rows, HEAD_WIDTH), lambda i: (0, at))
        return call(
            functools.partial(attention_kernel, ctx),
            shape((rows, groups * wide), bf16),
            4 * rows * wide * ctx * rows,
            4 * rows * wide,
            grid=(1,),
            in_specs=[scalar, scalar, pl.BlockSpec((rows, wide), lambda i: (0, group))]
            + [spot(group)] * ctx
            + [spot(group + groups)] * ctx
            + [pl.BlockSpec(memory_space=pl.ANY)] * len(more),
            out_specs=pl.BlockSpec((rows, wide), lambda i: (0, group)),
            scratch_shapes=[pltpu.VMEM((ctx * rows, rows), f32)],
            input_output_aliases={3 + 2 * ctx: 0} if more else {},
        )(index_in, source, query, *pieces, *pieces, *more)

    pieces = [after(key_values, states[0])]
    step = ctx // 2
    while step >= 1:
        swap = [(i, i ^ step) for i in range(ctx)]
        pieces = pieces + [lax.ppermute(piece, "ctx", swap) for piece in pieces]
        step //= 2

    gated, sums, back = [], [], []
    for chunk in range(CHUNKS):
        some, part, away = indexed(
            outer_kernel,
            (shape((rows, width), bf16), shape((8, rows), f32), shape((rows, width), bf16)),
            4 * rows * rows * width,
            8 * rows * width,
            [whole(NST, width)] * 2
            + [whole(1, width)]
            + [whole(rows, width)] * 4
            + [
                fixed((rows, NST), 0, 1),
                fixed((rows, NST), 0, width // NST + 1),
                columns(chunk),
            ],
            (whole(rows, width), whole(8, rows), whole(rows, width)),
        )(index_in, states[chunk], firsts[chunk], leads[chunk], *inner[chunk], maps, got[0], gate)
        gated.append(hand(some))
        sums.append(part)
        back.append(lax.ppermute(away, "ctx", partner))
    for chunk in range(CHUNKS):
        some, part = indexed(
            gate_kernel,
            (shape((rows, width), bf16), shape((8, rows), f32)),
            2 * rows * width,
            8 * rows * width,
            [whole(rows, width), others(chunk)],
            (whole(rows, width), whole(8, rows)),
        )(index_in, after(back[chunk], query, source, gated[chunk]), gate)
        gated.append(hand(some))
        sums.append(part)
    attention = None
    for group in range(groups):
        attention = attend(group, after(query, some, *gated[:3]), pieces, attention)
    sums = sum(sums)
    swap = [(i, (i + step) % tps) for step in range(1, tps) for i in range(tps)]
    sums = hand(sums + lax.ppermute(sums, "tp", swap))

    mamba = indexed(
        functools.partial(norm_kernel, channels * tps),
        shape((rows, channels), bf16),
        rows * channels,
        4 * rows * channels,
        [whole(rows, width)] * (2 * CHUNKS) + [whole(8, rows), whole(1, channels)],
        whole(rows, channels),
    )(index_in, *gated, sums, norm_gain.reshape(1, channels))
    return (mamba[None], attention[None])


def solution(mesh):
    placed = (
        P("segment", "ctx", "tp"),
        P("segment", "ctx", "tp"),
        P("segment", "ctx", "tp"),
        P("segment", "ctx", None),
        P("tp"),
        P("tp"),
        P("tp"),
        P("segment", "ctx", "tp"),
        P("segment", "ctx", "tp"),
        P("segment", "ctx", "tp"),
        P("segment"),
    )
    return jax.shard_map(
        on_device,
        mesh=mesh,
        in_specs=placed,
        out_specs=(P("segment", "ctx", "tp"), P("segment", "ctx", "tp")),
        check_vma=False,
    )
```

time: 214 us -> 82.1 us (0.38); the launches traced: 211 us -> 81.9 us
  blocking collectives: 64.8 us -> 0 us
  local copies, waits for them, and re-layouts: 45.2 us -> 0.99 us
  Pallas kernels: 0 us -> 23.8 us
  matrix products: 19.8 us -> 0 us
  other arithmetic: 15.9 us -> 0.01 us
  waiting for transfers between devices: 46.2 us -> 32.8 us
  starting transfers between devices: 17.3 us -> 23.5 us
    all_gather x3 -> x0, blocking collectives: 62.3 us -> none  [the longest x1 32.9 us: on_device(): value_piece = lax.all_gather(values[0], 'ctx', axis=0, tiled=True)]
    pallas_call x0 -> x14, Pallas kernels: none -> 23.8 us  [the longest x4 9.61 us: attend(): call(functools.partial(attention_kernel, ctx), shape((rows, groups * wide...]
    unnamed x39 -> x18, local copies, waits for them, and re-layouts: 22.9 us -> 0.82 us
    ppermute x2 -> x18, starting transfers between devices: 3.03 us -> 23.5 us  [the longest x8 11.4 us: hand(): return lax.ppermute(array, 'segment', onward)]
    dot_general x6 -> x0, matrix products: 19.8 us -> none  [the longest x1 5.52 us: on_device(): jnp.einsum('kgts,skd->kgtd', weights.astype(jnp.bfloat16), value_head_row...]
    all_to_all x3 -> x0, waiting for transfers between devices: 16.3 us -> none  [the longest x1 16.3 us: on_device(): lax.all_to_all(mixer_in, 'ctx', split_axis=1, concat_axis=0, tiled=True)]
    all_to_all x3 -> x0, starting transfers between devices: 14.3 us -> none  [the longest x1 6.46 us: on_device(): lax.all_to_all(step_in, 'ctx', split_axis=1, concat_axis=0, tiled=True)]
    slice x5 -> x0, local copies, waits for them, and re-layouts: 12.4 us -> none  [the longest x1 12.3 us: scan_blocks(): inc_states[:-1]]
  transfers between devices with their start and end apart: 5 -> 18, of which waited for: 3 -> 8; matrix products, arithmetic and copies ran while one was open for 17% -> 0% of each run, Pallas kernels for 0% -> 25%
where the time goes in v2:
time: 82.1 us; the launch traced here: 81.9 us
  waiting for transfers between devices  32.8 us (40%)
  Pallas kernels  23.8 us (29%)
  starting transfers between devices  23.5 us (29%)
  local copies, waits for them, and re-layouts  0.99 us (1%)
    ppermute x8, starting transfers between devices, hand(): return lax.ppermute(array, 'segment', onward)  11.4 us
    ppermute x2, waiting for transfers between devices, on_device(): enter = lax.ppermute(state, 'ctx', further)  10.8 us
    pallas_call x4, Pallas kernels, attend(): call(functools.partial(attention_kernel, ctx), shape((rows, groups * wide...  9.61 us
    ppermute x2, waiting for transfers between devices, on_device(): got = [lax.ppermute(parcel, 'ctx', partner) for parcel in parcels]  7.43 us
    ppermute x3, waiting for transfers between devices, on_device(): pieces = pieces + [lax.ppermute(piece, 'ctx', swap) for piece in pieces]  5.67 us
    ppermute x2, waiting for transfers between devices, on_device(): back.append(lax.ppermute(away, 'ctx', partner))  5.3 us
    pallas_call x2, Pallas kernels, on_device(): indexed(functools.partial(inner_kernel, chunk), (shape((rows, width), f32...  4.43 us
    ppermute x2, starting transfers between devices, on_device(): enter = lax.ppermute(state, 'ctx', further)  4.37 us
  transfers between devices with their start and end apart: 18, of which 8 were waited for; matrix products, arithmetic and copies ran while one was open for 0% of the time, Pallas kernels for 25%

profile of v2, /device:TPU:0, one launch (start us, length us, event | category | flops | bytes accessed | tf_op | source)
XLA Modules:
  0.0 81.9 jit_solution(3479043346745212272)
XLA Ops:
  0.7 2.2 %shard_map.122 = (bf16[128,1408]{1,0:T(8,128)(2,1)}, bf16[128,1024]{1,0:T(8,128)(2,1)}, bf16[128,1024]{1,0:T(8,128)(2,1)}) custom-call(s32[1]{0:T(128)} %bitcast.index_ref, bf16[128,4096]{1,0:T(8,128)(2,1)} %bitcast.15, bf16[128,256]{1,0:T(8,128)(2,1)} %bitcast.24, bf16[64,128]{1,0:T(8,128)(2,1)} %bitcast.31, bf16[128,512]{1,0:T(8,128)(2,1)} %bitcast.45, ...), custom_call_target="tpu_custom_call" | custom-call | bytes 1048576 | tf_op jit(solution)/shard_map/pallas_call | solution.py:335
  2.9 3.1 %collective-permute-start = (bf16[128,1408]{1,0:T(8,128)(2,1)}, bf16[128,1408]{1,0:T(8,128)(2,1)S(1)}, u32[]{:S(2)}, u32[]{:S(2)}) collective-permute-start(bf16[128,1408]{1,0:T(8,128)(2,1)} %get-tuple-element.33), channel_id=1, source_target_pairs={{0,2},{2,0},{4,6},{6,4},{1,3},{3,1},{5,7},{7,5},{8,10},{10,8},{12,... | collective-permute-start | bytes 1081352 | tf_op jit(solution)/shard_map/ppermute | solution.py:349
  5.9 1.5 %collective-permute-start.7 = (bf16[128,4096]{1,0:T(8,128)(2,1)}, bf16[128,4096]{1,0:T(8,128)(2,1)S(1)}, u32[]{:S(2)}, u32[]{:S(2)}) collective-permute-start(bf16[128,4096]{1,0:T(8,128)(2,1)} %bitcast.47), channel_id=1, source_target_pairs={{0,8},{8,16},{16,24},{24,0},{1,9},{9,17},{17,25},{25,1},{2,10},{10... | collective-permute-start | bytes 3145736 | tf_op jit(solution)/shard_map/ppermute | solution.py:289
  8.0 7.4 %collective-permute-done.x2_ref.dt2_ref.b2_ref.maps2_ref.c2_ref = bf16[128,1408]{1,0:T(8,128)(2,1)S(1)} collective-permute-done((bf16[128,1408]{1,0:T(8,128)(2,1)}, bf16[128,1408]{1,0:T(8,128)(2,1)S(1)}, u32[]{:S(2)}, u32[]{:S(2)}) %collective-permute-start) | collective-permute-done | bytes 360480 | tf_op jit(solution)/shard_map/ppermute | solution.py:349
  15.4 1.9 %shard_map.123 = (bf16[128,1024]{1,0:T(8,128)(2,1)}, f32[128,1024]{1,0:T(8,128)S(1)}, f32[1,1024]{1,0:T(1,128)S(1)}, f32[1,1024]{1,0:T(1,128)}) custom-call(s32[1]{0:T(128)} %bitcast.index_ref, bf16[128,4096]{1,0:T(8,128)(2,1)S(1)} %bitcast.16, bf16[128,1408]{1,0:T(8,128)(2,1)S(1)} %collective-permute-done.x2_ref.dt2_ref.b2_ref.maps2_ref.c2_ref, ...), custom_call_target="tpu_custom_call" | custom-call | flops 67108864 | bytes 524288 | tf_op jit(solution)/shard_map/pallas_call | solution.py:363
  17.3 0.8 copy-done.3
  18.1 3.1 %collective-permute-start.1 = (bf16[128,1024]{1,0:T(8,128)(2,1)}, bf16[128,1024]{1,0:T(8,128)(2,1)S(1)}, u32[]{:S(2)}, u32[]{:S(2)}) collective-permute-start(bf16[128,1024]{1,0:T(8,128)(2,1)} %get-tuple-element.34), channel_id=1, source_target_pairs={{0,4},{2,6},{4,0},{6,2},{1,5},{3,7},{5,1},{7,3},{8,12},{10,14},{12... | collective-permute-start | bytes 786440 | tf_op jit(solution)/shard_map/ppermute | solution.py:371
  21.2 1.5 %collective-permute-start.14 = (bf16[128,1024]{1,0:T(8,128)(2,1)}, bf16[128,1024]{1,0:T(8,128)(2,1)S(1)}, u32[]{:S(2)}, u32[]{:S(2)}) collective-permute-start(bf16[128,1024]{1,0:T(8,128)(2,1)} %get-tuple-element.62), channel_id=1, source_target_pairs={{0,8},{8,16},{16,24},{24,0},{1,9},{9,17},{17,25},{25,1},{2,10},{10... | collective-permute-start | bytes 786440 | tf_op jit(solution)/shard_map/ppermute | solution.py:289
  22.8 1.9 %shard_map.126 = (bf16[128,1024]{1,0:T(8,128)(2,1)S(1)}, f32[128,1024]{1,0:T(8,128)S(1)}, f32[1,1024]{1,0:T(1,128)S(1)}, f32[1,1024]{1,0:T(1,128)}) custom-call(s32[1]{0:T(128)} %bitcast.index_ref, bf16[128,4096]{1,0:T(8,128)(2,1)S(1)} %bitcast.17, bf16[128,1024]{1,0:T(8,128)(2,1)S(1)} %collective-permute-done.3.x2_ref, bf16[64,128]{1,0:T(8,128)(2,1)S(1)} %bitcast.33, ...), custom_call_target="tpu_custom_call" | custom-call | flops 67108864 | bytes 524288 | tf_op jit(solution)/shard_map/pallas_call | solution.py:363
  24.7 1.3 %collective-permute-start.4 = (bf16[128,1024]{1,0:T(8,128)(2,1)S(1)}, bf16[128,1024]{1,0:T(8,128)(2,1)S(1)}, u32[]{:S(2)}, u32[]{:S(2)}) collective-permute-start(bf16[128,1024]{1,0:T(8,128)(2,1)S(1)} %get-tuple-element.43), channel_id=1, source_target_pairs={{0,4},{2,6},{4,0},{6,2},{1,5},{3,7},{5,1},{7,3},{8,12},{10,14},{12... | collective-permute-start | bytes 786440 | tf_op jit(solution)/shard_map/ppermute | solution.py:371
  26.0 2.1 %shard_map.124 = (f32[128,1024]{1,0:T(8,128)S(1)}, f32[128,1024]{1,0:T(8,128)S(1)}, f32[128,1024]{1,0:T(8,128)S(1)}, f32[128,1024]{1,0:T(8,128)S(1)}) custom-call(s32[1]{0:T(128)} %bitcast.index_ref, bf16[128,4096]{1,0:T(8,128)(2,1)S(1)} %bitcast.18, bf16[128,1408]{1,0:T(8,128)(2,1)S(1)} %collective-permute-done.x2_ref.dt2_ref.b2_ref.maps2_ref.c2_ref, ...), custom_call_target="tpu_custom_call" | custom-call | flops 134217728 | bytes 786432 | tf_op jit(solution)/shard_map/pallas_call | solution.py:380
  28.2 10.8 %collective-permute-done.1.enter_ref = bf16[128,1024]{1,0:T(8,128)(2,1)S(1)} collective-permute-done((bf16[128,1024]{1,0:T(8,128)(2,1)}, bf16[128,1024]{1,0:T(8,128)(2,1)S(1)}, u32[]{:S(2)}, u32[]{:S(2)}) %collective-permute-start.1) | collective-permute-done | bytes 262176 | tf_op jit(solution)/shard_map/ppermute | solution.py:371
  39.0 0.8 shard_map.125
  39.8 1.7 %collective-permute-start.2 = (bf16[128,1024]{1,0:T(8,128)(2,1)S(1)}, bf16[128,1024]{1,0:T(8,128)(2,1)S(1)}, u32[]{:S(2)}, u32[]{:S(2)}) collective-permute-start(bf16[128,1024]{1,0:T(8,128)(2,1)S(1)} %get-tuple-element.41), channel_id=1, source_target_pairs={{0,8},{8,16},{16,24},{24,0},{1,9},{9,17},{17,25},{25,1},{2,10},{10... | collective-permute-start | bytes 786440 | tf_op jit(solution)/shard_map/ppermute | solution.py:289
  41.5 2.2 %collective-permute-start.15 = (bf16[128,1024]{1,0:T(8,128)(2,1)S(1)}, bf16[128,1024]{1,0:T(8,128)(2,1)S(1)}, u32[]{:S(2)}, u32[]{:S(2)}) collective-permute-start(bf16[128,1024]{1,0:T(8,128)(2,1)S(1)} %collective-permute-done.14.refs_0_.refs_4_), channel_id=1, source_target_pairs={{0,4},{2,6},{4,0},{6,2},{1,5},{3,7},{5,1},{7,3},{8,12},{10,14},{12... | collective-permute-start | bytes 786440 | tf_op jit(solution)/shard_map/ppermute | solution.py:418
  43.7 2.3 %shard_map.127 = (f32[128,1024]{1,0:T(8,128)S(1)}, f32[128,1024]{1,0:T(8,128)S(1)}, f32[128,1024]{1,0:T(8,128)S(1)}, f32[128,1024]{1,0:T(8,128)S(1)}) custom-call(s32[1]{0:T(128)} %bitcast.index_ref, bf16[128,4096]{1,0:T(8,128)(2,1)S(1)} %bitcast.19, bf16[128,1024]{1,0:T(8,128)(2,1)S(1)} %collective-permute-done.3.x2_ref, bf16[64,128]{1,0:T(8,128)(2,1)S(1)} %bitcast.35, ...), custom_call_target="tpu_custom_call" | custom-call | flops 134217728 | bytes 786432 | tf_op jit(solution)/shard_map/pallas_call | solution.py:380
  46.0 1.5 %collective-permute-start.8 = (s32[1]{0:T(128)}, s32[1]{0:T(128)}, u32[]{:S(2)}, u32[]{:S(2)}) collective-permute-start(s32[1]{0:T(128)} %param.21), channel_id=1, source_target_pairs={{0,8},{8,16},{16,24},{24,0},{1,9},{9,17},{17,25},{25,1},{2,10},{10... | collective-permute-start | bytes 20 | tf_op jit(solution)/shard_map/ppermute | solution.py:289
  47.5 0.8 shard_map.128
  48.3 2.4 %collective-permute-done.8.source_ref = s32[1]{0:T(128)} collective-permute-done((s32[1]{0:T(128)}, s32[1]{0:T(128)}, u32[]{:S(2)}, u32[]{:S(2)}) %collective-permute-start.8) | collective-permute-done | bytes 36 | tf_op jit(solution)/shard_map/ppermute | solution.py:289
  51.3 3.6 %collective-permute-done.6.raw_ref = bf16[128,1024]{1,0:T(8,128)(2,1)S(1)} collective-permute-done((bf16[128,1024]{1,0:T(8,128)(2,1)S(1)}, bf16[128,1024]{1,0:T(8,128)(2,1)S(1)}, u32[]{:S(2)}, u32[]{:S(2)}) %collective-permute-start.6) | collective-permute-done | bytes 262176 | tf_op jit(solution)/shard_map/ppermute | solution.py:440
  55.4 1.5 %collective-permute-start.9 = (bf16[128,1024]{1,0:T(8,128)(2,1)S(1)}, bf16[128,1024]{1,0:T(8,128)(2,1)S(1)}, u32[]{:S(2)}, u32[]{:S(2)}) collective-permute-start(bf16[128,1024]{1,0:T(8,128)(2,1)S(1)} %get-tuple-element.53), channel_id=1, source_target_pairs={{0,8},{8,16},{16,24},{24,0},{1,9},{9,17},{17,25},{25,1},{2,10},{10... | collective-permute-start | bytes 786440 | tf_op jit(solution)/shard_map/ppermute | solution.py:289
  56.9 2.0 %collective-permute-start.17 = (bf16[128,1024]{1,0:T(8,128)(2,1)S(1)}, bf16[128,1024]{1,0:T(8,128)(2,1)S(1)}, u32[]{:S(2)}, u32[]{:S(2)}) collective-permute-start(bf16[128,1024]{1,0:T(8,128)(2,1)S(1)} %collective-permute-done.15.refs_1_.refs_5_), channel_id=1, source_target_pairs={{0,2},{2,0},{4,6},{6,4},{1,3},{3,1},{5,7},{7,5},{8,10},{10,8},{12,... | collective-permute-start | bytes 786440 | tf_op jit(solution)/shard_map/ppermute | solution.py:418
  58.9 1.7 %collective-permute-done.10.raw_ref = bf16[128,1024]{1,0:T(8,128)(2,1)S(1)} collective-permute-done((bf16[128,1024]{1,0:T(8,128)(2,1)S(1)}, bf16[128,1024]{1,0:T(8,128)(2,1)S(1)}, u32[]{:S(2)}, u32[]{:S(2)}) %collective-permute-start.10) | collective-permute-done | bytes 262176 | tf_op jit(solution)/shard_map/ppermute | solution.py:440
  61.0 2.4 %collective-permute-start.11 = (bf16[128,1024]{1,0:T(8,128)(2,1)S(1)}, bf16[128,1024]{1,0:T(8,128)(2,1)S(1)}, u32[]{:S(2)}, u32[]{:S(2)}) collective-permute-start(bf16[128,1024]{1,0:T(8,128)(2,1)S(1)} %get-tuple-element.56), channel_id=1, source_target_pairs={{0,8},{8,16},{16,24},{24,0},{1,9},{9,17},{17,25},{25,1},{2,10},{10... | collective-permute-start | bytes 786440 | tf_op jit(solution)/shard_map/ppermute | solution.py:289
  63.4 1.2 %collective-permute-done.12 = f32[8,128]{1,0:T(8,128)S(1)} collective-permute-done((f32[8,128]{1,0:T(8,128)S(1)}, f32[8,128]{1,0:T(8,128)S(1)}, u32[]{:S(2)}, u32[]{:S(2)}) %collective-permute-start.12) | collective-permute-done | bytes 4128 | tf_op jit(solution)/shard_map/ppermute | solution.py:457
  65.2 1.0 %collective-permute-done.16.refs_2_.refs_6_ = bf16[128,1024]{1,0:T(8,128)(2,1)S(1)} collective-permute-done((bf16[128,1024]{1,0:T(8,128)(2,1)S(1)}, bf16[128,1024]{1,0:T(8,128)(2,1)S(1)}, u32[]{:S(2)}, u32[]{:S(2)}) %collective-permute-start.16) | collective-permute-done | bytes 262176 | tf_op jit(solution)/shard_map/ppermute | solution.py:418
  66.2 4.7 %collective-permute-done.17.refs_3_.refs_7_ = bf16[128,1024]{1,0:T(8,128)(2,1)S(1)} collective-permute-done((bf16[128,1024]{1,0:T(8,128)(2,1)S(1)}, bf16[128,1024]{1,0:T(8,128)(2,1)S(1)}, u32[]{:S(2)}, u32[]{:S(2)}) %collective-permute-start.17) | collective-permute-done | bytes 262176 | tf_op jit(solution)/shard_map/ppermute | solution.py:418
  70.8 2.4 %shard_map.132.refs_8_ = bf16[128,4096]{1,0:T(8,128)(2,1)} custom-call(s32[1]{0:T(128)} %bitcast.index_ref, s32[1]{0:T(128)} %collective-permute-done.8.source_ref, bf16[128,4096]{1,0:T(8,128)(2,1)S(1)} %collective-permute-done.7.q_ref, bf16[128,1024]{1,0:T(8,128)(2,1)S(1)} %collective-permute-done.14.refs_0_.refs_4_, ...), custom_call_target="tpu_custom_call" | custom-call | flops 268435456 | bytes 524288 | tf_op jit(solution)/shard_map/pallas_call | solution.py:399
  73.2 2.4 %shard_map.133.refs_8_ = bf16[128,4096]{1,0:T(8,128)(2,1)} custom-call(s32[1]{0:T(128)} %bitcast.index_ref, s32[1]{0:T(128)} %collective-permute-done.8.source_ref, bf16[128,4096]{1,0:T(8,128)(2,1)S(1)} %collective-permute-done.7.q_ref, bf16[128,1024]{1,0:T(8,128)(2,1)S(1)} %collective-permute-done.14.refs_0_.refs_4_, ...), custom_call_target="tpu_custom_call", output_to_operand_aliasing={{}: (11, {})} | custom-call | flops 268435456 | bytes 524288 | tf_op jit(solution)/shard_map/pallas_call | solution.py:399
  75.6 2.4 %shard_map.134.refs_8_ = bf16[128,4096]{1,0:T(8,128)(2,1)} custom-call(s32[1]{0:T(128)} %bitcast.index_ref, s32[1]{0:T(128)} %collective-permute-done.8.source_ref, bf16[128,4096]{1,0:T(8,128)(2,1)S(1)} %collective-permute-done.7.q_ref, bf16[128,1024]{1,0:T(8,128)(2,1)S(1)} %collective-permute-done.14.refs_0_.refs_4_, ...), custom_call_target="tpu_custom_call", output_to_operand_aliasing={{}: (11, {})} | custom-call | flops 268435456 | bytes 524288 | tf_op jit(solution)/shard_map/pallas_call | solution.py:399
  78.0 2.4 %shard_map.135 = bf16[128,4096]{1,0:T(8,128)(2,1)} custom-call(s32[1]{0:T(128)} %bitcast.index_ref, s32[1]{0:T(128)} %collective-permute-done.8.source_ref, bf16[128,4096]{1,0:T(8,128)(2,1)S(1)} %collective-permute-done.7.q_ref, bf16[128,1024]{1,0:T(8,128)(2,1)S(1)} %collective-permute-done.14.refs_0_.refs_4_, ...), custom_call_target="tpu_custom_call", output_to_operand_aliasing={{}: (11, {})} | custom-call | flops 268435456 | bytes 524288 | tf_op jit(solution)/shard_map/pallas_call | solution.py:399
  80.5 1.4 %shard_map.131 = bf16[128,4096]{1,0:T(8,128)(2,1)} custom-call(s32[1]{0:T(128)} %bitcast.index_ref, bf16[128,1024]{1,0:T(8,128)(2,1)S(1)} %collective-permute-done.2.refs_0_, bf16[128,1024]{1,0:T(8,128)(2,1)S(1)} %collective-permute-done.5.refs_1_, bf16[128,1024]{1,0:T(8,128)(2,1)S(1)} %collective-permute-done.9.refs_2_, ...), custom_call_target="tpu_custom_call" | custom-call | flops 524288 | bytes 2097152 | tf_op jit(solution)/shard_map/pallas_call | solution.py:459
  (40 shorter events, 2.7 us)
Async XLA Ops:
  0.6 14.8 %copy-start = (bf16[1,128,4096]{2,1,0:T(8,128)(2,1)S(1)}, bf16[1,128,4096]{2,1,0:T(8,128)(2,1)}, u32[]{:S(2)}) copy-start(bf16[1,128,4096]{2,1,0:T(8,128)(2,1)} %param.11) | copy-start | bytes 3145732
  0.6 14.8 %copy-start.2 = (bf16[1,128,256]{2,1,0:T(8,128)(2,1)S(1)}, bf16[1,128,256]{2,1,0:T(8,128)(2,1)}, u32[]{:S(2)}) copy-start(bf16[1,128,256]{2,1,0:T(8,128)(2,1)} %param.14) | copy-start | bytes 196612
  0.7 14.7 %copy-start.5 = (bf16[1,128,64]{1,2,0:T(8,128)(2,1)S(1)}, bf16[1,128,64]{1,2,0:T(8,128)(2,1)}, u32[]{:S(2)}) copy-start(bf16[1,128,64]{1,2,0:T(8,128)(2,1)} %param.13) | copy-start | bytes 49156
  2.9 12.5 %collective-permute-start = (bf16[128,1408]{1,0:T(8,128)(2,1)}, bf16[128,1408]{1,0:T(8,128)(2,1)S(1)}, u32[]{:S(2)}, u32[]{:S(2)}) collective-permute-start(bf16[128,1408]{1,0:T(8,128)(2,1)} %get-tuple-element.33), channel_id=1, source_target_pairs={{0,2},{2,0},{4,6},{6,4},{1,3},{3,1},{5,7},{7,5},{8,10},{10,8},{12,... | collective-permute-start | bytes 1081352 | tf_op jit(solution)/shard_map/ppermute | solution.py:349
  5.9 1.9 %copy-start.7 = (f32[64]{0:T(128)S(1)}, f32[64]{0:T(128)}, u32[]{:S(2)}) copy-start(f32[64]{0:T(128)} %param.15) | copy-start | bytes 772
  5.9 49.0 %collective-permute-start.7 = (bf16[128,4096]{1,0:T(8,128)(2,1)}, bf16[128,4096]{1,0:T(8,128)(2,1)S(1)}, u32[]{:S(2)}, u32[]{:S(2)}) collective-permute-start(bf16[128,4096]{1,0:T(8,128)(2,1)} %bitcast.47), channel_id=1, source_target_pairs={{0,8},{8,16},{16,24},{24,0},{1,9},{9,17},{17,25},{25,1},{2,10},{10... | collective-permute-start | bytes 3145736 | tf_op jit(solution)/shard_map/ppermute | solution.py:289
  7.4 15.3 %collective-permute-start.3 = (bf16[128,1024]{1,0:T(8,128)(2,1)}, bf16[128,1024]{1,0:T(8,128)(2,1)S(1)}, u32[]{:S(2)}, u32[]{:S(2)}) collective-permute-start(bf16[128,1024]{1,0:T(8,128)(2,1)} %get-tuple-element.42), channel_id=1, source_target_pairs={{0,2},{2,0},{4,6},{6,4},{1,3},{3,1},{5,7},{7,5},{8,10},{10,8},{12,... | collective-permute-start | bytes 786440 | tf_op jit(solution)/shard_map/ppermute | solution.py:349
  17.3 0.8 copy-start.3
  18.1 4.6 %copy-start.8 = (f32[64]{0:T(128)S(1)}, f32[64]{0:T(128)}, u32[]{:S(2)}) copy-start(f32[64]{0:T(128)} %param.16) | copy-start | bytes 772
  18.1 20.9 %collective-permute-start.1 = (bf16[128,1024]{1,0:T(8,128)(2,1)}, bf16[128,1024]{1,0:T(8,128)(2,1)S(1)}, u32[]{:S(2)}, u32[]{:S(2)}) collective-permute-start(bf16[128,1024]{1,0:T(8,128)(2,1)} %get-tuple-element.34), channel_id=1, source_target_pairs={{0,4},{2,6},{4,0},{6,2},{1,5},{3,7},{5,1},{7,3},{8,12},{10,14},{12... | collective-permute-start | bytes 786440 | tf_op jit(solution)/shard_map/ppermute | solution.py:371
  21.2 20.3 %collective-permute-start.14 = (bf16[128,1024]{1,0:T(8,128)(2,1)}, bf16[128,1024]{1,0:T(8,128)(2,1)S(1)}, u32[]{:S(2)}, u32[]{:S(2)}) collective-permute-start(bf16[128,1024]{1,0:T(8,128)(2,1)} %get-tuple-element.62), channel_id=1, source_target_pairs={{0,8},{8,16},{16,24},{24,0},{1,9},{9,17},{17,25},{25,1},{2,10},{10... | collective-permute-start | bytes 786440 | tf_op jit(solution)/shard_map/ppermute | solution.py:289
  24.7 21.3 %collective-permute-start.4 = (bf16[128,1024]{1,0:T(8,128)(2,1)S(1)}, bf16[128,1024]{1,0:T(8,128)(2,1)S(1)}, u32[]{:S(2)}, u32[]{:S(2)}) collective-permute-start(bf16[128,1024]{1,0:T(8,128)(2,1)S(1)} %get-tuple-element.43), channel_id=1, source_target_pairs={{0,4},{2,6},{4,0},{6,2},{1,5},{3,7},{5,1},{7,3},{8,12},{10,14},{12... | collective-permute-start | bytes 786440 | tf_op jit(solution)/shard_map/ppermute | solution.py:371
  26.0 13.0 %copy-start.1 = (bf16[1,128,4096]{2,1,0:T(8,128)(2,1)S(1)}, bf16[1,128,4096]{2,1,0:T(8,128)(2,1)}, u32[]{:S(2)}) copy-start(bf16[1,128,4096]{2,1,0:T(8,128)(2,1)} %param.12) | copy-start | bytes 3145732
  26.0 13.0 %copy-start.4 = (f32[128,1024]{1,0:T(8,128)S(1)}, f32[128,1024]{1,0:T(8,128)}, u32[]{:S(2)}) copy-start(f32[128,1024]{1,0:T(8,128)} %copy-done.3) | copy-start | bytes 1572868
  39.8 11.5 %collective-permute-start.2 = (bf16[128,1024]{1,0:T(8,128)(2,1)S(1)}, bf16[128,1024]{1,0:T(8,128)(2,1)S(1)}, u32[]{:S(2)}, u32[]{:S(2)}) collective-permute-start(bf16[128,1024]{1,0:T(8,128)(2,1)S(1)} %get-tuple-element.41), channel_id=1, source_target_pairs={{0,8},{8,16},{16,24},{24,0},{1,9},{9,17},{17,25},{25,1},{2,10},{10... | collective-permute-start | bytes 786440 | tf_op jit(solution)/shard_map/ppermute | solution.py:289
  41.4 13.5 %collective-permute-start.6 = (bf16[128,1024]{1,0:T(8,128)(2,1)S(1)}, bf16[128,1024]{1,0:T(8,128)(2,1)S(1)}, u32[]{:S(2)}, u32[]{:S(2)}) collective-permute-start(bf16[128,1024]{1,0:T(8,128)(2,1)S(1)} %get-tuple-element.51), channel_id=1, source_target_pairs={{0,2},{2,0},{4,6},{6,4},{1,3},{3,1},{5,7},{7,5},{8,10},{10,8},{12,... | collective-permute-start | bytes 786440 | tf_op jit(solution)/shard_map/ppermute | solution.py:440
  41.5 15.4 %collective-permute-start.15 = (bf16[128,1024]{1,0:T(8,128)(2,1)S(1)}, bf16[128,1024]{1,0:T(8,128)(2,1)S(1)}, u32[]{:S(2)}, u32[]{:S(2)}) collective-permute-start(bf16[128,1024]{1,0:T(8,128)(2,1)S(1)} %collective-permute-done.14.refs_0_.refs_4_), channel_id=1, source_target_pairs={{0,4},{2,6},{4,0},{6,2},{1,5},{3,7},{5,1},{7,3},{8,12},{10,14},{12... | collective-permute-start | bytes 786440 | tf_op jit(solution)/shard_map/ppermute | solution.py:418
  46.0 4.7 %collective-permute-start.8 = (s32[1]{0:T(128)}, s32[1]{0:T(128)}, u32[]{:S(2)}, u32[]{:S(2)}) collective-permute-start(s32[1]{0:T(128)} %param.21), channel_id=1, source_target_pairs={{0,8},{8,16},{16,24},{24,0},{1,9},{9,17},{17,25},{25,1},{2,10},{10... | collective-permute-start | bytes 20 | tf_op jit(solution)/shard_map/ppermute | solution.py:289
  50.7 8.2 %collective-permute-start.5 = (bf16[128,1024]{1,0:T(8,128)(2,1)S(1)}, bf16[128,1024]{1,0:T(8,128)(2,1)S(1)}, u32[]{:S(2)}, u32[]{:S(2)}) collective-permute-start(bf16[128,1024]{1,0:T(8,128)(2,1)S(1)} %get-tuple-element.50), channel_id=1, source_target_pairs={{0,8},{8,16},{16,24},{24,0},{1,9},{9,17},{17,25},{25,1},{2,10},{10... | collective-permute-start | bytes 786440 | tf_op jit(solution)/shard_map/ppermute | solution.py:289
  51.3 9.3 %collective-permute-start.10 = (bf16[128,1024]{1,0:T(8,128)(2,1)S(1)}, bf16[128,1024]{1,0:T(8,128)(2,1)S(1)}, u32[]{:S(2)}, u32[]{:S(2)}) collective-permute-start(bf16[128,1024]{1,0:T(8,128)(2,1)S(1)} %get-tuple-element.54), channel_id=1, source_target_pairs={{0,2},{2,0},{4,6},{6,4},{1,3},{3,1},{5,7},{7,5},{8,10},{10,8},{12,... | collective-permute-start | bytes 786440 | tf_op jit(solution)/shard_map/ppermute | solution.py:440
  55.4 9.8 %collective-permute-start.9 = (bf16[128,1024]{1,0:T(8,128)(2,1)S(1)}, bf16[128,1024]{1,0:T(8,128)(2,1)S(1)}, u32[]{:S(2)}, u32[]{:S(2)}) collective-permute-start(bf16[128,1024]{1,0:T(8,128)(2,1)S(1)} %get-tuple-element.53), channel_id=1, source_target_pairs={{0,8},{8,16},{16,24},{24,0},{1,9},{9,17},{17,25},{25,1},{2,10},{10... | collective-permute-start | bytes 786440 | tf_op jit(solution)/shard_map/ppermute | solution.py:289
  56.9 9.3 %collective-permute-start.16 = (bf16[128,1024]{1,0:T(8,128)(2,1)S(1)}, bf16[128,1024]{1,0:T(8,128)(2,1)S(1)}, u32[]{:S(2)}, u32[]{:S(2)}) collective-permute-start(bf16[128,1024]{1,0:T(8,128)(2,1)S(1)} %collective-permute-done.14.refs_0_.refs_4_), channel_id=1, source_target_pairs={{0,2},{2,0},{4,6},{6,4},{1,3},{3,1},{5,7},{7,5},{8,10},{10,8},{12,... | collective-permute-start | bytes 786440 | tf_op jit(solution)/shard_map/ppermute | solution.py:418
  56.9 14.0 %collective-permute-start.17 = (bf16[128,1024]{1,0:T(8,128)(2,1)S(1)}, bf16[128,1024]{1,0:T(8,128)(2,1)S(1)}, u32[]{:S(2)}, u32[]{:S(2)}) collective-permute-start(bf16[128,1024]{1,0:T(8,128)(2,1)S(1)} %collective-permute-done.15.refs_1_.refs_5_), channel_id=1, source_target_pairs={{0,2},{2,0},{4,6},{6,4},{1,3},{3,1},{5,7},{7,5},{8,10},{10,8},{12,... | collective-permute-start | bytes 786440 | tf_op jit(solution)/shard_map/ppermute | solution.py:418
  61.0 19.5 %collective-permute-start.11 = (bf16[128,1024]{1,0:T(8,128)(2,1)S(1)}, bf16[128,1024]{1,0:T(8,128)(2,1)S(1)}, u32[]{:S(2)}, u32[]{:S(2)}) collective-permute-start(bf16[128,1024]{1,0:T(8,128)(2,1)S(1)} %get-tuple-element.56), channel_id=1, source_target_pairs={{0,8},{8,16},{16,24},{24,0},{1,9},{9,17},{17,25},{25,1},{2,10},{10... | collective-permute-start | bytes 786440 | tf_op jit(solution)/shard_map/ppermute | solution.py:289
  63.4 1.2 %collective-permute-start.12 = (f32[8,128]{1,0:T(8,128)S(1)}, f32[8,128]{1,0:T(8,128)S(1)}, u32[]{:S(2)}, u32[]{:S(2)}) collective-permute-start(f32[8,128]{1,0:T(8,128)S(1)} %add_add_fusion), channel_id=1, source_target_pairs={{0,1},{1,0},{2,3},{3,2},{4,5},{5,4},{6,7},{7,6},{8,9},{9,8},{10,11... | collective-permute-start | bytes 12296 | tf_op jit(solution)/shard_map/ppermute | solution.py:457
  64.5 15.9 %collective-permute-start.13 = (f32[8,128]{1,0:T(8,128)S(1)}, f32[8,128]{1,0:T(8,128)S(1)}, u32[]{:S(2)}, u32[]{:S(2)}) collective-permute-start(f32[8,128]{1,0:T(8,128)S(1)} %add.15), channel_id=1, source_target_pairs={{0,8},{8,16},{16,24},{24,0},{1,9},{9,17},{17,25},{25,1},{2,10},{10... | collective-permute-start | bytes 12296 | tf_op jit(solution)/shard_map/ppermute | solution.py:289
  78.0 2.4 %copy-start.6 = (f32[4096]{0:T(1024)S(1)}, f32[4096]{0:T(1024)}, u32[]{:S(2)}) copy-start(f32[4096]{0:T(1024)} %param.17) | copy-start | bytes 49156

commit v3 on v2

--- a/solution.py
+++ b/solution.py
@@ -55,8 +55,10 @@
     )
 
 
-def parcel_kernel(index_ref, x_ref, maps_ref, dt_ref, key_ref, value_ref, *refs):
-    *parcel_refs, packed_ref, sem = refs
+def parcel_kernel(
+    index_ref, x_ref, maps_ref, dt_ref, key_ref, value_ref, rate_ref, skip_ref, *refs
+):
+    *parcel_refs, packed_ref, rate_out, skip_out, sem = refs
     rows = x_ref.shape[0]
     side, half = x_ref.shape[1] // 2, dt_ref.shape[0] // 2
     width, kv = side // CHUNKS, key_ref.shape[1]
@@ -78,6 +80,8 @@
     )
     moves.append((key_ref, packed_ref.at[:, pl.ds(0, kv)]))
     moves.append((value_ref, packed_ref.at[:, pl.ds(kv, kv)]))
+    moves.append((rate_ref, rate_out))
+    moves.append((skip_ref, skip_out))
     copies = [
         pltpu.make_async_copy(src, dst, sem.at[number]) for number, (src, dst) in enumerate(moves)
     ]
@@ -85,6 +89,14 @@
         copy.start()
     for copy in copies:
         copy.wait()
+
+
+def own_heads(ref, early, chunk, count):
+    row = ref[...]
+    half = row.shape[1] // 2
+    low = row[:, chunk * count : chunk * count + count]
+    high = row[:, half + chunk * count : half + chunk * count + count]
+    return jnp.where(early, low, high)
 
 
 def decays(dt, rate, heads):
@@ -104,7 +116,7 @@
     count = width // HP
     at = slice(chunk * count, chunk * count + count)
     early = index_ref[0] % 2 == 0
-    rate = rate_ref[0][:, at]
+    rate = own_heads(rate_ref, early, chunk, count)
     halves = []
     for x, dt, b in ((x_ref, dt_ref, b_ref), (x2_ref, dt2_ref, b2_ref)):
         step = dt[at, :]
@@ -137,12 +149,13 @@
     chunk, index_ref, x_ref, x2_ref, dt_ref, dt2_ref, rate_ref, skip_ref, maps_ref, maps2_ref,
     out_ref, grow_ref, out2_ref, grow2_ref,
 ):
-    del index_ref
+    early = index_ref[0] % 2 == 0
     rows, width = x_ref.shape
     count = width // HP
     at = slice(chunk * count, chunk * count + count)
     lane = lax.broadcasted_iota(jnp.int32, (rows, 128), 1)
-    rate, skip = rate_ref[0][:, at], skip_ref[0][:, at]
+    rate = own_heads(rate_ref, early, chunk, count)
+    skip = own_heads(skip_ref, early, chunk, count)
     for x, dt, maps, out, spread_out in (
         (x_ref, dt_ref, maps_ref, out_ref, grow_ref),
         (x2_ref, dt2_ref, maps2_ref, out2_ref, grow2_ref),
@@ -299,8 +312,6 @@
     side = channels // 2
     width = side // CHUNKS
     wire = bf16 if ctx <= 8 else f32
-    rate = decay_rate.reshape(2, 1, half)
-    skip = skip_gain.reshape(2, 1, half)
     groups = keys.shape[2] // HEAD_WIDTH
     wide = GROUP * HEAD_WIDTH
 
@@ -332,30 +343,41 @@
     parcel_width = width + 2 * NST + rows
     hbm = pl.BlockSpec(memory_space=pltpu.HBM)
     kv_width = 2 * groups * HEAD_WIDTH
-    *parcels, packed = indexed(
+    *parcels, packed, rate, skip = indexed(
         parcel_kernel,
         (shape((rows, parcel_width), bf16),)
         + (shape((rows, width), bf16),) * (CHUNKS - 1)
-        + (shape((rows, kv_width), bf16),),
+        + (shape((rows, kv_width), bf16),)
+        + (shape((1, heads), f32),) * 2,
         0,
         4 * rows * side,
-        [hbm] * 5,
+        [hbm] * 7,
         (whole(rows, parcel_width),)
         + (whole(rows, width),) * (CHUNKS - 1)
-        + (whole(rows, kv_width),),
-        [pltpu.SemaphoreType.DMA((CHUNKS + 4,))],
+        + (whole(rows, kv_width),)
+        + (whole(1, heads),) * 2,
+        [pltpu.SemaphoreType.DMA((CHUNKS + 6,))],
         PARCEL_VMEM,
-    )(index_in, x, maps, dt, keys[0], values[0])
+    )(
+        index_in,
+        x,
+        maps,
+        dt,
+        keys[0],
+        values[0],
+        decay_rate.reshape(1, heads),
+        skip_gain.reshape(1, heads),
+    )
     got = [lax.ppermute(parcel, "ctx", partner) for parcel in parcels]
     key_values = hand(packed)
-    query = hand(queries[0])
     source = hand(source_len)
+    query = hand(after(queries[0], key_values, got[0], source))
     pairs = [
         columns,
         lambda chunk: whole(rows, width),
         lambda chunk: mine((half, rows)),
         lambda chunk: fixed((half, rows), 0, (width + 2 * NST) // rows),
-        lambda chunk: mine((1, 1, half)),
+        lambda chunk: whole(1, heads),
     ]
     places = lambda chunk: [spec(chunk) for spec in pairs]
     states, firsts, leads, inner = [], [], [], []
@@ -375,6 +397,7 @@
         states.append(enter)
         firsts.append(first)
         leads.append(lead)
+    nearby = lax.ppermute(after(key_values, firsts[0]), "ctx", partner)
     for chunk in range(CHUNKS):
         inner.append(
             indexed(
@@ -384,7 +407,7 @@
                 6 * rows * width,
                 places(chunk)
                 + [
-                    mine((1, 1, half)),
+                    whole(1, heads),
                     whole(rows, 2 * NST),
                     fixed((rows, 2 * NST), 0, width // (2 * NST)),
                 ],
@@ -393,31 +416,16 @@
         )
     scalar = pl.BlockSpec(memory_space=pltpu.SMEM)
 
-    def attend(group, query, pieces, out):
-        more = [] if out is None else [out]
-        spot = lambda at: pl.BlockSpec((rows, HEAD_WIDTH), lambda i: (0, at))
-        return call(
-            functools.partial(attention_kernel, ctx),
-            shape((rows, groups * wide), bf16),
-            4 * rows * wide * ctx * rows,
-            4 * rows * wide,
-            grid=(1,),
-            in_specs=[scalar, scalar, pl.BlockSpec((rows, wide), lambda i: (0, group))]
-            + [spot(group)] * ctx
-            + [spot(group + groups)] * ctx
-            + [pl.BlockSpec(memory_space=pl.ANY)] * len(more),
-            out_specs=pl.BlockSpec((rows, wide), lambda i: (0, group)),
-            scratch_shapes=[pltpu.VMEM((ctx * rows, rows), f32)],
-            input_output_aliases={3 + 2 * ctx: 0} if more else {},
-        )(index_in, source, query, *pieces, *pieces, *more)
-
-    pieces = [after(key_values, states[0])]
+
+    pieces = [key_values]
     step = ctx // 2
-    while step >= 1:
+    while step > 1:
         swap = [(i, i ^ step) for i in range(ctx)]
-        pieces = pieces + [lax.ppermute(piece, "ctx", swap) for piece in pieces]
+        pieces = pieces + [
+            lax.ppermute(after(piece, states[0]), "ctx", swap) for piece in pieces
+        ]
         step //= 2
-
+    pieces = pieces + [nearby] + [lax.ppermute(piece, "ctx", partner) for piece in pieces[1:]]
     gated, sums, back = [], [], []
     for chunk in range(CHUNKS):
         some, part, away = indexed(
@@ -434,7 +442,7 @@
                 columns(chunk),
             ],
             (whole(rows, width), whole(8, rows), whole(rows, width)),
-        )(index_in, states[chunk], firsts[chunk], leads[chunk], *inner[chunk], maps, got[0], gate)
+        )(index_in, after(states[chunk], query, nearby) if chunk else after(states[chunk], *[part for parts in inner for part in parts]), firsts[chunk], leads[chunk], *inner[chunk], maps, got[0], gate)
         gated.append(hand(some))
         sums.append(part)
         back.append(lax.ppermute(away, "ctx", partner))
@@ -446,12 +454,23 @@
             8 * rows * width,
             [whole(rows, width), others(chunk)],
             (whole(rows, width), whole(8, rows)),
-        )(index_in, after(back[chunk], query, source, gated[chunk]), gate)
+        )(index_in, after(back[chunk], gated[0], gated[1]), gate)
         gated.append(hand(some))
         sums.append(part)
-    attention = None
-    for group in range(groups):
-        attention = attend(group, after(query, some, *gated[:3]), pieces, attention)
+    query_now = after(query, some, *gated[:3])
+    spots = lambda first: pl.BlockSpec((rows, HEAD_WIDTH), lambda g: (0, first + g))
+    attention = call(
+        functools.partial(attention_kernel, ctx),
+        shape((rows, groups * wide), bf16),
+        4 * rows * wide * groups * ctx * rows,
+        8 * rows * wide * groups,
+        grid=(groups,),
+        in_specs=[scalar, scalar, pl.BlockSpec((rows, wide), lambda g: (0, g))]
+        + [spots(0)] * ctx
+        + [spots(groups)] * ctx,
+        out_specs=pl.BlockSpec((rows, wide), lambda g: (0, g)),
+        scratch_shapes=[pltpu.VMEM((ctx * rows, rows), f32)],
+    )(index_in, source, query_now, *pieces, *pieces)
     sums = sum(sums)
     swap = [(i, (i + step) % tps) for step in range(1, tps) for i in range(tps)]
     sums = hand(sums + lax.ppermute(sums, "tp", swap))

time: 82.1 us -> 74.7 us (0.910)
  waiting for transfers between devices: 32.8 us -> 27.9 us
  Pallas kernels: 23.8 us -> 20.3 us
  starting transfers between devices: 23.5 us -> 25.6 us
  local copies, waits for them, and re-layouts: 0.99 us -> 0.03 us
    ppermute x8, waiting for transfers between devices: 2.43 us -> 8.29 us  [hand(): return lax.ppermute(array, 'segment', onward)]
    ppermute x2, waiting for transfers between devices: 10.8 us -> 5.64 us  [on_device(): enter = lax.ppermute(state, 'ctx', further)]
    pallas_call x4 -> x1, Pallas kernels: 9.61 us -> 6.23 us  [on_device(): call(functools.partial(attention_kernel, ctx), shape((rows, groups * wide...]
    ppermute x2, waiting for transfers between devices: 7.43 us -> 4.45 us  [on_device(): got = [lax.ppermute(parcel, 'ctx', partner) for parcel in parcels]]
    ppermute x3, waiting for transfers between devices: 5.67 us -> 3.75 us  [the longest x1 3.74 us: on_device(): lax.ppermute(after(piece, states[0]), 'ctx', swap)]
    ppermute x2, starting transfers between devices: 0.01 us -> 1.85 us  [on_device(): back.append(lax.ppermute(away, 'ctx', partner))]
    ppermute x3, starting transfers between devices: 4.24 us -> 2.98 us  [the longest x1 1.6 us: on_device(): nearby = lax.ppermute(after(key_values, firsts[0]), 'ctx', partner)]
    ppermute x2, starting transfers between devices: 3.54 us -> 4.67 us  [on_device(): got = [lax.ppermute(parcel, 'ctx', partner) for parcel in parcels]]
  transfers between devices with their start and end apart: 18 -> 18, of which waited for: 8 -> 10; matrix products, arithmetic and copies ran while one was open for 0% -> 0% of each run, Pallas kernels for 25% -> 22%
where the time goes in v3:
time: 74.7 us; the launch traced here: 74.5 us
  waiting for transfers between devices  27.9 us (37%)
  starting transfers between devices  25.6 us (34%)
  Pallas kernels  20.3 us (27%)
    ppermute x8, starting transfers between devices, hand(): return lax.ppermute(array, 'segment', onward)  11.8 us
    ppermute x8, waiting for transfers between devices, hand(): return lax.ppermute(array, 'segment', onward)  8.29 us
    pallas_call x1, Pallas kernels, on_device(): call(functools.partial(attention_kernel, ctx), shape((rows, groups * wide...  6.23 us
    ppermute x2, waiting for transfers between devices, on_device(): enter = lax.ppermute(state, 'ctx', further)  5.64 us
    ppermute x2, starting transfers between devices, on_device(): got = [lax.ppermute(parcel, 'ctx', partner) for parcel in parcels]  4.67 us
    ppermute x2, waiting for transfers between devices, on_device(): back.append(lax.ppermute(away, 'ctx', partner))  4.62 us
    ppermute x2, waiting for transfers between devices, on_device(): got = [lax.ppermute(parcel, 'ctx', partner) for parcel in parcels]  4.45 us
    pallas_call x2, Pallas kernels, on_device(): indexed(functools.partial(inner_kernel, chunk), (shape((rows, width), f32...  4.45 us
  transfers between devices with their start and end apart: 18, of which 10 were waited for; matrix products, arithmetic and copies ran while one was open for 0% of the time, Pallas kernels for 22%

profile of v3, /device:TPU:0, one launch (start us, length us, event | category | flops | bytes accessed | tf_op | source)
XLA Modules:
  0.0 74.5 jit_solution(10028142223390177377)
XLA Ops:
  0.7 2.2 %shard_map.122 = (bf16[128,1408]{1,0:T(8,128)(2,1)}, bf16[128,1024]{1,0:T(8,128)(2,1)}, bf16[128,1024]{1,0:T(8,128)(2,1)}, f32[1,64]{1,0:T(1,128)}, f32[1,64]{1,0:T(1,128)}) custom-call(s32[1]{0:T(128)} %bitcast.index_ref, bf16[128,4096]{1,0:T(8,128)(2,1)} %bitcast.15, bf16[128,256]{1,0:T(8,128)(2,1)} %bitcast.24, bf16[64,128]{1,0:T(8,128)(2,1)} %bitcast.31, ...), custom_call_target="tpu_custom_call" | custom-call | bytes 1048576 | tf_op jit(solution)/shard_map/pallas_call | solution.py:346
  2.9 3.1 %collective-permute-start = (bf16[128,1408]{1,0:T(8,128)(2,1)}, bf16[128,1408]{1,0:T(8,128)(2,1)S(1)}, u32[]{:S(2)}, u32[]{:S(2)}) collective-permute-start(bf16[128,1408]{1,0:T(8,128)(2,1)} %get-tuple-element.39), channel_id=1, source_target_pairs={{0,2},{2,0},{4,6},{6,4},{1,3},{3,1},{5,7},{7,5},{8,10},{10,8},{12,... | collective-permute-start | bytes 1081352 | tf_op jit(solution)/shard_map/ppermute | solution.py:371
  6.0 1.5 %collective-permute-start.5 = (bf16[128,1024]{1,0:T(8,128)(2,1)}, bf16[128,1024]{1,0:T(8,128)(2,1)S(1)}, u32[]{:S(2)}, u32[]{:S(2)}) collective-permute-start(bf16[128,1024]{1,0:T(8,128)(2,1)} %get-tuple-element.57), channel_id=1, source_target_pairs={{0,8},{8,16},{16,24},{24,0},{1,9},{9,17},{17,25},{25,1},{2,10},{10... | collective-permute-start | bytes 786440 | tf_op jit(solution)/shard_map/ppermute | solution.py:302
  7.5 1.5 %collective-permute-start.6 = (s32[1]{0:T(128)}, s32[1]{0:T(128)}, u32[]{:S(2)}, u32[]{:S(2)}) collective-permute-start(s32[1]{0:T(128)} %param.21), channel_id=1, source_target_pairs={{0,8},{8,16},{16,24},{24,0},{1,9},{9,17},{17,25},{25,1},{2,10},{10... | collective-permute-start | bytes 20 | tf_op jit(solution)/shard_map/ppermute | solution.py:302
  9.0 5.9 %collective-permute-done.6.source_ref = s32[1]{0:T(128)} collective-permute-done((s32[1]{0:T(128)}, s32[1]{0:T(128)}, u32[]{:S(2)}, u32[]{:S(2)}) %collective-permute-start.6) | collective-permute-done | bytes 36 | tf_op jit(solution)/shard_map/ppermute | solution.py:302
  14.9 1.4 %collective-permute-start.7 = (bf16[128,4096]{1,0:T(8,128)(2,1)}, bf16[128,4096]{1,0:T(8,128)(2,1)S(1)}, u32[]{:S(2)}, u32[]{:S(2)}) collective-permute-start(bf16[128,4096]{1,0:T(8,128)(2,1)} %bitcast.43), channel_id=1, source_target_pairs={{0,8},{8,16},{16,24},{24,0},{1,9},{9,17},{17,25},{25,1},{2,10},{10... | collective-permute-start | bytes 3145736 | tf_op jit(solution)/shard_map/ppermute | solution.py:302
  16.3 1.6 %collective-permute-start.2 = (bf16[128,1024]{1,0:T(8,128)(2,1)}, bf16[128,1024]{1,0:T(8,128)(2,1)S(1)}, u32[]{:S(2)}, u32[]{:S(2)}) collective-permute-start(bf16[128,1024]{1,0:T(8,128)(2,1)} %get-tuple-element.47), channel_id=1, source_target_pairs={{0,2},{2,0},{4,6},{6,4},{1,3},{3,1},{5,7},{7,5},{8,10},{10,8},{12,... | collective-permute-start | bytes 786440 | tf_op jit(solution)/shard_map/ppermute | solution.py:371
  17.9 1.8 %shard_map.123 = (bf16[128,1024]{1,0:T(8,128)(2,1)S(1)}, f32[128,1024]{1,0:T(8,128)S(1)}, f32[1,1024]{1,0:T(1,128)S(1)}, f32[1,1024]{1,0:T(1,128)}) custom-call(s32[1]{0:T(128)} %bitcast.index_ref, bf16[128,4096]{1,0:T(8,128)(2,1)S(1)} %bitcast.16, bf16[128,1408]{1,0:T(8,128)(2,1)S(1)} %collective-permute-done.x2_ref.dt2_ref.b2_ref.maps2_ref.c2_ref, ...), custom_call_target="tpu_custom_call" | custom-call | flops 67108864 | bytes 524288 | tf_op jit(solution)/shard_map/pallas_call | solution.py:385
  19.6 2.6 %collective-permute-start.1 = (bf16[128,1024]{1,0:T(8,128)(2,1)S(1)}, bf16[128,1024]{1,0:T(8,128)(2,1)S(1)}, u32[]{:S(2)}, u32[]{:S(2)}) collective-permute-start(bf16[128,1024]{1,0:T(8,128)(2,1)S(1)} %get-tuple-element.41), channel_id=1, source_target_pairs={{0,4},{2,6},{4,0},{6,2},{1,5},{3,7},{5,1},{7,3},{8,12},{10,14},{12... | collective-permute-start | bytes 786440 | tf_op jit(solution)/shard_map/ppermute | solution.py:393
  22.2 4.4 %collective-permute-done.2.x2_ref = bf16[128,1024]{1,0:T(8,128)(2,1)S(1)} collective-permute-done((bf16[128,1024]{1,0:T(8,128)(2,1)}, bf16[128,1024]{1,0:T(8,128)(2,1)S(1)}, u32[]{:S(2)}, u32[]{:S(2)}) %collective-permute-start.2) | collective-permute-done | bytes 262176 | tf_op jit(solution)/shard_map/ppermute | solution.py:371
  26.7 1.9 %shard_map.127 = (bf16[128,1024]{1,0:T(8,128)(2,1)S(1)}, f32[128,1024]{1,0:T(8,128)S(1)}, f32[1,1024]{1,0:T(1,128)S(1)}, f32[1,1024]{1,0:T(1,128)}) custom-call(s32[1]{0:T(128)} %bitcast.index_ref, bf16[128,4096]{1,0:T(8,128)(2,1)S(1)} %bitcast.17, bf16[128,1024]{1,0:T(8,128)(2,1)S(1)} %collective-permute-done.2.x2_ref, bf16[64,128]{1,0:T(8,128)(2,1)S(1)} %bitcast.33, ...), custom_call_target="tpu_custom_call" | custom-call | flops 67108864 | bytes 524288 | tf_op jit(solution)/shard_map/pallas_call | solution.py:385
  28.5 1.6 %collective-permute-start.4 = (bf16[128,1024]{1,0:T(8,128)(2,1)S(1)}, bf16[128,1024]{1,0:T(8,128)(2,1)S(1)}, u32[]{:S(2)}, u32[]{:S(2)}) collective-permute-start(bf16[128,1024]{1,0:T(8,128)(2,1)S(1)} %get-tuple-element.56), channel_id=1, source_target_pairs={{0,4},{2,6},{4,0},{6,2},{1,5},{3,7},{5,1},{7,3},{8,12},{10,14},{12... | collective-permute-start | bytes 786440 | tf_op jit(solution)/shard_map/ppermute | solution.py:393
  30.2 1.6 %collective-permute-start.8 = (bf16[128,1024]{1,0:T(8,128)(2,1)S(1)}, bf16[128,1024]{1,0:T(8,128)(2,1)S(1)}, u32[]{:S(2)}, u32[]{:S(2)}) collective-permute-start(bf16[128,1024]{1,0:T(8,128)(2,1)S(1)} %collective-permute-done.5.refs_0_.refs_4_), channel_id=1, source_target_pairs={{0,2},{2,0},{4,6},{6,4},{1,3},{3,1},{5,7},{7,5},{8,10},{10,8},{12,... | collective-permute-start | bytes 786440 | tf_op jit(solution)/shard_map/ppermute | solution.py:400
  31.8 2.2 %shard_map.124 = (f32[128,1024]{1,0:T(8,128)S(1)}, f32[128,1024]{1,0:T(8,128)S(1)}, f32[128,1024]{1,0:T(8,128)S(1)}, f32[128,1024]{1,0:T(8,128)S(1)}) custom-call(s32[1]{0:T(128)} %bitcast.index_ref, bf16[128,4096]{1,0:T(8,128)(2,1)S(1)} %bitcast.18, bf16[128,1408]{1,0:T(8,128)(2,1)S(1)} %collective-permute-done.x2_ref.dt2_ref.b2_ref.maps2_ref.c2_ref, ...), custom_call_target="tpu_custom_call" | custom-call | flops 134217728 | bytes 786432 | tf_op jit(solution)/shard_map/pallas_call | solution.py:403
  34.0 2.3 %shard_map.125 = (f32[128,1024]{1,0:T(8,128)S(1)}, f32[128,1024]{1,0:T(8,128)S(1)}, f32[128,1024]{1,0:T(8,128)S(1)}, f32[128,1024]{1,0:T(8,128)S(1)}) custom-call(s32[1]{0:T(128)} %bitcast.index_ref, bf16[128,4096]{1,0:T(8,128)(2,1)S(1)} %bitcast.19, bf16[128,1024]{1,0:T(8,128)(2,1)S(1)} %collective-permute-done.2.x2_ref, bf16[64,128]{1,0:T(8,128)(2,1)S(1)} %bitcast.35, ...), custom_call_target="tpu_custom_call" | custom-call | flops 134217728 | bytes 786432 | tf_op jit(solution)/shard_map/pallas_call | solution.py:403
  36.3 4.3 %collective-permute-done.1.enter_ref = bf16[128,1024]{1,0:T(8,128)(2,1)S(1)} collective-permute-done((bf16[128,1024]{1,0:T(8,128)(2,1)S(1)}, bf16[128,1024]{1,0:T(8,128)(2,1)S(1)}, u32[]{:S(2)}, u32[]{:S(2)}) %collective-permute-start.1) | collective-permute-done | bytes 262176 | tf_op jit(solution)/shard_map/ppermute | solution.py:393
  40.6 0.8 %shard_map.126 = (bf16[128,1024]{1,0:T(8,128)(2,1)S(1)}, f32[8,128]{1,0:T(8,128)S(1)}, bf16[128,1024]{1,0:T(8,128)(2,1)S(1)}) custom-call(s32[1]{0:T(128)} %bitcast.index_ref, bf16[128,1024]{1,0:T(8,128)(2,1)S(1)} %collective-permute-done.1.enter_ref, f32[128,1024]{1,0:T(8,128)S(1)} %get-tuple-element.53.first_ref, ...), custom_call_target="tpu_custom_call" | custom-call | flops 67108864 | bytes 1048576 | tf_op jit(solution)/shard_map/pallas_call | solution.py:431
  41.4 1.5 %collective-permute-start.3 = (bf16[128,1024]{1,0:T(8,128)(2,1)S(1)}, bf16[128,1024]{1,0:T(8,128)(2,1)S(1)}, u32[]{:S(2)}, u32[]{:S(2)}) collective-permute-start(bf16[128,1024]{1,0:T(8,128)(2,1)S(1)} %get-tuple-element.55), channel_id=1, source_target_pairs={{0,8},{8,16},{16,24},{24,0},{1,9},{9,17},{17,25},{25,1},{2,10},{10... | collective-permute-start | bytes 786440 | tf_op jit(solution)/shard_map/ppermute | solution.py:302
  42.8 1.3 %collective-permute-done.4.enter_ref = bf16[128,1024]{1,0:T(8,128)(2,1)S(1)} collective-permute-done((bf16[128,1024]{1,0:T(8,128)(2,1)S(1)}, bf16[128,1024]{1,0:T(8,128)(2,1)S(1)}, u32[]{:S(2)}, u32[]{:S(2)}) %collective-permute-start.4) | collective-permute-done | bytes 262176 | tf_op jit(solution)/shard_map/ppermute | solution.py:393
  44.9 1.8 %collective-permute-start.9 = (bf16[128,1024]{1,0:T(8,128)(2,1)S(1)}, bf16[128,1024]{1,0:T(8,128)(2,1)S(1)}, u32[]{:S(2)}, u32[]{:S(2)}) collective-permute-start(bf16[128,1024]{1,0:T(8,128)(2,1)S(1)} %get-tuple-element.63), channel_id=1, source_target_pairs={{0,8},{8,16},{16,24},{24,0},{1,9},{9,17},{17,25},{25,1},{2,10},{10... | collective-permute-start | bytes 786440 | tf_op jit(solution)/shard_map/ppermute | solution.py:302
  46.7 1.4 %collective-permute-start.16 = (bf16[128,1024]{1,0:T(8,128)(2,1)S(1)}, bf16[128,1024]{1,0:T(8,128)(2,1)S(1)}, u32[]{:S(2)}, u32[]{:S(2)}) collective-permute-start(bf16[128,1024]{1,0:T(8,128)(2,1)S(1)} %collective-permute-done.5.refs_0_.refs_4_), channel_id=1, source_target_pairs={{0,4},{2,6},{4,0},{6,2},{1,5},{3,7},{5,1},{7,3},{8,12},{10,14},{12... | collective-permute-start | bytes 786440 | tf_op jit(solution)/shard_map/ppermute | solution.py:425
  48.0 1.9 %collective-permute-start.12 = (bf16[128,1024]{1,0:T(8,128)(2,1)S(1)}, bf16[128,1024]{1,0:T(8,128)(2,1)S(1)}, u32[]{:S(2)}, u32[]{:S(2)}) collective-permute-start(bf16[128,1024]{1,0:T(8,128)(2,1)S(1)} %get-tuple-element.67), channel_id=1, source_target_pairs={{0,2},{2,0},{4,6},{6,4},{1,3},{3,1},{5,7},{7,5},{8,10},{10,8},{12,... | collective-permute-start | bytes 786440 | tf_op jit(solution)/shard_map/ppermute | solution.py:448
  49.9 1.0 %collective-permute-done.3.refs_0_ = bf16[128,1024]{1,0:T(8,128)(2,1)S(1)} collective-permute-done((bf16[128,1024]{1,0:T(8,128)(2,1)S(1)}, bf16[128,1024]{1,0:T(8,128)(2,1)S(1)}, u32[]{:S(2)}, u32[]{:S(2)}) %collective-permute-start.3) | collective-permute-done | bytes 262176 | tf_op jit(solution)/shard_map/ppermute | solution.py:302
  50.9 2.0 %collective-permute-done.10.raw_ref = bf16[128,1024]{1,0:T(8,128)(2,1)S(1)} collective-permute-done((bf16[128,1024]{1,0:T(8,128)(2,1)S(1)}, bf16[128,1024]{1,0:T(8,128)(2,1)S(1)}, u32[]{:S(2)}, u32[]{:S(2)}) %collective-permute-start.10) | collective-permute-done | bytes 262176 | tf_op jit(solution)/shard_map/ppermute | solution.py:448
  53.0 1.3 %collective-permute-done.9.refs_1_ = bf16[128,1024]{1,0:T(8,128)(2,1)S(1)} collective-permute-done((bf16[128,1024]{1,0:T(8,128)(2,1)S(1)}, bf16[128,1024]{1,0:T(8,128)(2,1)S(1)}, u32[]{:S(2)}, u32[]{:S(2)}) %collective-permute-start.9) | collective-permute-done | bytes 262176 | tf_op jit(solution)/shard_map/ppermute | solution.py:302
  55.3 3.7 %collective-permute-done.16.refs_1_.refs_5_ = bf16[128,1024]{1,0:T(8,128)(2,1)S(1)} collective-permute-done((bf16[128,1024]{1,0:T(8,128)(2,1)S(1)}, bf16[128,1024]{1,0:T(8,128)(2,1)S(1)}, u32[]{:S(2)}, u32[]{:S(2)}) %collective-permute-start.16) | collective-permute-done | bytes 262176 | tf_op jit(solution)/shard_map/ppermute | solution.py:425
  59.0 2.6 %collective-permute-done.12.raw_ref = bf16[128,1024]{1,0:T(8,128)(2,1)S(1)} collective-permute-done((bf16[128,1024]{1,0:T(8,128)(2,1)S(1)}, bf16[128,1024]{1,0:T(8,128)(2,1)S(1)}, u32[]{:S(2)}, u32[]{:S(2)}) %collective-permute-start.12) | collective-permute-done | bytes 262176 | tf_op jit(solution)/shard_map/ppermute | solution.py:448
  62.1 1.9 %collective-permute-start.13 = (bf16[128,1024]{1,0:T(8,128)(2,1)S(1)}, bf16[128,1024]{1,0:T(8,128)(2,1)S(1)}, u32[]{:S(2)}, u32[]{:S(2)}) collective-permute-start(bf16[128,1024]{1,0:T(8,128)(2,1)S(1)} %get-tuple-element.69), channel_id=1, source_target_pairs={{0,8},{8,16},{16,24},{24,0},{1,9},{9,17},{17,25},{25,1},{2,10},{10... | collective-permute-start | bytes 786440 | tf_op jit(solution)/shard_map/ppermute | solution.py:302
  64.0 1.2 %collective-permute-done.14 = f32[8,128]{1,0:T(8,128)S(1)} collective-permute-done((f32[8,128]{1,0:T(8,128)S(1)}, f32[8,128]{1,0:T(8,128)S(1)}, u32[]{:S(2)}, u32[]{:S(2)}) %collective-permute-start.14) | collective-permute-done | bytes 4128 | tf_op jit(solution)/shard_map/ppermute | solution.py:476
  65.2 1.7 %collective-permute-start.15 = (f32[8,128]{1,0:T(8,128)S(1)}, f32[8,128]{1,0:T(8,128)S(1)}, u32[]{:S(2)}, u32[]{:S(2)}) collective-permute-start(f32[8,128]{1,0:T(8,128)S(1)} %add.15), channel_id=1, source_target_pairs={{0,8},{8,16},{16,24},{24,0},{1,9},{9,17},{17,25},{25,1},{2,10},{10... | collective-permute-start | bytes 12296 | tf_op jit(solution)/shard_map/ppermute | solution.py:302
  66.9 6.2 %shard_map.132 = bf16[128,4096]{1,0:T(8,128)(2,1)} custom-call(s32[1]{0:T(128)} %bitcast.index_ref, s32[1]{0:T(128)} %collective-permute-done.6.source_ref, bf16[128,4096]{1,0:T(8,128)(2,1)S(1)} %collective-permute-done.7.q_ref, bf16[128,1024]{1,0:T(8,128)(2,1)S(1)} %collective-permute-done.5.refs_0_.refs_4_, ...), custom_call_target="tpu_custom_call" | custom-call | flops 1073741824 | bytes 4194304 | tf_op jit(solution)/shard_map/pallas_call | solution.py:462
  73.1 1.4 %shard_map.131 = bf16[128,4096]{1,0:T(8,128)(2,1)} custom-call(s32[1]{0:T(128)} %bitcast.index_ref, bf16[128,1024]{1,0:T(8,128)(2,1)S(1)} %collective-permute-done.3.refs_0_, bf16[128,1024]{1,0:T(8,128)(2,1)S(1)} %collective-permute-done.9.refs_1_, bf16[128,1024]{1,0:T(8,128)(2,1)S(1)} %collective-permute-done.11.refs_2_, ...), custom_call_target="tpu_custom_call" | custom-call | flops 524288 | bytes 2097152 | tf_op jit(solution)/shard_map/pallas_call | solution.py:478
  (31 shorter events, 2.3 us)
Async XLA Ops:
  0.6 17.2 %copy-start = (bf16[1,128,4096]{2,1,0:T(8,128)(2,1)S(1)}, bf16[1,128,4096]{2,1,0:T(8,128)(2,1)}, u32[]{:S(2)}) copy-start(bf16[1,128,4096]{2,1,0:T(8,128)(2,1)} %param.11) | copy-start | bytes 3145732
  0.6 17.2 %copy-start.2 = (bf16[1,128,256]{2,1,0:T(8,128)(2,1)S(1)}, bf16[1,128,256]{2,1,0:T(8,128)(2,1)}, u32[]{:S(2)}) copy-start(bf16[1,128,256]{2,1,0:T(8,128)(2,1)} %param.14) | copy-start | bytes 196612
  0.7 17.2 %copy-start.3 = (bf16[1,128,64]{1,2,0:T(8,128)(2,1)S(1)}, bf16[1,128,64]{1,2,0:T(8,128)(2,1)}, u32[]{:S(2)}) copy-start(bf16[1,128,64]{1,2,0:T(8,128)(2,1)} %param.13) | copy-start | bytes 49156
  2.9 12.0 %collective-permute-start = (bf16[128,1408]{1,0:T(8,128)(2,1)}, bf16[128,1408]{1,0:T(8,128)(2,1)S(1)}, u32[]{:S(2)}, u32[]{:S(2)}) collective-permute-start(bf16[128,1408]{1,0:T(8,128)(2,1)} %get-tuple-element.39), channel_id=1, source_target_pairs={{0,2},{2,0},{4,6},{6,4},{1,3},{3,1},{5,7},{7,5},{8,10},{10,8},{12,... | collective-permute-start | bytes 1081352 | tf_op jit(solution)/shard_map/ppermute | solution.py:371
  6.0 8.9 %collective-permute-start.5 = (bf16[128,1024]{1,0:T(8,128)(2,1)}, bf16[128,1024]{1,0:T(8,128)(2,1)S(1)}, u32[]{:S(2)}, u32[]{:S(2)}) collective-permute-start(bf16[128,1024]{1,0:T(8,128)(2,1)} %get-tuple-element.57), channel_id=1, source_target_pairs={{0,8},{8,16},{16,24},{24,0},{1,9},{9,17},{17,25},{25,1},{2,10},{10... | collective-permute-start | bytes 786440 | tf_op jit(solution)/shard_map/ppermute | solution.py:302
  7.5 7.4 %collective-permute-start.6 = (s32[1]{0:T(128)}, s32[1]{0:T(128)}, u32[]{:S(2)}, u32[]{:S(2)}) collective-permute-start(s32[1]{0:T(128)} %param.21), channel_id=1, source_target_pairs={{0,8},{8,16},{16,24},{24,0},{1,9},{9,17},{17,25},{25,1},{2,10},{10... | collective-permute-start | bytes 20 | tf_op jit(solution)/shard_map/ppermute | solution.py:302
  14.9 29.3 %collective-permute-start.7 = (bf16[128,4096]{1,0:T(8,128)(2,1)}, bf16[128,4096]{1,0:T(8,128)(2,1)S(1)}, u32[]{:S(2)}, u32[]{:S(2)}) collective-permute-start(bf16[128,4096]{1,0:T(8,128)(2,1)} %bitcast.43), channel_id=1, source_target_pairs={{0,8},{8,16},{16,24},{24,0},{1,9},{9,17},{17,25},{25,1},{2,10},{10... | collective-permute-start | bytes 3145736 | tf_op jit(solution)/shard_map/ppermute | solution.py:302
  16.3 1.6 %copy-start.5 = (f32[1,64]{1,0:T(1,128)S(1)}, f32[1,64]{1,0:T(1,128)}, u32[]{:S(2)}) copy-start(f32[1,64]{1,0:T(1,128)} %get-tuple-element.40.rate_ref) | copy-start | bytes 772
  16.3 10.4 %collective-permute-start.2 = (bf16[128,1024]{1,0:T(8,128)(2,1)}, bf16[128,1024]{1,0:T(8,128)(2,1)S(1)}, u32[]{:S(2)}, u32[]{:S(2)}) collective-permute-start(bf16[128,1024]{1,0:T(8,128)(2,1)} %get-tuple-element.47), channel_id=1, source_target_pairs={{0,2},{2,0},{4,6},{6,4},{1,3},{3,1},{5,7},{7,5},{8,10},{10,8},{12,... | collective-permute-start | bytes 786440 | tf_op jit(solution)/shard_map/ppermute | solution.py:371
  19.6 21.0 %collective-permute-start.1 = (bf16[128,1024]{1,0:T(8,128)(2,1)S(1)}, bf16[128,1024]{1,0:T(8,128)(2,1)S(1)}, u32[]{:S(2)}, u32[]{:S(2)}) collective-permute-start(bf16[128,1024]{1,0:T(8,128)(2,1)S(1)} %get-tuple-element.41), channel_id=1, source_target_pairs={{0,4},{2,6},{4,0},{6,2},{1,5},{3,7},{5,1},{7,3},{8,12},{10,14},{12... | collective-permute-start | bytes 786440 | tf_op jit(solution)/shard_map/ppermute | solution.py:393
  28.5 15.6 %collective-permute-start.4 = (bf16[128,1024]{1,0:T(8,128)(2,1)S(1)}, bf16[128,1024]{1,0:T(8,128)(2,1)S(1)}, u32[]{:S(2)}, u32[]{:S(2)}) collective-permute-start(bf16[128,1024]{1,0:T(8,128)(2,1)S(1)} %get-tuple-element.56), channel_id=1, source_target_pairs={{0,4},{2,6},{4,0},{6,2},{1,5},{3,7},{5,1},{7,3},{8,12},{10,14},{12... | collective-permute-start | bytes 786440 | tf_op jit(solution)/shard_map/ppermute | solution.py:393
  30.2 1.6 %copy-start.6 = (f32[1,64]{1,0:T(1,128)S(1)}, f32[1,64]{1,0:T(1,128)}, u32[]{:S(2)}) copy-start(f32[1,64]{1,0:T(1,128)} %get-tuple-element.42.skip_ref) | copy-start | bytes 772
  30.2 14.0 %collective-permute-start.8 = (bf16[128,1024]{1,0:T(8,128)(2,1)S(1)}, bf16[128,1024]{1,0:T(8,128)(2,1)S(1)}, u32[]{:S(2)}, u32[]{:S(2)}) collective-permute-start(bf16[128,1024]{1,0:T(8,128)(2,1)S(1)} %collective-permute-done.5.refs_0_.refs_4_), channel_id=1, source_target_pairs={{0,2},{2,0},{4,6},{6,4},{1,3},{3,1},{5,7},{7,5},{8,10},{10,8},{12,... | collective-permute-start | bytes 786440 | tf_op jit(solution)/shard_map/ppermute | solution.py:400
  34.0 6.6 %copy-start.1 = (bf16[1,128,4096]{2,1,0:T(8,128)(2,1)S(1)}, bf16[1,128,4096]{2,1,0:T(8,128)(2,1)}, u32[]{:S(2)}) copy-start(bf16[1,128,4096]{2,1,0:T(8,128)(2,1)} %param.12) | copy-start | bytes 3145732
  41.4 9.6 %collective-permute-start.3 = (bf16[128,1024]{1,0:T(8,128)(2,1)S(1)}, bf16[128,1024]{1,0:T(8,128)(2,1)S(1)}, u32[]{:S(2)}, u32[]{:S(2)}) collective-permute-start(bf16[128,1024]{1,0:T(8,128)(2,1)S(1)} %get-tuple-element.55), channel_id=1, source_target_pairs={{0,8},{8,16},{16,24},{24,0},{1,9},{9,17},{17,25},{25,1},{2,10},{10... | collective-permute-start | bytes 786440 | tf_op jit(solution)/shard_map/ppermute | solution.py:302
  42.8 10.1 %collective-permute-start.10 = (bf16[128,1024]{1,0:T(8,128)(2,1)S(1)}, bf16[128,1024]{1,0:T(8,128)(2,1)S(1)}, u32[]{:S(2)}, u32[]{:S(2)}) collective-permute-start(bf16[128,1024]{1,0:T(8,128)(2,1)S(1)} %get-tuple-element.64), channel_id=1, source_target_pairs={{0,2},{2,0},{4,6},{6,4},{1,3},{3,1},{5,7},{7,5},{8,10},{10,8},{12,... | collective-permute-start | bytes 786440 | tf_op jit(solution)/shard_map/ppermute | solution.py:448
  44.9 9.4 %collective-permute-start.9 = (bf16[128,1024]{1,0:T(8,128)(2,1)S(1)}, bf16[128,1024]{1,0:T(8,128)(2,1)S(1)}, u32[]{:S(2)}, u32[]{:S(2)}) collective-permute-start(bf16[128,1024]{1,0:T(8,128)(2,1)S(1)} %get-tuple-element.63), channel_id=1, source_target_pairs={{0,8},{8,16},{16,24},{24,0},{1,9},{9,17},{17,25},{25,1},{2,10},{10... | collective-permute-start | bytes 786440 | tf_op jit(solution)/shard_map/ppermute | solution.py:302
  46.7 12.4 %collective-permute-start.16 = (bf16[128,1024]{1,0:T(8,128)(2,1)S(1)}, bf16[128,1024]{1,0:T(8,128)(2,1)S(1)}, u32[]{:S(2)}, u32[]{:S(2)}) collective-permute-start(bf16[128,1024]{1,0:T(8,128)(2,1)S(1)} %collective-permute-done.5.refs_0_.refs_4_), channel_id=1, source_target_pairs={{0,4},{2,6},{4,0},{6,2},{1,5},{3,7},{5,1},{7,3},{8,12},{10,14},{12... | collective-permute-start | bytes 786440 | tf_op jit(solution)/shard_map/ppermute | solution.py:425
  48.0 13.6 %collective-permute-start.12 = (bf16[128,1024]{1,0:T(8,128)(2,1)S(1)}, bf16[128,1024]{1,0:T(8,128)(2,1)S(1)}, u32[]{:S(2)}, u32[]{:S(2)}) collective-permute-start(bf16[128,1024]{1,0:T(8,128)(2,1)S(1)} %get-tuple-element.67), channel_id=1, source_target_pairs={{0,2},{2,0},{4,6},{6,4},{1,3},{3,1},{5,7},{7,5},{8,10},{10,8},{12,... | collective-permute-start | bytes 786440 | tf_op jit(solution)/shard_map/ppermute | solution.py:448
  54.7 12.2 %collective-permute-start.11 = (bf16[128,1024]{1,0:T(8,128)(2,1)S(1)}, bf16[128,1024]{1,0:T(8,128)(2,1)S(1)}, u32[]{:S(2)}, u32[]{:S(2)}) collective-permute-start(bf16[128,1024]{1,0:T(8,128)(2,1)S(1)} %get-tuple-element.66), channel_id=1, source_target_pairs={{0,8},{8,16},{16,24},{24,0},{1,9},{9,17},{17,25},{25,1},{2,10},{10... | collective-permute-start | bytes 786440 | tf_op jit(solution)/shard_map/ppermute | solution.py:302
  59.0 7.8 %collective-permute-start.17 = (bf16[128,1024]{1,0:T(8,128)(2,1)S(1)}, bf16[128,1024]{1,0:T(8,128)(2,1)S(1)}, u32[]{:S(2)}, u32[]{:S(2)}) collective-permute-start(bf16[128,1024]{1,0:T(8,128)(2,1)S(1)} %collective-permute-done.16.refs_1_.refs_5_), channel_id=1, source_target_pairs={{0,2},{2,0},{4,6},{6,4},{1,3},{3,1},{5,7},{7,5},{8,10},{10,8},{12,... | collective-permute-start | bytes 786440 | tf_op jit(solution)/shard_map/ppermute | solution.py:428
  62.1 11.1 %collective-permute-start.13 = (bf16[128,1024]{1,0:T(8,128)(2,1)S(1)}, bf16[128,1024]{1,0:T(8,128)(2,1)S(1)}, u32[]{:S(2)}, u32[]{:S(2)}) collective-permute-start(bf16[128,1024]{1,0:T(8,128)(2,1)S(1)} %get-tuple-element.69), channel_id=1, source_target_pairs={{0,8},{8,16},{16,24},{24,0},{1,9},{9,17},{17,25},{25,1},{2,10},{10... | collective-permute-start | bytes 786440 | tf_op jit(solution)/shard_map/ppermute | solution.py:302
  64.0 1.2 %collective-permute-start.14 = (f32[8,128]{1,0:T(8,128)S(1)}, f32[8,128]{1,0:T(8,128)S(1)}, u32[]{:S(2)}, u32[]{:S(2)}) collective-permute-start(f32[8,128]{1,0:T(8,128)S(1)} %add_add_fusion), channel_id=1, source_target_pairs={{0,1},{1,0},{2,3},{3,2},{4,5},{5,4},{6,7},{7,6},{8,9},{9,8},{10,11... | collective-permute-start | bytes 12296 | tf_op jit(solution)/shard_map/ppermute | solution.py:476
  65.2 7.9 %copy-start.4 = (f32[4096]{0:T(1024)S(1)}, f32[4096]{0:T(1024)}, u32[]{:S(2)}) copy-start(f32[4096]{0:T(1024)} %param.17) | copy-start | bytes 49156
  65.2 7.9 %collective-permute-start.15 = (f32[8,128]{1,0:T(8,128)S(1)}, f32[8,128]{1,0:T(8,128)S(1)}, u32[]{:S(2)}, u32[]{:S(2)}) collective-permute-start(f32[8,128]{1,0:T(8,128)S(1)} %add.15), channel_id=1, source_target_pairs={{0,8},{8,16},{16,24},{24,0},{1,9},{9,17},{17,25},{25,1},{2,10},{10... | collective-permute-start | bytes 12296 | tf_op jit(solution)/shard_map/ppermute | solution.py:302

commit v4 on v3

--- a/solution.py
+++ b/solution.py
@@ -15,7 +15,7 @@
 HP = 64
 GROUP = QUERY_HEADS // KEY_VALUE_HEADS
 CHUNKS = 2
-VMEM = 40 * 1024 * 1024
+VMEM = 16 * 1024 * 1024
 PARCEL_VMEM = 60 * 1024 * 1024
 HIGH = lax.Precision.HIGHEST
 
@@ -26,11 +26,11 @@
     )
 
 
-def call(kernel, out_shape, flops, nbytes, **kw):
+def call(kernel, out_shape, flops, nbytes, vmem=VMEM, **kw):
     return pl.pallas_call(
         kernel,
         out_shape=out_shape,
-        compiler_params=pltpu.CompilerParams(vmem_limit_bytes=VMEM),
+        compiler_params=pltpu.CompilerParams(vmem_limit_bytes=vmem),
         cost_estimate=pl.CostEstimate(flops=flops, bytes_accessed=nbytes, transcendentals=0),
         **kw,
     )
@@ -49,10 +49,31 @@
     return jnp.where(lane < HP, first, second)
 
 
+def load_kernel(index_ref, x_ref, maps_ref, dt_ref, x_out, maps_out, dt_out, sem):
+    side, half = x_out.shape[1], dt_out.shape[0]
+    mine = index_ref[0] % 2
+    moves = [
+        (x_ref.at[:, pl.ds(pl.multiple_of(mine * side, 128), side)], x_out),
+        (maps_ref, maps_out),
+        (dt_ref.at[pl.ds(pl.multiple_of(mine * half, half), half), :], dt_out),
+    ]
+    copy_all(moves, sem)
+
+
 def spread(row, first, width):
     return jnp.concatenate(
         [pair_columns(row, first // 2 + pair, 1) for pair in range(width // (2 * HP))], axis=1
     )
+
+
+def copy_all(moves, sem):
+    copies = [
+        pltpu.make_async_copy(src, dst, sem.at[number]) for number, (src, dst) in enumerate(moves)
+    ]
+    for copy in copies:
+        copy.start()
+    for copy in copies:
+        copy.wait()
 
 
 def parcel_kernel(
@@ -82,13 +103,7 @@
     moves.append((value_ref, packed_ref.at[:, pl.ds(kv, kv)]))
     moves.append((rate_ref, rate_out))
     moves.append((skip_ref, skip_out))
-    copies = [
-        pltpu.make_async_copy(src, dst, sem.at[number]) for number, (src, dst) in enumerate(moves)
-    ]
-    for copy in copies:
-        copy.start()
-    for copy in copies:
-        copy.wait()
+    copy_all(moves, sem)
 
 
 def own_heads(ref, early, chunk, count):
@@ -236,42 +251,53 @@
         )
 
 
-def attention_kernel(ctx, index_ref, source_ref, q_ref, *refs):
-    out_ref, bias_ref = refs[-2:]
-    key = jnp.concatenate([ref[...] for ref in refs[:ctx]], axis=0)
-    value = jnp.concatenate([ref[...] for ref in refs[ctx : 2 * ctx]], axis=0)
+def attention_kernel(offsets, index_ref, source_ref, q_ref, *refs):
+    blocks = len(offsets)
+    key_refs, value_refs, rest = refs[:blocks], refs[blocks : 2 * blocks], refs[2 * blocks :]
+    bias_ref = rest[-1]
     rows = q_ref.shape[0]
-    keys = key.shape[0]
     index = index_ref[0]
     source = source_ref[0]
-    place = lax.broadcasted_iota(jnp.int32, (keys, rows), 0)
-    away = place // rows
-    owner = jnp.zeros_like(place)
-    step, bit = ctx // 2, 1
-    while step >= 1:
-        owner = owner + jnp.where((away & bit) != 0, step, 0)
-        step, bit = step // 2, bit * 2
-    key_pos = (owner ^ index) * rows + place % rows
-    query_pos = index * rows + lax.broadcasted_iota(jnp.int32, (keys, rows), 1)
-    bias_ref[...] = jnp.where((key_pos <= query_pos) | (key_pos < source), 0.0, -jnp.inf)
+    query_pos = index * rows + lax.broadcasted_iota(jnp.int32, (rows, rows), 1)
+    for block, offset in enumerate(offsets):
+        key_pos = (index ^ offset) * rows + lax.broadcasted_iota(jnp.int32, (rows, rows), 0)
+        bias_ref[block * rows : block * rows + rows, :] = jnp.where(
+            (key_pos <= query_pos) | (key_pos < source), 0.0, -jnp.inf
+        )
     factor = math.log2(math.e) / math.sqrt(HEAD_WIDTH)
     span = lambda head: slice(head * HEAD_WIDTH, (head + 1) * HEAD_WIDTH)
+    part = lambda head: slice(head * rows, (head + 1) * rows)
     query = jnp.concatenate([q_ref[:, span(head)] for head in range(GROUP)], axis=0)
+    key = jnp.concatenate([ref[...] for ref in key_refs], axis=0)
+    value = jnp.concatenate([ref[...] for ref in value_refs], axis=0)
     value = jnp.transpose(value.astype(jnp.float32)).astype(jnp.bfloat16)
     scores = dot(key, query, ((1,), (1,)))
-    weights, totals = [], []
+    last = len(rest) == 4
+    weights, totals, tops, olds = [], [], [], []
     for head in range(GROUP):
-        kept = scores[:, head * rows : (head + 1) * rows] + bias_ref[...]
+        kept = scores[:, part(head)] + bias_ref[...]
         top = jnp.max(kept, axis=0, keepdims=True)
+        if last:
+            before = rest[1][0, 0:1, part(head)]
+            top = jnp.maximum(top, before)
         weight = jnp.exp2((kept - top) * factor)
-        totals.append(jnp.sum(weight, axis=0, keepdims=True))
+        total = jnp.sum(weight, axis=0, keepdims=True)
+        if last:
+            old = jnp.exp2((before - top) * factor)
+            total = total + rest[1][0, 1:2, part(head)] * old
+            olds.append(old)
+        tops.append(top)
+        totals.append(total)
         weights.append(weight.astype(jnp.bfloat16))
     mixed = dot(value, jnp.concatenate(weights, axis=1), ((1,), (0,)))
-    mixed = mixed / jnp.concatenate(totals, axis=1)
+    if not last:
+        rest[0][0] = mixed
+        rest[1][0, 0:1, :] = jnp.concatenate(tops, axis=1)
+        rest[1][0, 1:2, :] = jnp.concatenate(totals, axis=1)
+        return
+    mixed = (mixed + rest[0][0] * jnp.concatenate(olds, axis=1)) / jnp.concatenate(totals, axis=1)
     for head in range(GROUP):
-        out_ref[:, span(head)] = jnp.transpose(
-            mixed[:, head * rows : (head + 1) * rows]
-        ).astype(jnp.bfloat16)
+        rest[2][:, span(head)] = jnp.transpose(mixed[:, part(head)]).astype(jnp.bfloat16)
 
 
 def on_device(
@@ -317,7 +343,6 @@
 
     whole = lambda *dims: pl.BlockSpec(dims, lambda i, s: (0,) * len(dims))
     fixed = lambda dims, *at: pl.BlockSpec(dims, lambda i, s: at)
-    mine = lambda dims: pl.BlockSpec(dims, lambda i, s: (s[0] % 2,) + (0,) * (len(dims) - 1))
     columns = lambda chunk: pl.BlockSpec(
         (rows, width), lambda i, s: (0, (s[0] % 2) * CHUNKS + chunk)
     )
@@ -371,11 +396,21 @@
     got = [lax.ppermute(parcel, "ctx", partner) for parcel in parcels]
     key_values = hand(packed)
     source = hand(source_len)
-    query = hand(after(queries[0], key_values, got[0], source))
+    x_own, maps_own, dt_own = indexed(
+        load_kernel,
+        (shape((rows, side), bf16), shape((rows, 2 * NST), bf16), shape((half, rows), bf16)),
+        0,
+        4 * rows * side,
+        [hbm] * 3,
+        (whole(rows, side), whole(rows, 2 * NST), whole(half, rows)),
+        [pltpu.SemaphoreType.DMA((3,))],
+        VMEM,
+    )(after(index_in, parcels[0]), x, maps, dt)
+    query = hand(after(queries[0], key_values, got[0], source, x_own))
     pairs = [
-        columns,
+        lambda chunk: fixed((rows, width), 0, chunk),
         lambda chunk: whole(rows, width),
-        lambda chunk: mine((half, rows)),
+        lambda chunk: whole(half, rows),
         lambda chunk: fixed((half, rows), 0, (width + 2 * NST) // rows),
         lambda chunk: whole(1, heads),
     ]
@@ -389,7 +424,7 @@
             4 * rows * width,
             places(chunk) + [whole(rows, NST), fixed((rows, NST), 0, width // NST)],
             (whole(NST, width),) * 2 + (whole(1, width),) * 2,
-        )(index_in, x, got[chunk], dt, got[0], rate, maps, got[0])
+        )(index_in, x_own, got[chunk], dt_own, got[0], rate, maps_own, got[0])
         enter = lax.ppermute(state, "ctx", further)
         for _ in range(ctx // 2 - 2):
             enter = jnp.where(index < 2, 0.0, enter.astype(f32))
@@ -412,20 +447,44 @@
                     fixed((rows, 2 * NST), 0, width // (2 * NST)),
                 ],
                 (whole(rows, width),) * 4,
-            )(index_in, x, got[chunk], dt, got[0], rate, skip, maps, got[0])
+            )(index_in, x_own, got[chunk], dt_own, got[0], rate, skip, maps_own, got[0])
         )
     scalar = pl.BlockSpec(memory_space=pltpu.SMEM)
 
 
-    pieces = [key_values]
+    pieces, offsets = [key_values], [0]
     step = ctx // 2
     while step > 1:
         swap = [(i, i ^ step) for i in range(ctx)]
         pieces = pieces + [
             lax.ppermute(after(piece, states[0]), "ctx", swap) for piece in pieces
         ]
+        offsets = offsets + [offset ^ step for offset in offsets]
         step //= 2
-    pieces = pieces + [nearby] + [lax.ppermute(piece, "ctx", partner) for piece in pieces[1:]]
+    far_pieces = pieces[1:] + [lax.ppermute(piece, "ctx", partner) for piece in pieces[1:]]
+    far_offsets = offsets[1:] + [offset ^ 1 for offset in offsets[1:]]
+
+    def attend(query, pieces, offsets, more, out_shape, out_specs):
+        spots = lambda first: pl.BlockSpec((rows, HEAD_WIDTH), lambda g: (0, first + g))
+        return call(
+            functools.partial(attention_kernel, offsets),
+            out_shape,
+            4 * rows * wide * groups * len(offsets) * rows,
+            8 * rows * wide * groups,
+            VMEM + 8 * len(offsets) * rows * GROUP * rows,
+            grid=(groups,),
+            in_specs=[scalar, scalar, pl.BlockSpec((rows, wide), lambda g: (0, g))]
+            + [spots(0)] * len(offsets)
+            + [spots(groups)] * len(offsets)
+            + (halves if more else []),
+            out_specs=out_specs,
+            scratch_shapes=[pltpu.VMEM((len(offsets) * rows, rows), f32)],
+        )(index_in, source, query, *pieces, *pieces, *more)
+
+    halves = [
+        pl.BlockSpec((1, HEAD_WIDTH, GROUP * rows), lambda g: (g, 0, 0)),
+        pl.BlockSpec((1, 2, GROUP * rows), lambda g: (g, 0, 0)),
+    ]
     gated, sums, back = [], [], []
     for chunk in range(CHUNKS):
         some, part, away = indexed(
@@ -442,10 +501,21 @@
                 columns(chunk),
             ],
             (whole(rows, width), whole(8, rows), whole(rows, width)),
-        )(index_in, after(states[chunk], query, nearby) if chunk else after(states[chunk], *[part for parts in inner for part in parts]), firsts[chunk], leads[chunk], *inner[chunk], maps, got[0], gate)
+        )(index_in, after(states[chunk], query, nearby) if chunk else after(states[chunk], *[part for parts in inner for part in parts]), firsts[chunk], leads[chunk], *inner[chunk], maps_own, got[0], gate)
         gated.append(hand(some))
         sums.append(part)
         back.append(lax.ppermute(away, "ctx", partner))
+    near = attend(
+        after(query, some),
+        [key_values, nearby],
+        [0, 1],
+        (),
+        (
+            shape((groups, HEAD_WIDTH, GROUP * rows), f32),
+            shape((groups, 2, GROUP * rows), f32),
+        ),
+        tuple(halves),
+    )
     for chunk in range(CHUNKS):
         some, part = indexed(
             gate_kernel,
@@ -454,23 +524,17 @@
             8 * rows * width,
             [whole(rows, width), others(chunk)],
             (whole(rows, width), whole(8, rows)),
-        )(index_in, after(back[chunk], gated[0], gated[1]), gate)
+        )(index_in, after(back[chunk], gated[0], gated[1], *near), gate)
         gated.append(hand(some))
         sums.append(part)
-    query_now = after(query, some, *gated[:3])
-    spots = lambda first: pl.BlockSpec((rows, HEAD_WIDTH), lambda g: (0, first + g))
-    attention = call(
-        functools.partial(attention_kernel, ctx),
+    attention = attend(
+        after(query, some, *gated[:3]),
+        far_pieces,
+        far_offsets,
+        near,
         shape((rows, groups * wide), bf16),
-        4 * rows * wide * groups * ctx * rows,
-        8 * rows * wide * groups,
-        grid=(groups,),
-        in_specs=[scalar, scalar, pl.BlockSpec((rows, wide), lambda g: (0, g))]
-        + [spots(0)] * ctx
-        + [spots(groups)] * ctx,
-        out_specs=pl.BlockSpec((rows, wide), lambda g: (0, g)),
-        scratch_shapes=[pltpu.VMEM((ctx * rows, rows), f32)],
-    )(index_in, source, query_now, *pieces, *pieces)
+        pl.BlockSpec((rows, wide), lambda g: (0, g)),
+    )
     sums = sum(sums)
     swap = [(i, (i + step) % tps) for step in range(1, tps) for i in range(tps)]
     sums = hand(sums + lax.ppermute(sums, "tp", swap))

time: 74.7 us -> 73.5 us (0.984)
  waiting for transfers between devices: 27.9 us -> 21.7 us
  local copies, waits for them, and re-layouts: 0.03 us -> 2.23 us
  Pallas kernels: 20.3 us -> 22.5 us
    ppermute x8, waiting for transfers between devices: 8.29 us -> 4.99 us  [hand(): return lax.ppermute(array, 'segment', onward)]
    ppermute x2, waiting for transfers between devices: 4.62 us -> 2.35 us  [on_device(): back.append(lax.ppermute(away, 'ctx', partner))]
    pallas_call x1 -> x3, Pallas kernels: 6.23 us -> 8.45 us  [the longest x2 8.3 us: attend(): call(functools.partial(attention_kernel, offsets), out_shape, 4 * rows *...]
    unnamed x14, local copies, waits for them, and re-layouts: 0.03 us -> 2.23 us
    ppermute x2, waiting for transfers between devices: 4.45 us -> 2.63 us  [on_device(): got = [lax.ppermute(parcel, 'ctx', partner) for parcel in parcels]]
    ppermute x2, starting transfers between devices: 4.24 us -> 5.42 us  [on_device(): enter = lax.ppermute(state, 'ctx', further)]
    ppermute x2, waiting for transfers between devices: 5.64 us -> 6.49 us  [on_device(): enter = lax.ppermute(state, 'ctx', further)]
  transfers between devices with their start and end apart: 18 -> 18, of which waited for: 10 -> 8; matrix products, arithmetic and copies ran while one was open for 0% -> 0% of each run, Pallas kernels for 22% -> 26%
where the time goes in v4:
time: 73.5 us; the launch traced here: 73.2 us
  starting transfers between devices  26.1 us (36%)
  Pallas kernels  22.5 us (31%)
  waiting for transfers between devices  21.7 us (30%)
  local copies, waits for them, and re-layouts  2.23 us (3%)
    ppermute x8, starting transfers between devices, hand(): return lax.ppermute(array, 'segment', onward)  11.5 us
    pallas_call x2, Pallas kernels, attend(): call(functools.partial(attention_kernel, offsets), out_shape, 4 * rows *...  8.3 us
    ppermute x2, waiting for transfers between devices, on_device(): enter = lax.ppermute(state, 'ctx', further)  6.49 us
    ppermute x2, starting transfers between devices, on_device(): enter = lax.ppermute(state, 'ctx', further)  5.42 us
    ppermute x8, waiting for transfers between devices, hand(): return lax.ppermute(array, 'segment', onward)  4.99 us
    ppermute x2, starting transfers between devices, on_device(): got = [lax.ppermute(parcel, 'ctx', partner) for parcel in parcels]  4.67 us
    pallas_call x2, Pallas kernels, on_device(): indexed(functools.partial(inner_kernel, chunk), (shape((rows, width), f32...  4.43 us
    ppermute x1, waiting for transfers between devices, on_device(): lax.ppermute(after(piece, states[0]), 'ctx', swap)  4.08 us
  transfers between devices with their start and end apart: 18, of which 8 were waited for; matrix products, arithmetic and copies ran while one was open for 0% of the time, Pallas kernels for 26%

profile of v4, /device:TPU:0, one launch (start us, length us, event | category | flops | bytes accessed | tf_op | source)
XLA Modules:
  0.0 73.2 jit_solution(5640480608066741009)
XLA Ops:
  0.6 2.2 %shard_map.122 = (bf16[128,1408]{1,0:T(8,128)(2,1)}, bf16[128,1024]{1,0:T(8,128)(2,1)}, bf16[128,1024]{1,0:T(8,128)(2,1)}, f32[1,64]{1,0:T(1,128)}, f32[1,64]{1,0:T(1,128)}) custom-call(s32[1]{0:T(128)} %bitcast.index_ref, bf16[128,4096]{1,0:T(8,128)(2,1)} %bitcast.19, bf16[128,256]{1,0:T(8,128)(2,1)} %bitcast.21, bf16[64,128]{1,0:T(8,128)(2,1)} %bitcast.23, ...), custom_call_target="tpu_custom_call" | custom-call | bytes 1048576 | tf_op jit(solution)/shard_map/pallas_call | solution.py:371
  2.9 3.1 %collective-permute-start = (bf16[128,1408]{1,0:T(8,128)(2,1)}, bf16[128,1408]{1,0:T(8,128)(2,1)S(1)}, u32[]{:S(2)}, u32[]{:S(2)}) collective-permute-start(bf16[128,1408]{1,0:T(8,128)(2,1)} %get-tuple-element.46), channel_id=1, source_target_pairs={{0,2},{2,0},{4,6},{6,4},{1,3},{3,1},{5,7},{7,5},{8,10},{10,8},{12,... | collective-permute-start | bytes 1081352 | tf_op jit(solution)/shard_map/ppermute | solution.py:396
  6.0 1.5 %collective-permute-start.5 = (bf16[128,1024]{1,0:T(8,128)(2,1)}, bf16[128,1024]{1,0:T(8,128)(2,1)S(1)}, u32[]{:S(2)}, u32[]{:S(2)}) collective-permute-start(bf16[128,1024]{1,0:T(8,128)(2,1)} %get-tuple-element.68), channel_id=1, source_target_pairs={{0,8},{8,16},{16,24},{24,0},{1,9},{9,17},{17,25},{25,1},{2,10},{10... | collective-permute-start | bytes 786440 | tf_op jit(solution)/shard_map/ppermute | solution.py:328
  7.5 1.5 %collective-permute-start.6 = (s32[1]{0:T(128)}, s32[1]{0:T(128)}, u32[]{:S(2)}, u32[]{:S(2)}) collective-permute-start(s32[1]{0:T(128)} %param.21), channel_id=1, source_target_pairs={{0,8},{8,16},{16,24},{24,0},{1,9},{9,17},{17,25},{25,1},{2,10},{10... | collective-permute-start | bytes 20 | tf_op jit(solution)/shard_map/ppermute | solution.py:328
  9.0 0.8 %copy-done.2 = bf16[1,128,256]{2,1,0:T(8,128)(2,1)S(1)} copy-done((bf16[1,128,256]{2,1,0:T(8,128)(2,1)S(1)}, bf16[1,128,256]{2,1,0:T(8,128)(2,1)}, u32[]{:S(2)}) %copy-start.2) | copy-done | bytes 65560
  10.7 4.2 %collective-permute-done.6.source_ref = s32[1]{0:T(128)} collective-permute-done((s32[1]{0:T(128)}, s32[1]{0:T(128)}, u32[]{:S(2)}, u32[]{:S(2)}) %collective-permute-start.6) | collective-permute-done | bytes 36 | tf_op jit(solution)/shard_map/ppermute | solution.py:328
  14.9 1.4 %collective-permute-start.7 = (bf16[128,4096]{1,0:T(8,128)(2,1)}, bf16[128,4096]{1,0:T(8,128)(2,1)S(1)}, u32[]{:S(2)}, u32[]{:S(2)}) collective-permute-start(bf16[128,4096]{1,0:T(8,128)(2,1)} %bitcast.32), channel_id=1, source_target_pairs={{0,8},{8,16},{16,24},{24,0},{1,9},{9,17},{17,25},{25,1},{2,10},{10... | collective-permute-start | bytes 3145736 | tf_op jit(solution)/shard_map/ppermute | solution.py:328
  16.2 1.6 %collective-permute-start.2 = (bf16[128,1024]{1,0:T(8,128)(2,1)}, bf16[128,1024]{1,0:T(8,128)(2,1)S(1)}, u32[]{:S(2)}, u32[]{:S(2)}) collective-permute-start(bf16[128,1024]{1,0:T(8,128)(2,1)} %get-tuple-element.58), channel_id=1, source_target_pairs={{0,2},{2,0},{4,6},{6,4},{1,3},{3,1},{5,7},{7,5},{8,10},{10,8},{12,... | collective-permute-start | bytes 786440 | tf_op jit(solution)/shard_map/ppermute | solution.py:396
  18.5 1.8 %shard_map.124 = (bf16[128,1024]{1,0:T(8,128)(2,1)S(1)}, f32[128,1024]{1,0:T(8,128)S(1)}, f32[1,1024]{1,0:T(1,128)S(1)}, f32[1,1024]{1,0:T(1,128)}) custom-call(s32[1]{0:T(128)} %bitcast.index_ref, bf16[128,2048]{1,0:T(8,128)(2,1)S(1)} %get-tuple-element.48.x_ref, bf16[128,1408]{1,0:T(8,128)(2,1)S(1)} %collective-permute-done.x2_ref.dt2_ref.b2_ref.maps2_ref.c2_ref, ...), custom_call_target="tpu_custom_call" | custom-call | flops 67108864 | bytes 524288 | tf_op jit(solution)/shard_map/pallas_call | solution.py:420
  20.2 2.6 %collective-permute-start.1 = (bf16[128,1024]{1,0:T(8,128)(2,1)S(1)}, bf16[128,1024]{1,0:T(8,128)(2,1)S(1)}, u32[]{:S(2)}, u32[]{:S(2)}) collective-permute-start(bf16[128,1024]{1,0:T(8,128)(2,1)S(1)} %get-tuple-element.52), channel_id=1, source_target_pairs={{0,4},{2,6},{4,0},{6,2},{1,5},{3,7},{5,1},{7,3},{8,12},{10,14},{12... | collective-permute-start | bytes 786440 | tf_op jit(solution)/shard_map/ppermute | solution.py:428
  22.8 2.6 %collective-permute-done.2.x2_ref = bf16[128,1024]{1,0:T(8,128)(2,1)S(1)} collective-permute-done((bf16[128,1024]{1,0:T(8,128)(2,1)}, bf16[128,1024]{1,0:T(8,128)(2,1)S(1)}, u32[]{:S(2)}, u32[]{:S(2)}) %collective-permute-start.2) | collective-permute-done | bytes 262176 | tf_op jit(solution)/shard_map/ppermute | solution.py:396
  25.4 1.9 %shard_map.128 = (bf16[128,1024]{1,0:T(8,128)(2,1)S(1)}, f32[128,1024]{1,0:T(8,128)S(1)}, f32[1,1024]{1,0:T(1,128)S(1)}, f32[1,1024]{1,0:T(1,128)}) custom-call(s32[1]{0:T(128)} %bitcast.index_ref, bf16[128,2048]{1,0:T(8,128)(2,1)S(1)} %get-tuple-element.48.x_ref, bf16[128,1024]{1,0:T(8,128)(2,1)S(1)} %collective-permute-done.2.x2_ref, ...), custom_call_target="tpu_custom_call" | custom-call | flops 67108864 | bytes 524288 | tf_op jit(solution)/shard_map/pallas_call | solution.py:420
  27.3 2.8 %collective-permute-start.4 = (bf16[128,1024]{1,0:T(8,128)(2,1)S(1)}, bf16[128,1024]{1,0:T(8,128)(2,1)S(1)}, u32[]{:S(2)}, u32[]{:S(2)}) collective-permute-start(bf16[128,1024]{1,0:T(8,128)(2,1)S(1)} %get-tuple-element.67), channel_id=1, source_target_pairs={{0,4},{2,6},{4,0},{6,2},{1,5},{3,7},{5,1},{7,3},{8,12},{10,14},{12... | collective-permute-start | bytes 786440 | tf_op jit(solution)/shard_map/ppermute | solution.py:428
  30.2 1.4 %collective-permute-start.8 = (bf16[128,1024]{1,0:T(8,128)(2,1)S(1)}, bf16[128,1024]{1,0:T(8,128)(2,1)S(1)}, u32[]{:S(2)}, u32[]{:S(2)}) collective-permute-start(bf16[128,1024]{1,0:T(8,128)(2,1)S(1)} %collective-permute-done.5.refs_0_.refs_2_), channel_id=1, source_target_pairs={{0,2},{2,0},{4,6},{6,4},{1,3},{3,1},{5,7},{7,5},{8,10},{10,8},{12,... | collective-permute-start | bytes 786440 | tf_op jit(solution)/shard_map/ppermute | solution.py:435
  31.6 2.2 %shard_map.125 = (f32[128,1024]{1,0:T(8,128)S(1)}, f32[128,1024]{1,0:T(8,128)S(1)}, f32[128,1024]{1,0:T(8,128)S(1)}, f32[128,1024]{1,0:T(8,128)S(1)}) custom-call(s32[1]{0:T(128)} %bitcast.index_ref, bf16[128,2048]{1,0:T(8,128)(2,1)S(1)} %get-tuple-element.48.x_ref, bf16[128,1408]{1,0:T(8,128)(2,1)S(1)} %collective-permute-done.x2_ref.dt2_ref.b2_ref.maps2_ref.c2_ref, ...), custom_call_target="tpu_custom_call" | custom-call | flops 134217728 | bytes 786432 | tf_op jit(solution)/shard_map/pallas_call | solution.py:438
  33.7 2.3 %shard_map.126 = (f32[128,1024]{1,0:T(8,128)S(1)}, f32[128,1024]{1,0:T(8,128)S(1)}, f32[128,1024]{1,0:T(8,128)S(1)}, f32[128,1024]{1,0:T(8,128)S(1)}) custom-call(s32[1]{0:T(128)} %bitcast.index_ref, bf16[128,2048]{1,0:T(8,128)(2,1)S(1)} %get-tuple-element.48.x_ref, bf16[128,1024]{1,0:T(8,128)(2,1)S(1)} %collective-permute-done.2.x2_ref, ...), custom_call_target="tpu_custom_call" | custom-call | flops 134217728 | bytes 786432 | tf_op jit(solution)/shard_map/pallas_call | solution.py:438
  36.0 4.8 %collective-permute-done.1.enter_ref = bf16[128,1024]{1,0:T(8,128)(2,1)S(1)} collective-permute-done((bf16[128,1024]{1,0:T(8,128)(2,1)S(1)}, bf16[128,1024]{1,0:T(8,128)(2,1)S(1)}, u32[]{:S(2)}, u32[]{:S(2)}) %collective-permute-start.1) | collective-permute-done | bytes 262176 | tf_op jit(solution)/shard_map/ppermute | solution.py:428
  41.6 1.5 %collective-permute-start.3 = (bf16[128,1024]{1,0:T(8,128)(2,1)S(1)}, bf16[128,1024]{1,0:T(8,128)(2,1)S(1)}, u32[]{:S(2)}, u32[]{:S(2)}) collective-permute-start(bf16[128,1024]{1,0:T(8,128)(2,1)S(1)} %get-tuple-element.66), channel_id=1, source_target_pairs={{0,8},{8,16},{16,24},{24,0},{1,9},{9,17},{17,25},{25,1},{2,10},{10... | collective-permute-start | bytes 786440 | tf_op jit(solution)/shard_map/ppermute | solution.py:328
  43.1 1.6 %collective-permute-done.4.enter_ref = bf16[128,1024]{1,0:T(8,128)(2,1)S(1)} collective-permute-done((bf16[128,1024]{1,0:T(8,128)(2,1)S(1)}, bf16[128,1024]{1,0:T(8,128)(2,1)S(1)}, u32[]{:S(2)}, u32[]{:S(2)}) %collective-permute-start.4) | collective-permute-done | bytes 262176 | tf_op jit(solution)/shard_map/ppermute | solution.py:428
  44.7 0.8 %shard_map.129 = (bf16[128,1024]{1,0:T(8,128)(2,1)S(1)}, f32[8,128]{1,0:T(8,128)S(1)}, bf16[128,1024]{1,0:T(8,128)(2,1)S(1)}) custom-call(s32[1]{0:T(128)} %bitcast.index_ref, bf16[128,1024]{1,0:T(8,128)(2,1)S(1)} %collective-permute-done.4.enter_ref, f32[128,1024]{1,0:T(8,128)S(1)} %get-tuple-element.72.first_ref, ...), custom_call_target="tpu_custom_call" | custom-call | flops 67108864 | bytes 1048576 | tf_op jit(solution)/shard_map/pallas_call | solution.py:490
  45.5 1.5 %collective-permute-start.9 = (bf16[128,1024]{1,0:T(8,128)(2,1)S(1)}, bf16[128,1024]{1,0:T(8,128)(2,1)S(1)}, u32[]{:S(2)}, u32[]{:S(2)}) collective-permute-start(bf16[128,1024]{1,0:T(8,128)(2,1)S(1)} %get-tuple-element.74), channel_id=1, source_target_pairs={{0,8},{8,16},{16,24},{24,0},{1,9},{9,17},{17,25},{25,1},{2,10},{10... | collective-permute-start | bytes 786440 | tf_op jit(solution)/shard_map/ppermute | solution.py:328
  47.0 1.5 %collective-permute-start.16 = (bf16[128,1024]{1,0:T(8,128)(2,1)S(1)}, bf16[128,1024]{1,0:T(8,128)(2,1)S(1)}, u32[]{:S(2)}, u32[]{:S(2)}) collective-permute-start(bf16[128,1024]{1,0:T(8,128)(2,1)S(1)} %collective-permute-done.5.refs_0_.refs_2_), channel_id=1, source_target_pairs={{0,4},{2,6},{4,0},{6,2},{1,5},{3,7},{5,1},{7,3},{8,12},{10,14},{12... | collective-permute-start | bytes 786440 | tf_op jit(solution)/shard_map/ppermute | solution.py:460
  48.5 1.5 %collective-permute-start.12 = (bf16[128,1024]{1,0:T(8,128)(2,1)S(1)}, bf16[128,1024]{1,0:T(8,128)(2,1)S(1)}, u32[]{:S(2)}, u32[]{:S(2)}) collective-permute-start(bf16[128,1024]{1,0:T(8,128)(2,1)S(1)} %get-tuple-element.81), channel_id=1, source_target_pairs={{0,2},{2,0},{4,6},{6,4},{1,3},{3,1},{5,7},{7,5},{8,10},{10,8},{12,... | collective-permute-start | bytes 786440 | tf_op jit(solution)/shard_map/ppermute | solution.py:507
  50.1 3.6 %shard_map.130 = (f32[4,128,1024]{2,1,0:T(8,128)S(1)}, f32[4,2,1024]{2,1,0:T(2,128)S(1)}) custom-call(s32[1]{0:T(128)} %bitcast.index_ref, s32[1]{0:T(128)} %collective-permute-done.6.source_ref, bf16[128,4096]{1,0:T(8,128)(2,1)S(1)} %collective-permute-done.7.q_ref, bf16[128,1024]{1,0:T(8,128)(2,1)S(1)} %collective-permute-done.5.refs_0_.refs_2_, ...), custom_call_target="tpu_custom_call" | custom-call | flops 536870912 | bytes 4194304 | tf_op jit(solution)/shard_map/pallas_call | solution.py:469
  53.7 0.8 %collective-permute-done.9.refs_1_ = bf16[128,1024]{1,0:T(8,128)(2,1)S(1)} collective-permute-done((bf16[128,1024]{1,0:T(8,128)(2,1)S(1)}, bf16[128,1024]{1,0:T(8,128)(2,1)S(1)}, u32[]{:S(2)}, u32[]{:S(2)}) %collective-permute-start.9) | collective-permute-done | bytes 262176 | tf_op jit(solution)/shard_map/ppermute | solution.py:328
  55.6 4.1 %collective-permute-done.16.refs_0_.refs_2_ = bf16[128,1024]{1,0:T(8,128)(2,1)S(1)} collective-permute-done((bf16[128,1024]{1,0:T(8,128)(2,1)S(1)}, bf16[128,1024]{1,0:T(8,128)(2,1)S(1)}, u32[]{:S(2)}, u32[]{:S(2)}) %collective-permute-start.16) | collective-permute-done | bytes 262176 | tf_op jit(solution)/shard_map/ppermute | solution.py:460
  59.7 2.4 %collective-permute-done.12.raw_ref = bf16[128,1024]{1,0:T(8,128)(2,1)S(1)} collective-permute-done((bf16[128,1024]{1,0:T(8,128)(2,1)S(1)}, bf16[128,1024]{1,0:T(8,128)(2,1)S(1)}, u32[]{:S(2)}, u32[]{:S(2)}) %collective-permute-start.12) | collective-permute-done | bytes 262176 | tf_op jit(solution)/shard_map/ppermute | solution.py:507
  62.5 1.6 %collective-permute-start.13 = (bf16[128,1024]{1,0:T(8,128)(2,1)S(1)}, bf16[128,1024]{1,0:T(8,128)(2,1)S(1)}, u32[]{:S(2)}, u32[]{:S(2)}) collective-permute-start(bf16[128,1024]{1,0:T(8,128)(2,1)S(1)} %get-tuple-element.83), channel_id=1, source_target_pairs={{0,8},{8,16},{16,24},{24,0},{1,9},{9,17},{17,25},{25,1},{2,10},{10... | collective-permute-start | bytes 786440 | tf_op jit(solution)/shard_map/ppermute | solution.py:328
  64.0 1.2 %collective-permute-done.14 = f32[8,128]{1,0:T(8,128)S(1)} collective-permute-done((f32[8,128]{1,0:T(8,128)S(1)}, f32[8,128]{1,0:T(8,128)S(1)}, u32[]{:S(2)}, u32[]{:S(2)}) %collective-permute-start.14) | collective-permute-done | bytes 4128 | tf_op jit(solution)/shard_map/ppermute | solution.py:540
  65.2 1.9 %collective-permute-start.15 = (f32[8,128]{1,0:T(8,128)S(1)}, f32[8,128]{1,0:T(8,128)S(1)}, u32[]{:S(2)}, u32[]{:S(2)}) collective-permute-start(f32[8,128]{1,0:T(8,128)S(1)} %add.15), channel_id=1, source_target_pairs={{0,8},{8,16},{16,24},{24,0},{1,9},{9,17},{17,25},{25,1},{2,10},{10... | collective-permute-start | bytes 12296 | tf_op jit(solution)/shard_map/ppermute | solution.py:328
  67.1 4.7 %shard_map.134 = bf16[128,4096]{1,0:T(8,128)(2,1)} custom-call(s32[1]{0:T(128)} %bitcast.index_ref, s32[1]{0:T(128)} %collective-permute-done.6.source_ref, bf16[128,4096]{1,0:T(8,128)(2,1)S(1)} %collective-permute-done.7.q_ref, bf16[128,1024]{1,0:T(8,128)(2,1)S(1)} %collective-permute-done.16.refs_0_.refs_2_, ...), custom_call_target="tpu_custom_call" | custom-call | flops 536870912 | bytes 4194304 | tf_op jit(solution)/shard_map/pallas_call | solution.py:469
  71.8 1.4 %shard_map.133 = bf16[128,4096]{1,0:T(8,128)(2,1)} custom-call(s32[1]{0:T(128)} %bitcast.index_ref, bf16[128,1024]{1,0:T(8,128)(2,1)S(1)} %collective-permute-done.3.refs_0_, bf16[128,1024]{1,0:T(8,128)(2,1)S(1)} %collective-permute-done.9.refs_1_, bf16[128,1024]{1,0:T(8,128)(2,1)S(1)} %collective-permute-done.11.refs_2_, ...), custom_call_target="tpu_custom_call" | custom-call | flops 524288 | bytes 2097152 | tf_op jit(solution)/shard_map/pallas_call | solution.py:542
  (33 shorter events, 3.9 us)
Async XLA Ops:
  0.6 8.3 %copy-start.1 = (bf16[1,128,4096]{2,1,0:T(8,128)(2,1)S(1)}, bf16[1,128,4096]{2,1,0:T(8,128)(2,1)}, u32[]{:S(2)}) copy-start(bf16[1,128,4096]{2,1,0:T(8,128)(2,1)} %param.11) | copy-start | bytes 3145732
  2.9 12.0 %collective-permute-start = (bf16[128,1408]{1,0:T(8,128)(2,1)}, bf16[128,1408]{1,0:T(8,128)(2,1)S(1)}, u32[]{:S(2)}, u32[]{:S(2)}) collective-permute-start(bf16[128,1408]{1,0:T(8,128)(2,1)} %get-tuple-element.46), channel_id=1, source_target_pairs={{0,2},{2,0},{4,6},{6,4},{1,3},{3,1},{5,7},{7,5},{8,10},{10,8},{12,... | collective-permute-start | bytes 1081352 | tf_op jit(solution)/shard_map/ppermute | solution.py:396
  6.0 25.6 %copy-start.6 = (f32[1,64]{1,0:T(1,128)S(1)}, f32[1,64]{1,0:T(1,128)}, u32[]{:S(2)}) copy-start(f32[1,64]{1,0:T(1,128)} %get-tuple-element.53.skip_ref) | copy-start | bytes 772
  6.0 8.9 %collective-permute-start.5 = (bf16[128,1024]{1,0:T(8,128)(2,1)}, bf16[128,1024]{1,0:T(8,128)(2,1)S(1)}, u32[]{:S(2)}, u32[]{:S(2)}) collective-permute-start(bf16[128,1024]{1,0:T(8,128)(2,1)} %get-tuple-element.68), channel_id=1, source_target_pairs={{0,8},{8,16},{16,24},{24,0},{1,9},{9,17},{17,25},{25,1},{2,10},{10... | collective-permute-start | bytes 786440 | tf_op jit(solution)/shard_map/ppermute | solution.py:328
  7.5 7.4 %collective-permute-start.6 = (s32[1]{0:T(128)}, s32[1]{0:T(128)}, u32[]{:S(2)}, u32[]{:S(2)}) collective-permute-start(s32[1]{0:T(128)} %param.21), channel_id=1, source_target_pairs={{0,8},{8,16},{16,24},{24,0},{1,9},{9,17},{17,25},{25,1},{2,10},{10... | collective-permute-start | bytes 20 | tf_op jit(solution)/shard_map/ppermute | solution.py:328
  9.0 0.8 %copy-start.2 = (bf16[1,128,256]{2,1,0:T(8,128)(2,1)S(1)}, bf16[1,128,256]{2,1,0:T(8,128)(2,1)}, u32[]{:S(2)}) copy-start(bf16[1,128,256]{2,1,0:T(8,128)(2,1)} %param.14) | copy-start | bytes 196612
  9.8 0.7 copy-start.3
  14.9 29.8 %collective-permute-start.7 = (bf16[128,4096]{1,0:T(8,128)(2,1)}, bf16[128,4096]{1,0:T(8,128)(2,1)S(1)}, u32[]{:S(2)}, u32[]{:S(2)}) collective-permute-start(bf16[128,4096]{1,0:T(8,128)(2,1)} %bitcast.32), channel_id=1, source_target_pairs={{0,8},{8,16},{16,24},{24,0},{1,9},{9,17},{17,25},{25,1},{2,10},{10... | collective-permute-start | bytes 3145736 | tf_op jit(solution)/shard_map/ppermute | solution.py:328
  16.2 9.2 %collective-permute-start.2 = (bf16[128,1024]{1,0:T(8,128)(2,1)}, bf16[128,1024]{1,0:T(8,128)(2,1)S(1)}, u32[]{:S(2)}, u32[]{:S(2)}) collective-permute-start(bf16[128,1024]{1,0:T(8,128)(2,1)} %get-tuple-element.58), channel_id=1, source_target_pairs={{0,2},{2,0},{4,6},{6,4},{1,3},{3,1},{5,7},{7,5},{8,10},{10,8},{12,... | collective-permute-start | bytes 786440 | tf_op jit(solution)/shard_map/ppermute | solution.py:396
  17.8 0.7 copy-start.5
  20.2 20.6 %copy-start = (bf16[1,128,4096]{2,1,0:T(8,128)(2,1)S(1)}, bf16[1,128,4096]{2,1,0:T(8,128)(2,1)}, u32[]{:S(2)}) copy-start(bf16[1,128,4096]{2,1,0:T(8,128)(2,1)} %param.12) | copy-start | bytes 3145732
  20.2 20.6 %collective-permute-start.1 = (bf16[128,1024]{1,0:T(8,128)(2,1)S(1)}, bf16[128,1024]{1,0:T(8,128)(2,1)S(1)}, u32[]{:S(2)}, u32[]{:S(2)}) collective-permute-start(bf16[128,1024]{1,0:T(8,128)(2,1)S(1)} %get-tuple-element.52), channel_id=1, source_target_pairs={{0,4},{2,6},{4,0},{6,2},{1,5},{3,7},{5,1},{7,3},{8,12},{10,14},{12... | collective-permute-start | bytes 786440 | tf_op jit(solution)/shard_map/ppermute | solution.py:428
  27.3 17.4 %collective-permute-start.4 = (bf16[128,1024]{1,0:T(8,128)(2,1)S(1)}, bf16[128,1024]{1,0:T(8,128)(2,1)S(1)}, u32[]{:S(2)}, u32[]{:S(2)}) collective-permute-start(bf16[128,1024]{1,0:T(8,128)(2,1)S(1)} %get-tuple-element.67), channel_id=1, source_target_pairs={{0,4},{2,6},{4,0},{6,2},{1,5},{3,7},{5,1},{7,3},{8,12},{10,14},{12... | collective-permute-start | bytes 786440 | tf_op jit(solution)/shard_map/ppermute | solution.py:428
  30.2 14.6 %collective-permute-start.8 = (bf16[128,1024]{1,0:T(8,128)(2,1)S(1)}, bf16[128,1024]{1,0:T(8,128)(2,1)S(1)}, u32[]{:S(2)}, u32[]{:S(2)}) collective-permute-start(bf16[128,1024]{1,0:T(8,128)(2,1)S(1)} %collective-permute-done.5.refs_0_.refs_2_), channel_id=1, source_target_pairs={{0,2},{2,0},{4,6},{6,4},{1,3},{3,1},{5,7},{7,5},{8,10},{10,8},{12,... | collective-permute-start | bytes 786440 | tf_op jit(solution)/shard_map/ppermute | solution.py:435
  41.6 12.1 %collective-permute-start.3 = (bf16[128,1024]{1,0:T(8,128)(2,1)S(1)}, bf16[128,1024]{1,0:T(8,128)(2,1)S(1)}, u32[]{:S(2)}, u32[]{:S(2)}) collective-permute-start(bf16[128,1024]{1,0:T(8,128)(2,1)S(1)} %get-tuple-element.66), channel_id=1, source_target_pairs={{0,8},{8,16},{16,24},{24,0},{1,9},{9,17},{17,25},{25,1},{2,10},{10... | collective-permute-start | bytes 786440 | tf_op jit(solution)/shard_map/ppermute | solution.py:328
  43.1 10.7 %collective-permute-start.10 = (bf16[128,1024]{1,0:T(8,128)(2,1)S(1)}, bf16[128,1024]{1,0:T(8,128)(2,1)S(1)}, u32[]{:S(2)}, u32[]{:S(2)}) collective-permute-start(bf16[128,1024]{1,0:T(8,128)(2,1)S(1)} %get-tuple-element.75), channel_id=1, source_target_pairs={{0,2},{2,0},{4,6},{6,4},{1,3},{3,1},{5,7},{7,5},{8,10},{10,8},{12,... | collective-permute-start | bytes 786440 | tf_op jit(solution)/shard_map/ppermute | solution.py:507
  45.5 9.0 %collective-permute-start.9 = (bf16[128,1024]{1,0:T(8,128)(2,1)S(1)}, bf16[128,1024]{1,0:T(8,128)(2,1)S(1)}, u32[]{:S(2)}, u32[]{:S(2)}) collective-permute-start(bf16[128,1024]{1,0:T(8,128)(2,1)S(1)} %get-tuple-element.74), channel_id=1, source_target_pairs={{0,8},{8,16},{16,24},{24,0},{1,9},{9,17},{17,25},{25,1},{2,10},{10... | collective-permute-start | bytes 786440 | tf_op jit(solution)/shard_map/ppermute | solution.py:328
  47.0 12.7 %collective-permute-start.16 = (bf16[128,1024]{1,0:T(8,128)(2,1)S(1)}, bf16[128,1024]{1,0:T(8,128)(2,1)S(1)}, u32[]{:S(2)}, u32[]{:S(2)}) collective-permute-start(bf16[128,1024]{1,0:T(8,128)(2,1)S(1)} %collective-permute-done.5.refs_0_.refs_2_), channel_id=1, source_target_pairs={{0,4},{2,6},{4,0},{6,2},{1,5},{3,7},{5,1},{7,3},{8,12},{10,14},{12... | collective-permute-start | bytes 786440 | tf_op jit(solution)/shard_map/ppermute | solution.py:460
  48.5 13.5 %collective-permute-start.12 = (bf16[128,1024]{1,0:T(8,128)(2,1)S(1)}, bf16[128,1024]{1,0:T(8,128)(2,1)S(1)}, u32[]{:S(2)}, u32[]{:S(2)}) collective-permute-start(bf16[128,1024]{1,0:T(8,128)(2,1)S(1)} %get-tuple-element.81), channel_id=1, source_target_pairs={{0,2},{2,0},{4,6},{6,4},{1,3},{3,1},{5,7},{7,5},{8,10},{10,8},{12,... | collective-permute-start | bytes 786440 | tf_op jit(solution)/shard_map/ppermute | solution.py:507
  54.9 12.2 %collective-permute-start.11 = (bf16[128,1024]{1,0:T(8,128)(2,1)S(1)}, bf16[128,1024]{1,0:T(8,128)(2,1)S(1)}, u32[]{:S(2)}, u32[]{:S(2)}) collective-permute-start(bf16[128,1024]{1,0:T(8,128)(2,1)S(1)} %get-tuple-element.80), channel_id=1, source_target_pairs={{0,8},{8,16},{16,24},{24,0},{1,9},{9,17},{17,25},{25,1},{2,10},{10... | collective-permute-start | bytes 786440 | tf_op jit(solution)/shard_map/ppermute | solution.py:328
  59.7 7.4 %collective-permute-start.17 = (bf16[128,1024]{1,0:T(8,128)(2,1)S(1)}, bf16[128,1024]{1,0:T(8,128)(2,1)S(1)}, u32[]{:S(2)}, u32[]{:S(2)}) collective-permute-start(bf16[128,1024]{1,0:T(8,128)(2,1)S(1)} %collective-permute-done.16.refs_0_.refs_2_), channel_id=1, source_target_pairs={{0,2},{2,0},{4,6},{6,4},{1,3},{3,1},{5,7},{7,5},{8,10},{10,8},{12,... | collective-permute-start | bytes 786440 | tf_op jit(solution)/shard_map/ppermute | solution.py:464
  62.5 9.3 %collective-permute-start.13 = (bf16[128,1024]{1,0:T(8,128)(2,1)S(1)}, bf16[128,1024]{1,0:T(8,128)(2,1)S(1)}, u32[]{:S(2)}, u32[]{:S(2)}) collective-permute-start(bf16[128,1024]{1,0:T(8,128)(2,1)S(1)} %get-tuple-element.83), channel_id=1, source_target_pairs={{0,8},{8,16},{16,24},{24,0},{1,9},{9,17},{17,25},{25,1},{2,10},{10... | collective-permute-start | bytes 786440 | tf_op jit(solution)/shard_map/ppermute | solution.py:328
  64.0 1.2 %collective-permute-start.14 = (f32[8,128]{1,0:T(8,128)S(1)}, f32[8,128]{1,0:T(8,128)S(1)}, u32[]{:S(2)}, u32[]{:S(2)}) collective-permute-start(f32[8,128]{1,0:T(8,128)S(1)} %add_add_fusion), channel_id=1, source_target_pairs={{0,1},{1,0},{2,3},{3,2},{4,5},{5,4},{6,7},{7,6},{8,9},{9,8},{10,11... | collective-permute-start | bytes 12296 | tf_op jit(solution)/shard_map/ppermute | solution.py:540
  65.2 6.6 %copy-start.4 = (f32[4096]{0:T(1024)S(1)}, f32[4096]{0:T(1024)}, u32[]{:S(2)}) copy-start(f32[4096]{0:T(1024)} %param.17) | copy-start | bytes 49156
  65.2 6.6 %collective-permute-start.15 = (f32[8,128]{1,0:T(8,128)S(1)}, f32[8,128]{1,0:T(8,128)S(1)}, u32[]{:S(2)}, u32[]{:S(2)}) collective-permute-start(f32[8,128]{1,0:T(8,128)S(1)} %add.15), channel_id=1, source_target_pairs={{0,8},{8,16},{16,24},{24,0},{1,9},{9,17},{17,25},{25,1},{2,10},{10... | collective-permute-start | bytes 12296 | tf_op jit(solution)/shard_map/ppermute | solution.py:328

commit v5 on v4

--- a/solution.py
+++ b/solution.py
@@ -393,7 +393,7 @@
         decay_rate.reshape(1, heads),
         skip_gain.reshape(1, heads),
     )
-    got = [lax.ppermute(parcel, "ctx", partner) for parcel in parcels]
+    got = [lax.ppermute(parcels[0], "ctx", partner)]
     key_values = hand(packed)
     source = hand(source_len)
     x_own, maps_own, dt_own = indexed(
@@ -431,8 +431,9 @@
             enter = lax.ppermute((state.astype(f32) + both * enter).astype(wire), "ctx", further)
         states.append(enter)
         firsts.append(first)
+        if chunk + 1 < CHUNKS:
+            got.append(lax.ppermute(after(parcels[chunk + 1], first), "ctx", partner))
         leads.append(lead)
-    nearby = lax.ppermute(after(key_values, firsts[0]), "ctx", partner)
     for chunk in range(CHUNKS):
         inner.append(
             indexed(
@@ -452,6 +453,7 @@
     scalar = pl.BlockSpec(memory_space=pltpu.SMEM)
 
 
+    nearby = lax.ppermute(after(key_values, inner[0][0]), "ctx", partner)
     pieces, offsets = [key_values], [0]
     step = ctx // 2
     while step > 1:

time: 73.5 us -> 72.2 us (0.982)
  starting transfers between devices: 26.1 us -> 24.6 us
    ppermute x3, waiting for transfers between devices: 2.63 us -> 8.28 us  [the longest x1 8.28 us: on_device(): got.append(lax.ppermute(after(parcels[chunk + 1], first), 'ctx', partner))]
    ppermute x2, starting transfers between devices: 1.54 us -> 4.92 us  [on_device(): back.append(lax.ppermute(away, 'ctx', partner))]
    ppermute x1, waiting for transfers between devices: 4.08 us -> 1.41 us  [on_device(): lax.ppermute(after(piece, states[0]), 'ctx', swap)]
    ppermute x2, starting transfers between devices: 5.42 us -> 2.88 us  [on_device(): enter = lax.ppermute(state, 'ctx', further)]
    ppermute x2, waiting for transfers between devices: 6.49 us -> 4.32 us  [on_device(): enter = lax.ppermute(state, 'ctx', further)]
    ppermute x1, starting transfers between devices: 1.55 us -> 0.04 us  [on_device(): lax.ppermute(after(piece, states[0]), 'ctx', swap)]
    ppermute x3, starting transfers between devices: 6.06 us -> 5.18 us  [the longest x1 3.09 us: on_device(): got = [lax.ppermute(parcels[0], 'ctx', partner)]]
    unnamed x14 -> x16, local copies, waits for them, and re-layouts: 2.23 us -> 2.17 us
where the time goes in v5:
time: 72.2 us; the launch traced here: 71.9 us
  starting transfers between devices  24.6 us (34%)
  Pallas kernels  22.3 us (31%)
  waiting for transfers between devices  22.1 us (31%)
  local copies, waits for them, and re-layouts  2.17 us (3%)
  between operations  0.75 us (1%)
    ppermute x8, starting transfers between devices, hand(): return lax.ppermute(array, 'segment', onward)  11.2 us
    ppermute x1, waiting for transfers between devices, on_device(): got.append(lax.ppermute(after(parcels[chunk + 1], first), 'ctx', partner))  8.28 us
    pallas_call x2, Pallas kernels, attend(): call(functools.partial(attention_kernel, offsets), out_shape, 4 * rows *...  8.16 us
    ppermute x2, starting transfers between devices, on_device(): back.append(lax.ppermute(away, 'ctx', partner))  4.92 us
    ppermute x8, waiting for transfers between devices, hand(): return lax.ppermute(array, 'segment', onward)  4.58 us
    pallas_call x2, Pallas kernels, on_device(): indexed(functools.partial(inner_kernel, chunk), (shape((rows, width), f32...  4.43 us
    ppermute x2, waiting for transfers between devices, on_device(): enter = lax.ppermute(state, 'ctx', further)  4.32 us
    pallas_call x2, Pallas kernels, on_device(): indexed(functools.partial(state_kernel, chunk), (shape((NST, width), wire...  3.62 us
  transfers between devices with their start and end apart: 18, of which 8 were waited for; matrix products, arithmetic and copies ran while one was open for 0% of the time, Pallas kernels for 26%

profile of v5, /device:TPU:0, one launch (start us, length us, event | category | flops | bytes accessed | tf_op | source)
XLA Modules:
  0.0 71.9 jit_solution(1036488810195540547)
XLA Ops:
  0.6 2.2 %shard_map.122 = (bf16[128,1408]{1,0:T(8,128)(2,1)}, bf16[128,1024]{1,0:T(8,128)(2,1)}, bf16[128,1024]{1,0:T(8,128)(2,1)}, f32[1,64]{1,0:T(1,128)}, f32[1,64]{1,0:T(1,128)}) custom-call(s32[1]{0:T(128)} %bitcast.index_ref, bf16[128,4096]{1,0:T(8,128)(2,1)} %bitcast.19, bf16[128,256]{1,0:T(8,128)(2,1)} %bitcast.21, bf16[64,128]{1,0:T(8,128)(2,1)} %bitcast.23, ...), custom_call_target="tpu_custom_call" | custom-call | bytes 1048576 | tf_op jit(solution)/shard_map/pallas_call | solution.py:371
  2.9 3.1 %collective-permute-start = (bf16[128,1408]{1,0:T(8,128)(2,1)}, bf16[128,1408]{1,0:T(8,128)(2,1)S(1)}, u32[]{:S(2)}, u32[]{:S(2)}) collective-permute-start(bf16[128,1408]{1,0:T(8,128)(2,1)} %get-tuple-element.47), channel_id=1, source_target_pairs={{0,2},{2,0},{4,6},{6,4},{1,3},{3,1},{5,7},{7,5},{8,10},{10,8},{12,... | collective-permute-start | bytes 1081352 | tf_op jit(solution)/shard_map/ppermute | solution.py:396
  6.0 1.5 %collective-permute-start.5 = (bf16[128,1024]{1,0:T(8,128)(2,1)}, bf16[128,1024]{1,0:T(8,128)(2,1)S(1)}, u32[]{:S(2)}, u32[]{:S(2)}) collective-permute-start(bf16[128,1024]{1,0:T(8,128)(2,1)} %get-tuple-element.70), channel_id=1, source_target_pairs={{0,8},{8,16},{16,24},{24,0},{1,9},{9,17},{17,25},{25,1},{2,10},{10... | collective-permute-start | bytes 786440 | tf_op jit(solution)/shard_map/ppermute | solution.py:328
  7.5 1.5 %collective-permute-start.6 = (s32[1]{0:T(128)}, s32[1]{0:T(128)}, u32[]{:S(2)}, u32[]{:S(2)}) collective-permute-start(s32[1]{0:T(128)} %param.21), channel_id=1, source_target_pairs={{0,8},{8,16},{16,24},{24,0},{1,9},{9,17},{17,25},{25,1},{2,10},{10... | collective-permute-start | bytes 20 | tf_op jit(solution)/shard_map/ppermute | solution.py:328
  9.0 0.8 %copy-done.2 = bf16[1,128,256]{2,1,0:T(8,128)(2,1)S(1)} copy-done((bf16[1,128,256]{2,1,0:T(8,128)(2,1)S(1)}, bf16[1,128,256]{2,1,0:T(8,128)(2,1)}, u32[]{:S(2)}) %copy-start.2) | copy-done | bytes 65560
  9.8 0.7 copy-done.3
  10.7 4.2 %collective-permute-done.6.source_ref = s32[1]{0:T(128)} collective-permute-done((s32[1]{0:T(128)}, s32[1]{0:T(128)}, u32[]{:S(2)}, u32[]{:S(2)}) %collective-permute-start.6) | collective-permute-done | bytes 36 | tf_op jit(solution)/shard_map/ppermute | solution.py:328
  14.9 1.4 %collective-permute-start.7 = (bf16[128,4096]{1,0:T(8,128)(2,1)}, bf16[128,4096]{1,0:T(8,128)(2,1)S(1)}, u32[]{:S(2)}, u32[]{:S(2)}) collective-permute-start(bf16[128,4096]{1,0:T(8,128)(2,1)} %bitcast.32), channel_id=1, source_target_pairs={{0,8},{8,16},{16,24},{24,0},{1,9},{9,17},{17,25},{25,1},{2,10},{10... | collective-permute-start | bytes 3145736 | tf_op jit(solution)/shard_map/ppermute | solution.py:328
  16.3 0.6 copy-done.5
  16.8 1.8 %shard_map.124 = (bf16[128,1024]{1,0:T(8,128)(2,1)S(1)}, f32[128,1024]{1,0:T(8,128)S(1)}, f32[1,1024]{1,0:T(1,128)S(1)}, f32[1,1024]{1,0:T(1,128)}) custom-call(s32[1]{0:T(128)} %bitcast.index_ref, bf16[128,2048]{1,0:T(8,128)(2,1)S(1)} %get-tuple-element.49.x_ref, bf16[128,1408]{1,0:T(8,128)(2,1)S(1)} %collective-permute-done.x2_ref.dt2_ref.b2_ref.maps2_ref.c2_ref, ...), custom_call_target="tpu_custom_call" | custom-call | flops 67108864 | bytes 524288 | tf_op jit(solution)/shard_map/pallas_call | solution.py:420
  18.6 1.6 %collective-permute-start.2 = (bf16[128,1024]{1,0:T(8,128)(2,1)S(1)}, bf16[128,1024]{1,0:T(8,128)(2,1)S(1)}, u32[]{:S(2)}, u32[]{:S(2)}) collective-permute-start(bf16[128,1024]{1,0:T(8,128)(2,1)S(1)} %copy-done.7), channel_id=1, source_target_pairs={{0,2},{2,0},{4,6},{6,4},{1,3},{3,1},{5,7},{7,5},{8,10},{10,8},{12,... | collective-permute-start | bytes 786440 | tf_op jit(solution)/shard_map/ppermute | solution.py:435
  20.2 2.6 %collective-permute-start.1 = (bf16[128,1024]{1,0:T(8,128)(2,1)S(1)}, bf16[128,1024]{1,0:T(8,128)(2,1)S(1)}, u32[]{:S(2)}, u32[]{:S(2)}) collective-permute-start(bf16[128,1024]{1,0:T(8,128)(2,1)S(1)} %get-tuple-element.53), channel_id=1, source_target_pairs={{0,4},{2,6},{4,0},{6,2},{1,5},{3,7},{5,1},{7,3},{8,12},{10,14},{12... | collective-permute-start | bytes 786440 | tf_op jit(solution)/shard_map/ppermute | solution.py:428
  22.8 2.2 %shard_map.125 = (f32[128,1024]{1,0:T(8,128)S(1)}, f32[128,1024]{1,0:T(8,128)S(1)}, f32[128,1024]{1,0:T(8,128)S(1)}, f32[128,1024]{1,0:T(8,128)S(1)}) custom-call(s32[1]{0:T(128)} %bitcast.index_ref, bf16[128,2048]{1,0:T(8,128)(2,1)S(1)} %get-tuple-element.49.x_ref, bf16[128,1408]{1,0:T(8,128)(2,1)S(1)} %collective-permute-done.x2_ref.dt2_ref.b2_ref.maps2_ref.c2_ref, ...), custom_call_target="tpu_custom_call" | custom-call | flops 134217728 | bytes 786432 | tf_op jit(solution)/shard_map/pallas_call | solution.py:439
  24.9 0.5 collective-permute-start.8
  25.5 8.3 %collective-permute-done.2.x2_ref = bf16[128,1024]{1,0:T(8,128)(2,1)S(1)} collective-permute-done((bf16[128,1024]{1,0:T(8,128)(2,1)S(1)}, bf16[128,1024]{1,0:T(8,128)(2,1)S(1)}, u32[]{:S(2)}, u32[]{:S(2)}) %collective-permute-start.2) | collective-permute-done | bytes 262176 | tf_op jit(solution)/shard_map/ppermute | solution.py:435
  33.7 1.9 %shard_map.128 = (bf16[128,1024]{1,0:T(8,128)(2,1)S(1)}, f32[128,1024]{1,0:T(8,128)S(1)}, f32[1,1024]{1,0:T(1,128)S(1)}, f32[1,1024]{1,0:T(1,128)}) custom-call(s32[1]{0:T(128)} %bitcast.index_ref, bf16[128,2048]{1,0:T(8,128)(2,1)S(1)} %get-tuple-element.49.x_ref, bf16[128,1024]{1,0:T(8,128)(2,1)S(1)} %collective-permute-done.2.x2_ref, ...), custom_call_target="tpu_custom_call" | custom-call | flops 67108864 | bytes 524288 | tf_op jit(solution)/shard_map/pallas_call | solution.py:420
  35.9 2.3 %shard_map.126 = (f32[128,1024]{1,0:T(8,128)S(1)}, f32[128,1024]{1,0:T(8,128)S(1)}, f32[128,1024]{1,0:T(8,128)S(1)}, f32[128,1024]{1,0:T(8,128)S(1)}) custom-call(s32[1]{0:T(128)} %bitcast.index_ref, bf16[128,2048]{1,0:T(8,128)(2,1)S(1)} %get-tuple-element.49.x_ref, bf16[128,1024]{1,0:T(8,128)(2,1)S(1)} %collective-permute-done.2.x2_ref, ...), custom_call_target="tpu_custom_call" | custom-call | flops 134217728 | bytes 786432 | tf_op jit(solution)/shard_map/pallas_call | solution.py:439
  38.2 0.8 %shard_map.127 = (bf16[128,1024]{1,0:T(8,128)(2,1)S(1)}, f32[8,128]{1,0:T(8,128)S(1)}, bf16[128,1024]{1,0:T(8,128)(2,1)S(1)}) custom-call(s32[1]{0:T(128)} %bitcast.index_ref, bf16[128,1024]{1,0:T(8,128)(2,1)S(1)} %collective-permute-done.1.enter_ref, f32[128,1024]{1,0:T(8,128)S(1)} %get-tuple-element.60.first_ref, ...), custom_call_target="tpu_custom_call" | custom-call | flops 67108864 | bytes 1048576 | tf_op jit(solution)/shard_map/pallas_call | solution.py:492
  39.0 1.5 %collective-permute-start.3 = (bf16[128,1024]{1,0:T(8,128)(2,1)S(1)}, bf16[128,1024]{1,0:T(8,128)(2,1)S(1)}, u32[]{:S(2)}, u32[]{:S(2)}) collective-permute-start(bf16[128,1024]{1,0:T(8,128)(2,1)S(1)} %get-tuple-element.68), channel_id=1, source_target_pairs={{0,8},{8,16},{16,24},{24,0},{1,9},{9,17},{17,25},{25,1},{2,10},{10... | collective-permute-start | bytes 786440 | tf_op jit(solution)/shard_map/ppermute | solution.py:328
  40.5 2.5 %collective-permute-start.10 = (bf16[128,1024]{1,0:T(8,128)(2,1)S(1)}, bf16[128,1024]{1,0:T(8,128)(2,1)S(1)}, u32[]{:S(2)}, u32[]{:S(2)}) collective-permute-start(bf16[128,1024]{1,0:T(8,128)(2,1)S(1)} %get-tuple-element.77), channel_id=1, source_target_pairs={{0,2},{2,0},{4,6},{6,4},{1,3},{3,1},{5,7},{7,5},{8,10},{10,8},{12,... | collective-permute-start | bytes 786440 | tf_op jit(solution)/shard_map/ppermute | solution.py:509
  43.0 4.3 %collective-permute-done.4.enter_ref = bf16[128,1024]{1,0:T(8,128)(2,1)S(1)} collective-permute-done((bf16[128,1024]{1,0:T(8,128)(2,1)S(1)}, bf16[128,1024]{1,0:T(8,128)(2,1)S(1)}, u32[]{:S(2)}, u32[]{:S(2)}) %collective-permute-start.4) | collective-permute-done | bytes 262176 | tf_op jit(solution)/shard_map/ppermute | solution.py:428
  47.3 0.8 %shard_map.129 = (bf16[128,1024]{1,0:T(8,128)(2,1)S(1)}, f32[8,128]{1,0:T(8,128)S(1)}, bf16[128,1024]{1,0:T(8,128)(2,1)S(1)}) custom-call(s32[1]{0:T(128)} %bitcast.index_ref, bf16[128,1024]{1,0:T(8,128)(2,1)S(1)} %collective-permute-done.4.enter_ref, f32[128,1024]{1,0:T(8,128)S(1)} %get-tuple-element.74.first_ref, ...), custom_call_target="tpu_custom_call" | custom-call | flops 67108864 | bytes 1048576 | tf_op jit(solution)/shard_map/pallas_call | solution.py:492
  48.0 1.4 %collective-permute-start.9 = (bf16[128,1024]{1,0:T(8,128)(2,1)S(1)}, bf16[128,1024]{1,0:T(8,128)(2,1)S(1)}, u32[]{:S(2)}, u32[]{:S(2)}) collective-permute-start(bf16[128,1024]{1,0:T(8,128)(2,1)S(1)} %get-tuple-element.76), channel_id=1, source_target_pairs={{0,8},{8,16},{16,24},{24,0},{1,9},{9,17},{17,25},{25,1},{2,10},{10... | collective-permute-start | bytes 786440 | tf_op jit(solution)/shard_map/ppermute | solution.py:328
  49.5 2.4 %collective-permute-start.12 = (bf16[128,1024]{1,0:T(8,128)(2,1)S(1)}, bf16[128,1024]{1,0:T(8,128)(2,1)S(1)}, u32[]{:S(2)}, u32[]{:S(2)}) collective-permute-start(bf16[128,1024]{1,0:T(8,128)(2,1)S(1)} %get-tuple-element.83), channel_id=1, source_target_pairs={{0,2},{2,0},{4,6},{6,4},{1,3},{3,1},{5,7},{7,5},{8,10},{10,8},{12,... | collective-permute-start | bytes 786440 | tf_op jit(solution)/shard_map/ppermute | solution.py:509
  51.9 3.6 %shard_map.130 = (f32[4,128,1024]{2,1,0:T(8,128)S(1)}, f32[4,2,1024]{2,1,0:T(2,128)S(1)}) custom-call(s32[1]{0:T(128)} %bitcast.index_ref, s32[1]{0:T(128)} %collective-permute-done.6.source_ref, bf16[128,4096]{1,0:T(8,128)(2,1)S(1)} %collective-permute-done.7.q_ref, bf16[128,1024]{1,0:T(8,128)(2,1)S(1)} %collective-permute-done.5.refs_0_.refs_2_, ...), custom_call_target="tpu_custom_call" | custom-call | flops 536870912 | bytes 4194304 | tf_op jit(solution)/shard_map/pallas_call | solution.py:471
  56.3 1.8 %collective-permute-start.11 = (bf16[128,1024]{1,0:T(8,128)(2,1)S(1)}, bf16[128,1024]{1,0:T(8,128)(2,1)S(1)}, u32[]{:S(2)}, u32[]{:S(2)}) collective-permute-start(bf16[128,1024]{1,0:T(8,128)(2,1)S(1)} %get-tuple-element.82), channel_id=1, source_target_pairs={{0,8},{8,16},{16,24},{24,0},{1,9},{9,17},{17,25},{25,1},{2,10},{10... | collective-permute-start | bytes 786440 | tf_op jit(solution)/shard_map/ppermute | solution.py:328
  58.1 1.4 %collective-permute-done.16.refs_0_.refs_2_ = bf16[128,1024]{1,0:T(8,128)(2,1)S(1)} collective-permute-done((bf16[128,1024]{1,0:T(8,128)(2,1)S(1)}, bf16[128,1024]{1,0:T(8,128)(2,1)S(1)}, u32[]{:S(2)}, u32[]{:S(2)}) %collective-permute-start.16) | collective-permute-done | bytes 262176 | tf_op jit(solution)/shard_map/ppermute | solution.py:462
  59.8 2.0 %collective-permute-done.12.raw_ref = bf16[128,1024]{1,0:T(8,128)(2,1)S(1)} collective-permute-done((bf16[128,1024]{1,0:T(8,128)(2,1)S(1)}, bf16[128,1024]{1,0:T(8,128)(2,1)S(1)}, u32[]{:S(2)}, u32[]{:S(2)}) %collective-permute-start.12) | collective-permute-done | bytes 262176 | tf_op jit(solution)/shard_map/ppermute | solution.py:509
  62.2 1.8 %collective-permute-start.13 = (bf16[128,1024]{1,0:T(8,128)(2,1)S(1)}, bf16[128,1024]{1,0:T(8,128)(2,1)S(1)}, u32[]{:S(2)}, u32[]{:S(2)}) collective-permute-start(bf16[128,1024]{1,0:T(8,128)(2,1)S(1)} %get-tuple-element.85), channel_id=1, source_target_pairs={{0,8},{8,16},{16,24},{24,0},{1,9},{9,17},{17,25},{25,1},{2,10},{10... | collective-permute-start | bytes 786440 | tf_op jit(solution)/shard_map/ppermute | solution.py:328
  64.1 1.2 %collective-permute-done.14 = f32[8,128]{1,0:T(8,128)S(1)} collective-permute-done((f32[8,128]{1,0:T(8,128)S(1)}, f32[8,128]{1,0:T(8,128)S(1)}, u32[]{:S(2)}, u32[]{:S(2)}) %collective-permute-start.14) | collective-permute-done | bytes 4128 | tf_op jit(solution)/shard_map/ppermute | solution.py:542
  65.9 4.6 %shard_map.134 = bf16[128,4096]{1,0:T(8,128)(2,1)} custom-call(s32[1]{0:T(128)} %bitcast.index_ref, s32[1]{0:T(128)} %collective-permute-done.6.source_ref, bf16[128,4096]{1,0:T(8,128)(2,1)S(1)} %collective-permute-done.7.q_ref, bf16[128,1024]{1,0:T(8,128)(2,1)S(1)} %collective-permute-done.16.refs_0_.refs_2_, ...), custom_call_target="tpu_custom_call" | custom-call | flops 536870912 | bytes 4194304 | tf_op jit(solution)/shard_map/pallas_call | solution.py:471
  70.5 1.4 %shard_map.133 = bf16[128,4096]{1,0:T(8,128)(2,1)} custom-call(s32[1]{0:T(128)} %bitcast.index_ref, bf16[128,1024]{1,0:T(8,128)(2,1)S(1)} %collective-permute-done.3.refs_0_, bf16[128,1024]{1,0:T(8,128)(2,1)S(1)} %collective-permute-done.9.refs_1_, bf16[128,1024]{1,0:T(8,128)(2,1)S(1)} %collective-permute-done.11.refs_2_, ...), custom_call_target="tpu_custom_call" | custom-call | flops 524288 | bytes 2097152 | tf_op jit(solution)/shard_map/pallas_call | solution.py:544
  (35 shorter events, 2.7 us)
Async XLA Ops:
  0.6 8.3 %copy-start.1 = (bf16[1,128,4096]{2,1,0:T(8,128)(2,1)S(1)}, bf16[1,128,4096]{2,1,0:T(8,128)(2,1)}, u32[]{:S(2)}) copy-start(bf16[1,128,4096]{2,1,0:T(8,128)(2,1)} %param.11) | copy-start | bytes 3145732
  2.9 19.9 %copy-start.6 = (f32[1,64]{1,0:T(1,128)S(1)}, f32[1,64]{1,0:T(1,128)}, u32[]{:S(2)}) copy-start(f32[1,64]{1,0:T(1,128)} %get-tuple-element.54.skip_ref) | copy-start | bytes 772
  2.9 12.0 %collective-permute-start = (bf16[128,1408]{1,0:T(8,128)(2,1)}, bf16[128,1408]{1,0:T(8,128)(2,1)S(1)}, u32[]{:S(2)}, u32[]{:S(2)}) collective-permute-start(bf16[128,1408]{1,0:T(8,128)(2,1)} %get-tuple-element.47), channel_id=1, source_target_pairs={{0,2},{2,0},{4,6},{6,4},{1,3},{3,1},{5,7},{7,5},{8,10},{10,8},{12,... | collective-permute-start | bytes 1081352 | tf_op jit(solution)/shard_map/ppermute | solution.py:396
  6.0 8.9 %collective-permute-start.5 = (bf16[128,1024]{1,0:T(8,128)(2,1)}, bf16[128,1024]{1,0:T(8,128)(2,1)S(1)}, u32[]{:S(2)}, u32[]{:S(2)}) collective-permute-start(bf16[128,1024]{1,0:T(8,128)(2,1)} %get-tuple-element.70), channel_id=1, source_target_pairs={{0,8},{8,16},{16,24},{24,0},{1,9},{9,17},{17,25},{25,1},{2,10},{10... | collective-permute-start | bytes 786440 | tf_op jit(solution)/shard_map/ppermute | solution.py:328
  7.5 7.4 %collective-permute-start.6 = (s32[1]{0:T(128)}, s32[1]{0:T(128)}, u32[]{:S(2)}, u32[]{:S(2)}) collective-permute-start(s32[1]{0:T(128)} %param.21), channel_id=1, source_target_pairs={{0,8},{8,16},{16,24},{24,0},{1,9},{9,17},{17,25},{25,1},{2,10},{10... | collective-permute-start | bytes 20 | tf_op jit(solution)/shard_map/ppermute | solution.py:328
  9.0 0.8 %copy-start.2 = (bf16[1,128,256]{2,1,0:T(8,128)(2,1)S(1)}, bf16[1,128,256]{2,1,0:T(8,128)(2,1)}, u32[]{:S(2)}) copy-start(bf16[1,128,256]{2,1,0:T(8,128)(2,1)} %param.14) | copy-start | bytes 196612
  9.8 0.7 copy-start.3
  10.5 8.1 %copy-start.7 = (bf16[128,1024]{1,0:T(8,128)(2,1)S(1)}, bf16[128,1024]{1,0:T(8,128)(2,1)}, u32[]{:S(2)}) copy-start(bf16[128,1024]{1,0:T(8,128)(2,1)} %get-tuple-element.61) | copy-start | bytes 786436
  14.9 32.4 %collective-permute-start.7 = (bf16[128,4096]{1,0:T(8,128)(2,1)}, bf16[128,4096]{1,0:T(8,128)(2,1)S(1)}, u32[]{:S(2)}, u32[]{:S(2)}) collective-permute-start(bf16[128,4096]{1,0:T(8,128)(2,1)} %bitcast.32), channel_id=1, source_target_pairs={{0,8},{8,16},{16,24},{24,0},{1,9},{9,17},{17,25},{25,1},{2,10},{10... | collective-permute-start | bytes 3145736 | tf_op jit(solution)/shard_map/ppermute | solution.py:328
  16.3 0.6 copy-start.5
  18.6 15.1 %collective-permute-start.2 = (bf16[128,1024]{1,0:T(8,128)(2,1)S(1)}, bf16[128,1024]{1,0:T(8,128)(2,1)S(1)}, u32[]{:S(2)}, u32[]{:S(2)}) collective-permute-start(bf16[128,1024]{1,0:T(8,128)(2,1)S(1)} %copy-done.7), channel_id=1, source_target_pairs={{0,2},{2,0},{4,6},{6,4},{1,3},{3,1},{5,7},{7,5},{8,10},{10,8},{12,... | collective-permute-start | bytes 786440 | tf_op jit(solution)/shard_map/ppermute | solution.py:435
  20.2 18.0 %collective-permute-start.1 = (bf16[128,1024]{1,0:T(8,128)(2,1)S(1)}, bf16[128,1024]{1,0:T(8,128)(2,1)S(1)}, u32[]{:S(2)}, u32[]{:S(2)}) collective-permute-start(bf16[128,1024]{1,0:T(8,128)(2,1)S(1)} %get-tuple-element.53), channel_id=1, source_target_pairs={{0,4},{2,6},{4,0},{6,2},{1,5},{3,7},{5,1},{7,3},{8,12},{10,14},{12... | collective-permute-start | bytes 786440 | tf_op jit(solution)/shard_map/ppermute | solution.py:428
  22.8 15.4 %copy-start = (bf16[1,128,4096]{2,1,0:T(8,128)(2,1)S(1)}, bf16[1,128,4096]{2,1,0:T(8,128)(2,1)}, u32[]{:S(2)}) copy-start(bf16[1,128,4096]{2,1,0:T(8,128)(2,1)} %param.12) | copy-start | bytes 3145732
  24.9 18.0 %collective-permute-start.8 = (bf16[128,1024]{1,0:T(8,128)(2,1)S(1)}, bf16[128,1024]{1,0:T(8,128)(2,1)S(1)}, u32[]{:S(2)}, u32[]{:S(2)}) collective-permute-start(bf16[128,1024]{1,0:T(8,128)(2,1)S(1)} %collective-permute-done.5.refs_0_.refs_2_), channel_id=1, source_target_pairs={{0,2},{2,0},{4,6},{6,4},{1,3},{3,1},{5,7},{7,5},{8,10},{10,8},{12,... | collective-permute-start | bytes 786440 | tf_op jit(solution)/shard_map/ppermute | solution.py:456
  35.6 11.7 %collective-permute-start.4 = (bf16[128,1024]{1,0:T(8,128)(2,1)S(1)}, bf16[128,1024]{1,0:T(8,128)(2,1)S(1)}, u32[]{:S(2)}, u32[]{:S(2)}) collective-permute-start(bf16[128,1024]{1,0:T(8,128)(2,1)S(1)} %get-tuple-element.69), channel_id=1, source_target_pairs={{0,4},{2,6},{4,0},{6,2},{1,5},{3,7},{5,1},{7,3},{8,12},{10,14},{12... | collective-permute-start | bytes 786440 | tf_op jit(solution)/shard_map/ppermute | solution.py:428
  39.0 16.5 %collective-permute-start.3 = (bf16[128,1024]{1,0:T(8,128)(2,1)S(1)}, bf16[128,1024]{1,0:T(8,128)(2,1)S(1)}, u32[]{:S(2)}, u32[]{:S(2)}) collective-permute-start(bf16[128,1024]{1,0:T(8,128)(2,1)S(1)} %get-tuple-element.68), channel_id=1, source_target_pairs={{0,8},{8,16},{16,24},{24,0},{1,9},{9,17},{17,25},{25,1},{2,10},{10... | collective-permute-start | bytes 786440 | tf_op jit(solution)/shard_map/ppermute | solution.py:328
  40.5 15.0 %collective-permute-start.10 = (bf16[128,1024]{1,0:T(8,128)(2,1)S(1)}, bf16[128,1024]{1,0:T(8,128)(2,1)S(1)}, u32[]{:S(2)}, u32[]{:S(2)}) collective-permute-start(bf16[128,1024]{1,0:T(8,128)(2,1)S(1)} %get-tuple-element.77), channel_id=1, source_target_pairs={{0,2},{2,0},{4,6},{6,4},{1,3},{3,1},{5,7},{7,5},{8,10},{10,8},{12,... | collective-permute-start | bytes 786440 | tf_op jit(solution)/shard_map/ppermute | solution.py:509
  48.0 7.8 %collective-permute-start.9 = (bf16[128,1024]{1,0:T(8,128)(2,1)S(1)}, bf16[128,1024]{1,0:T(8,128)(2,1)S(1)}, u32[]{:S(2)}, u32[]{:S(2)}) collective-permute-start(bf16[128,1024]{1,0:T(8,128)(2,1)S(1)} %get-tuple-element.76), channel_id=1, source_target_pairs={{0,8},{8,16},{16,24},{24,0},{1,9},{9,17},{17,25},{25,1},{2,10},{10... | collective-permute-start | bytes 786440 | tf_op jit(solution)/shard_map/ppermute | solution.py:328
  49.4 10.1 %collective-permute-start.16 = (bf16[128,1024]{1,0:T(8,128)(2,1)S(1)}, bf16[128,1024]{1,0:T(8,128)(2,1)S(1)}, u32[]{:S(2)}, u32[]{:S(2)}) collective-permute-start(bf16[128,1024]{1,0:T(8,128)(2,1)S(1)} %collective-permute-done.5.refs_0_.refs_2_), channel_id=1, source_target_pairs={{0,4},{2,6},{4,0},{6,2},{1,5},{3,7},{5,1},{7,3},{8,12},{10,14},{12... | collective-permute-start | bytes 786440 | tf_op jit(solution)/shard_map/ppermute | solution.py:462
  49.5 12.4 %collective-permute-start.12 = (bf16[128,1024]{1,0:T(8,128)(2,1)S(1)}, bf16[128,1024]{1,0:T(8,128)(2,1)S(1)}, u32[]{:S(2)}, u32[]{:S(2)}) collective-permute-start(bf16[128,1024]{1,0:T(8,128)(2,1)S(1)} %get-tuple-element.83), channel_id=1, source_target_pairs={{0,2},{2,0},{4,6},{6,4},{1,3},{3,1},{5,7},{7,5},{8,10},{10,8},{12,... | collective-permute-start | bytes 786440 | tf_op jit(solution)/shard_map/ppermute | solution.py:509
  56.3 9.3 %collective-permute-start.11 = (bf16[128,1024]{1,0:T(8,128)(2,1)S(1)}, bf16[128,1024]{1,0:T(8,128)(2,1)S(1)}, u32[]{:S(2)}, u32[]{:S(2)}) collective-permute-start(bf16[128,1024]{1,0:T(8,128)(2,1)S(1)} %get-tuple-element.82), channel_id=1, source_target_pairs={{0,8},{8,16},{16,24},{24,0},{1,9},{9,17},{17,25},{25,1},{2,10},{10... | collective-permute-start | bytes 786440 | tf_op jit(solution)/shard_map/ppermute | solution.py:328
  59.5 6.4 %collective-permute-start.17 = (bf16[128,1024]{1,0:T(8,128)(2,1)S(1)}, bf16[128,1024]{1,0:T(8,128)(2,1)S(1)}, u32[]{:S(2)}, u32[]{:S(2)}) collective-permute-start(bf16[128,1024]{1,0:T(8,128)(2,1)S(1)} %collective-permute-done.16.refs_0_.refs_2_), channel_id=1, source_target_pairs={{0,2},{2,0},{4,6},{6,4},{1,3},{3,1},{5,7},{7,5},{8,10},{10,8},{12,... | collective-permute-start | bytes 786440 | tf_op jit(solution)/shard_map/ppermute | solution.py:466
  62.2 8.2 %collective-permute-start.13 = (bf16[128,1024]{1,0:T(8,128)(2,1)S(1)}, bf16[128,1024]{1,0:T(8,128)(2,1)S(1)}, u32[]{:S(2)}, u32[]{:S(2)}) collective-permute-start(bf16[128,1024]{1,0:T(8,128)(2,1)S(1)} %get-tuple-element.85), channel_id=1, source_target_pairs={{0,8},{8,16},{16,24},{24,0},{1,9},{9,17},{17,25},{25,1},{2,10},{10... | collective-permute-start | bytes 786440 | tf_op jit(solution)/shard_map/ppermute | solution.py:328
  64.1 1.2 %collective-permute-start.14 = (f32[8,128]{1,0:T(8,128)S(1)}, f32[8,128]{1,0:T(8,128)S(1)}, u32[]{:S(2)}, u32[]{:S(2)}) collective-permute-start(f32[8,128]{1,0:T(8,128)S(1)} %add_add_fusion), channel_id=1, source_target_pairs={{0,1},{1,0},{2,3},{3,2},{4,5},{5,4},{6,7},{7,6},{8,9},{9,8},{10,11... | collective-permute-start | bytes 12296 | tf_op jit(solution)/shard_map/ppermute | solution.py:542
  65.2 5.2 %copy-start.4 = (f32[4096]{0:T(1024)S(1)}, f32[4096]{0:T(1024)}, u32[]{:S(2)}) copy-start(f32[4096]{0:T(1024)} %param.17) | copy-start | bytes 49156
  65.2 5.2 %collective-permute-start.15 = (f32[8,128]{1,0:T(8,128)S(1)}, f32[8,128]{1,0:T(8,128)S(1)}, u32[]{:S(2)}, u32[]{:S(2)}) collective-permute-start(f32[8,128]{1,0:T(8,128)S(1)} %add.15), channel_id=1, source_target_pairs={{0,8},{8,16},{16,24},{24,0},{1,9},{9,17},{17,25},{25,1},{2,10},{10... | collective-permute-start | bytes 12296 | tf_op jit(solution)/shard_map/ppermute | solution.py:328

commit v6 on v5

--- a/solution.py
+++ b/solution.py
@@ -295,7 +295,8 @@
         rest[1][0, 0:1, :] = jnp.concatenate(tops, axis=1)
         rest[1][0, 1:2, :] = jnp.concatenate(totals, axis=1)
         return
-    mixed = (mixed + rest[0][0] * jnp.concatenate(olds, axis=1)) / jnp.concatenate(totals, axis=1)
+    scale = 1.0 / jnp.concatenate(totals, axis=1)
+    mixed = mixed * scale + rest[0][0] * (jnp.concatenate(olds, axis=1) * scale)
     for head in range(GROUP):
         rest[2][:, span(head)] = jnp.transpose(mixed[:, part(head)]).astype(jnp.bfloat16)
 

time: 72.2 us -> 72.2 us (level)
  no operation moved by 1% of the time
where the time goes in v6:
time: 72.2 us; the launch traced here: 71.9 us
  starting transfers between devices  24.6 us (34%)
  Pallas kernels  22.4 us (31%)
  waiting for transfers between devices  22.1 us (31%)
  local copies, waits for them, and re-layouts  2.17 us (3%)
  between operations  0.75 us (1%)
    ppermute x8, starting transfers between devices, hand(): return lax.ppermute(array, 'segment', onward)  11.2 us
    ppermute x1, waiting for transfers between devices, on_device(): got.append(lax.ppermute(after(parcels[chunk + 1], first), 'ctx', partner))  8.28 us
    pallas_call x2, Pallas kernels, attend(): call(functools.partial(attention_kernel, offsets), out_shape, 4 * rows *...  8.18 us
    ppermute x2, starting transfers between devices, on_device(): back.append(lax.ppermute(away, 'ctx', partner))  4.92 us
    ppermute x8, waiting for transfers between devices, hand(): return lax.ppermute(array, 'segment', onward)  4.58 us
    pallas_call x2, Pallas kernels, on_device(): indexed(functools.partial(inner_kernel, chunk), (shape((rows, width), f32...  4.43 us
    ppermute x2, waiting for transfers between devices, on_device(): enter = lax.ppermute(state, 'ctx', further)  4.32 us
    pallas_call x2, Pallas kernels, on_device(): indexed(functools.partial(state_kernel, chunk), (shape((NST, width), wire...  3.62 us
  transfers between devices with their start and end apart: 18, of which 8 were waited for; matrix products, arithmetic and copies ran while one was open for 0% of the time, Pallas kernels for 26%

profile of v6, /device:TPU:0, one launch (start us, length us, event | category | flops | bytes accessed | tf_op | source)
XLA Modules:
  0.0 71.9 jit_solution(4688611625365581178)
XLA Ops:
  0.6 2.2 %shard_map.122 = (bf16[128,1408]{1,0:T(8,128)(2,1)}, bf16[128,1024]{1,0:T(8,128)(2,1)}, bf16[128,1024]{1,0:T(8,128)(2,1)}, f32[1,64]{1,0:T(1,128)}, f32[1,64]{1,0:T(1,128)}) custom-call(s32[1]{0:T(128)} %bitcast.index_ref, bf16[128,4096]{1,0:T(8,128)(2,1)} %bitcast.19, bf16[128,256]{1,0:T(8,128)(2,1)} %bitcast.21, bf16[64,128]{1,0:T(8,128)(2,1)} %bitcast.23, ...), custom_call_target="tpu_custom_call" | custom-call | bytes 1048576 | tf_op jit(solution)/shard_map/pallas_call | solution.py:372
  2.9 3.1 %collective-permute-start = (bf16[128,1408]{1,0:T(8,128)(2,1)}, bf16[128,1408]{1,0:T(8,128)(2,1)S(1)}, u32[]{:S(2)}, u32[]{:S(2)}) collective-permute-start(bf16[128,1408]{1,0:T(8,128)(2,1)} %get-tuple-element.47), channel_id=1, source_target_pairs={{0,2},{2,0},{4,6},{6,4},{1,3},{3,1},{5,7},{7,5},{8,10},{10,8},{12,... | collective-permute-start | bytes 1081352 | tf_op jit(solution)/shard_map/ppermute | solution.py:397
  6.0 1.5 %collective-permute-start.5 = (bf16[128,1024]{1,0:T(8,128)(2,1)}, bf16[128,1024]{1,0:T(8,128)(2,1)S(1)}, u32[]{:S(2)}, u32[]{:S(2)}) collective-permute-start(bf16[128,1024]{1,0:T(8,128)(2,1)} %get-tuple-element.70), channel_id=1, source_target_pairs={{0,8},{8,16},{16,24},{24,0},{1,9},{9,17},{17,25},{25,1},{2,10},{10... | collective-permute-start | bytes 786440 | tf_op jit(solution)/shard_map/ppermute | solution.py:329
  7.5 1.5 %collective-permute-start.6 = (s32[1]{0:T(128)}, s32[1]{0:T(128)}, u32[]{:S(2)}, u32[]{:S(2)}) collective-permute-start(s32[1]{0:T(128)} %param.21), channel_id=1, source_target_pairs={{0,8},{8,16},{16,24},{24,0},{1,9},{9,17},{17,25},{25,1},{2,10},{10... | collective-permute-start | bytes 20 | tf_op jit(solution)/shard_map/ppermute | solution.py:329
  9.0 0.8 %copy-done.2 = bf16[1,128,256]{2,1,0:T(8,128)(2,1)S(1)} copy-done((bf16[1,128,256]{2,1,0:T(8,128)(2,1)S(1)}, bf16[1,128,256]{2,1,0:T(8,128)(2,1)}, u32[]{:S(2)}) %copy-start.2) | copy-done | bytes 65560
  9.8 0.7 copy-done.3
  10.7 4.2 %collective-permute-done.6.source_ref = s32[1]{0:T(128)} collective-permute-done((s32[1]{0:T(128)}, s32[1]{0:T(128)}, u32[]{:S(2)}, u32[]{:S(2)}) %collective-permute-start.6) | collective-permute-done | bytes 36 | tf_op jit(solution)/shard_map/ppermute | solution.py:329
  14.9 1.4 %collective-permute-start.7 = (bf16[128,4096]{1,0:T(8,128)(2,1)}, bf16[128,4096]{1,0:T(8,128)(2,1)S(1)}, u32[]{:S(2)}, u32[]{:S(2)}) collective-permute-start(bf16[128,4096]{1,0:T(8,128)(2,1)} %bitcast.32), channel_id=1, source_target_pairs={{0,8},{8,16},{16,24},{24,0},{1,9},{9,17},{17,25},{25,1},{2,10},{10... | collective-permute-start | bytes 3145736 | tf_op jit(solution)/shard_map/ppermute | solution.py:329
  16.3 0.6 copy-done.5
  16.8 1.8 %shard_map.124 = (bf16[128,1024]{1,0:T(8,128)(2,1)S(1)}, f32[128,1024]{1,0:T(8,128)S(1)}, f32[1,1024]{1,0:T(1,128)S(1)}, f32[1,1024]{1,0:T(1,128)}) custom-call(s32[1]{0:T(128)} %bitcast.index_ref, bf16[128,2048]{1,0:T(8,128)(2,1)S(1)} %get-tuple-element.49.x_ref, bf16[128,1408]{1,0:T(8,128)(2,1)S(1)} %collective-permute-done.x2_ref.dt2_ref.b2_ref.maps2_ref.c2_ref, ...), custom_call_target="tpu_custom_call" | custom-call | flops 67108864 | bytes 524288 | tf_op jit(solution)/shard_map/pallas_call | solution.py:421
  18.6 1.6 %collective-permute-start.2 = (bf16[128,1024]{1,0:T(8,128)(2,1)S(1)}, bf16[128,1024]{1,0:T(8,128)(2,1)S(1)}, u32[]{:S(2)}, u32[]{:S(2)}) collective-permute-start(bf16[128,1024]{1,0:T(8,128)(2,1)S(1)} %copy-done.7), channel_id=1, source_target_pairs={{0,2},{2,0},{4,6},{6,4},{1,3},{3,1},{5,7},{7,5},{8,10},{10,8},{12,... | collective-permute-start | bytes 786440 | tf_op jit(solution)/shard_map/ppermute | solution.py:436
  20.2 2.6 %collective-permute-start.1 = (bf16[128,1024]{1,0:T(8,128)(2,1)S(1)}, bf16[128,1024]{1,0:T(8,128)(2,1)S(1)}, u32[]{:S(2)}, u32[]{:S(2)}) collective-permute-start(bf16[128,1024]{1,0:T(8,128)(2,1)S(1)} %get-tuple-element.53), channel_id=1, source_target_pairs={{0,4},{2,6},{4,0},{6,2},{1,5},{3,7},{5,1},{7,3},{8,12},{10,14},{12... | collective-permute-start | bytes 786440 | tf_op jit(solution)/shard_map/ppermute | solution.py:429
  22.8 2.2 %shard_map.125 = (f32[128,1024]{1,0:T(8,128)S(1)}, f32[128,1024]{1,0:T(8,128)S(1)}, f32[128,1024]{1,0:T(8,128)S(1)}, f32[128,1024]{1,0:T(8,128)S(1)}) custom-call(s32[1]{0:T(128)} %bitcast.index_ref, bf16[128,2048]{1,0:T(8,128)(2,1)S(1)} %get-tuple-element.49.x_ref, bf16[128,1408]{1,0:T(8,128)(2,1)S(1)} %collective-permute-done.x2_ref.dt2_ref.b2_ref.maps2_ref.c2_ref, ...), custom_call_target="tpu_custom_call" | custom-call | flops 134217728 | bytes 786432 | tf_op jit(solution)/shard_map/pallas_call | solution.py:440
  24.9 0.5 collective-permute-start.8
  25.5 8.3 %collective-permute-done.2.x2_ref = bf16[128,1024]{1,0:T(8,128)(2,1)S(1)} collective-permute-done((bf16[128,1024]{1,0:T(8,128)(2,1)S(1)}, bf16[128,1024]{1,0:T(8,128)(2,1)S(1)}, u32[]{:S(2)}, u32[]{:S(2)}) %collective-permute-start.2) | collective-permute-done | bytes 262176 | tf_op jit(solution)/shard_map/ppermute | solution.py:436
  33.7 1.9 %shard_map.128 = (bf16[128,1024]{1,0:T(8,128)(2,1)S(1)}, f32[128,1024]{1,0:T(8,128)S(1)}, f32[1,1024]{1,0:T(1,128)S(1)}, f32[1,1024]{1,0:T(1,128)}) custom-call(s32[1]{0:T(128)} %bitcast.index_ref, bf16[128,2048]{1,0:T(8,128)(2,1)S(1)} %get-tuple-element.49.x_ref, bf16[128,1024]{1,0:T(8,128)(2,1)S(1)} %collective-permute-done.2.x2_ref, ...), custom_call_target="tpu_custom_call" | custom-call | flops 67108864 | bytes 524288 | tf_op jit(solution)/shard_map/pallas_call | solution.py:421
  35.9 2.3 %shard_map.126 = (f32[128,1024]{1,0:T(8,128)S(1)}, f32[128,1024]{1,0:T(8,128)S(1)}, f32[128,1024]{1,0:T(8,128)S(1)}, f32[128,1024]{1,0:T(8,128)S(1)}) custom-call(s32[1]{0:T(128)} %bitcast.index_ref, bf16[128,2048]{1,0:T(8,128)(2,1)S(1)} %get-tuple-element.49.x_ref, bf16[128,1024]{1,0:T(8,128)(2,1)S(1)} %collective-permute-done.2.x2_ref, ...), custom_call_target="tpu_custom_call" | custom-call | flops 134217728 | bytes 786432 | tf_op jit(solution)/shard_map/pallas_call | solution.py:440
  38.2 0.8 %shard_map.127 = (bf16[128,1024]{1,0:T(8,128)(2,1)S(1)}, f32[8,128]{1,0:T(8,128)S(1)}, bf16[128,1024]{1,0:T(8,128)(2,1)S(1)}) custom-call(s32[1]{0:T(128)} %bitcast.index_ref, bf16[128,1024]{1,0:T(8,128)(2,1)S(1)} %collective-permute-done.1.enter_ref, f32[128,1024]{1,0:T(8,128)S(1)} %get-tuple-element.60.first_ref, ...), custom_call_target="tpu_custom_call" | custom-call | flops 67108864 | bytes 1048576 | tf_op jit(solution)/shard_map/pallas_call | solution.py:493
  39.0 1.5 %collective-permute-start.3 = (bf16[128,1024]{1,0:T(8,128)(2,1)S(1)}, bf16[128,1024]{1,0:T(8,128)(2,1)S(1)}, u32[]{:S(2)}, u32[]{:S(2)}) collective-permute-start(bf16[128,1024]{1,0:T(8,128)(2,1)S(1)} %get-tuple-element.68), channel_id=1, source_target_pairs={{0,8},{8,16},{16,24},{24,0},{1,9},{9,17},{17,25},{25,1},{2,10},{10... | collective-permute-start | bytes 786440 | tf_op jit(solution)/shard_map/ppermute | solution.py:329
  40.5 2.5 %collective-permute-start.10 = (bf16[128,1024]{1,0:T(8,128)(2,1)S(1)}, bf16[128,1024]{1,0:T(8,128)(2,1)S(1)}, u32[]{:S(2)}, u32[]{:S(2)}) collective-permute-start(bf16[128,1024]{1,0:T(8,128)(2,1)S(1)} %get-tuple-element.77), channel_id=1, source_target_pairs={{0,2},{2,0},{4,6},{6,4},{1,3},{3,1},{5,7},{7,5},{8,10},{10,8},{12,... | collective-permute-start | bytes 786440 | tf_op jit(solution)/shard_map/ppermute | solution.py:510
  43.0 4.3 %collective-permute-done.4.enter_ref = bf16[128,1024]{1,0:T(8,128)(2,1)S(1)} collective-permute-done((bf16[128,1024]{1,0:T(8,128)(2,1)S(1)}, bf16[128,1024]{1,0:T(8,128)(2,1)S(1)}, u32[]{:S(2)}, u32[]{:S(2)}) %collective-permute-start.4) | collective-permute-done | bytes 262176 | tf_op jit(solution)/shard_map/ppermute | solution.py:429
  47.3 0.8 %shard_map.129 = (bf16[128,1024]{1,0:T(8,128)(2,1)S(1)}, f32[8,128]{1,0:T(8,128)S(1)}, bf16[128,1024]{1,0:T(8,128)(2,1)S(1)}) custom-call(s32[1]{0:T(128)} %bitcast.index_ref, bf16[128,1024]{1,0:T(8,128)(2,1)S(1)} %collective-permute-done.4.enter_ref, f32[128,1024]{1,0:T(8,128)S(1)} %get-tuple-element.74.first_ref, ...), custom_call_target="tpu_custom_call" | custom-call | flops 67108864 | bytes 1048576 | tf_op jit(solution)/shard_map/pallas_call | solution.py:493
  48.0 1.4 %collective-permute-start.9 = (bf16[128,1024]{1,0:T(8,128)(2,1)S(1)}, bf16[128,1024]{1,0:T(8,128)(2,1)S(1)}, u32[]{:S(2)}, u32[]{:S(2)}) collective-permute-start(bf16[128,1024]{1,0:T(8,128)(2,1)S(1)} %get-tuple-element.76), channel_id=1, source_target_pairs={{0,8},{8,16},{16,24},{24,0},{1,9},{9,17},{17,25},{25,1},{2,10},{10... | collective-permute-start | bytes 786440 | tf_op jit(solution)/shard_map/ppermute | solution.py:329
  49.5 2.4 %collective-permute-start.12 = (bf16[128,1024]{1,0:T(8,128)(2,1)S(1)}, bf16[128,1024]{1,0:T(8,128)(2,1)S(1)}, u32[]{:S(2)}, u32[]{:S(2)}) collective-permute-start(bf16[128,1024]{1,0:T(8,128)(2,1)S(1)} %get-tuple-element.83), channel_id=1, source_target_pairs={{0,2},{2,0},{4,6},{6,4},{1,3},{3,1},{5,7},{7,5},{8,10},{10,8},{12,... | collective-permute-start | bytes 786440 | tf_op jit(solution)/shard_map/ppermute | solution.py:510
  51.9 3.6 %shard_map.130 = (f32[4,128,1024]{2,1,0:T(8,128)S(1)}, f32[4,2,1024]{2,1,0:T(2,128)S(1)}) custom-call(s32[1]{0:T(128)} %bitcast.index_ref, s32[1]{0:T(128)} %collective-permute-done.6.source_ref, bf16[128,4096]{1,0:T(8,128)(2,1)S(1)} %collective-permute-done.7.q_ref, bf16[128,1024]{1,0:T(8,128)(2,1)S(1)} %collective-permute-done.5.refs_0_.refs_2_, ...), custom_call_target="tpu_custom_call" | custom-call | flops 536870912 | bytes 4194304 | tf_op jit(solution)/shard_map/pallas_call | solution.py:472
  56.3 1.8 %collective-permute-start.11 = (bf16[128,1024]{1,0:T(8,128)(2,1)S(1)}, bf16[128,1024]{1,0:T(8,128)(2,1)S(1)}, u32[]{:S(2)}, u32[]{:S(2)}) collective-permute-start(bf16[128,1024]{1,0:T(8,128)(2,1)S(1)} %get-tuple-element.82), channel_id=1, source_target_pairs={{0,8},{8,16},{16,24},{24,0},{1,9},{9,17},{17,25},{25,1},{2,10},{10... | collective-permute-start | bytes 786440 | tf_op jit(solution)/shard_map/ppermute | solution.py:329
  58.1 1.4 %collective-permute-done.16.refs_0_.refs_2_ = bf16[128,1024]{1,0:T(8,128)(2,1)S(1)} collective-permute-done((bf16[128,1024]{1,0:T(8,128)(2,1)S(1)}, bf16[128,1024]{1,0:T(8,128)(2,1)S(1)}, u32[]{:S(2)}, u32[]{:S(2)}) %collective-permute-start.16) | collective-permute-done | bytes 262176 | tf_op jit(solution)/shard_map/ppermute | solution.py:463
  59.8 2.0 %collective-permute-done.12.raw_ref = bf16[128,1024]{1,0:T(8,128)(2,1)S(1)} collective-permute-done((bf16[128,1024]{1,0:T(8,128)(2,1)S(1)}, bf16[128,1024]{1,0:T(8,128)(2,1)S(1)}, u32[]{:S(2)}, u32[]{:S(2)}) %collective-permute-start.12) | collective-permute-done | bytes 262176 | tf_op jit(solution)/shard_map/ppermute | solution.py:510
  62.2 1.8 %collective-permute-start.13 = (bf16[128,1024]{1,0:T(8,128)(2,1)S(1)}, bf16[128,1024]{1,0:T(8,128)(2,1)S(1)}, u32[]{:S(2)}, u32[]{:S(2)}) collective-permute-start(bf16[128,1024]{1,0:T(8,128)(2,1)S(1)} %get-tuple-element.85), channel_id=1, source_target_pairs={{0,8},{8,16},{16,24},{24,0},{1,9},{9,17},{17,25},{25,1},{2,10},{10... | collective-permute-start | bytes 786440 | tf_op jit(solution)/shard_map/ppermute | solution.py:329
  64.1 1.2 %collective-permute-done.14 = f32[8,128]{1,0:T(8,128)S(1)} collective-permute-done((f32[8,128]{1,0:T(8,128)S(1)}, f32[8,128]{1,0:T(8,128)S(1)}, u32[]{:S(2)}, u32[]{:S(2)}) %collective-permute-start.14) | collective-permute-done | bytes 4128 | tf_op jit(solution)/shard_map/ppermute | solution.py:543
  65.9 4.6 %shard_map.134 = bf16[128,4096]{1,0:T(8,128)(2,1)} custom-call(s32[1]{0:T(128)} %bitcast.index_ref, s32[1]{0:T(128)} %collective-permute-done.6.source_ref, bf16[128,4096]{1,0:T(8,128)(2,1)S(1)} %collective-permute-done.7.q_ref, bf16[128,1024]{1,0:T(8,128)(2,1)S(1)} %collective-permute-done.16.refs_0_.refs_2_, ...), custom_call_target="tpu_custom_call" | custom-call | flops 536870912 | bytes 4194304 | tf_op jit(solution)/shard_map/pallas_call | solution.py:472
  70.5 1.4 %shard_map.133 = bf16[128,4096]{1,0:T(8,128)(2,1)} custom-call(s32[1]{0:T(128)} %bitcast.index_ref, bf16[128,1024]{1,0:T(8,128)(2,1)S(1)} %collective-permute-done.3.refs_0_, bf16[128,1024]{1,0:T(8,128)(2,1)S(1)} %collective-permute-done.9.refs_1_, bf16[128,1024]{1,0:T(8,128)(2,1)S(1)} %collective-permute-done.11.refs_2_, ...), custom_call_target="tpu_custom_call" | custom-call | flops 524288 | bytes 2097152 | tf_op jit(solution)/shard_map/pallas_call | solution.py:545
  (35 shorter events, 2.7 us)
Async XLA Ops:
  0.6 8.3 %copy-start.1 = (bf16[1,128,4096]{2,1,0:T(8,128)(2,1)S(1)}, bf16[1,128,4096]{2,1,0:T(8,128)(2,1)}, u32[]{:S(2)}) copy-start(bf16[1,128,4096]{2,1,0:T(8,128)(2,1)} %param.11) | copy-start | bytes 3145732
  2.9 19.9 %copy-start.6 = (f32[1,64]{1,0:T(1,128)S(1)}, f32[1,64]{1,0:T(1,128)}, u32[]{:S(2)}) copy-start(f32[1,64]{1,0:T(1,128)} %get-tuple-element.54.skip_ref) | copy-start | bytes 772
  2.9 12.0 %collective-permute-start = (bf16[128,1408]{1,0:T(8,128)(2,1)}, bf16[128,1408]{1,0:T(8,128)(2,1)S(1)}, u32[]{:S(2)}, u32[]{:S(2)}) collective-permute-start(bf16[128,1408]{1,0:T(8,128)(2,1)} %get-tuple-element.47), channel_id=1, source_target_pairs={{0,2},{2,0},{4,6},{6,4},{1,3},{3,1},{5,7},{7,5},{8,10},{10,8},{12,... | collective-permute-start | bytes 1081352 | tf_op jit(solution)/shard_map/ppermute | solution.py:397
  6.0 8.9 %collective-permute-start.5 = (bf16[128,1024]{1,0:T(8,128)(2,1)}, bf16[128,1024]{1,0:T(8,128)(2,1)S(1)}, u32[]{:S(2)}, u32[]{:S(2)}) collective-permute-start(bf16[128,1024]{1,0:T(8,128)(2,1)} %get-tuple-element.70), channel_id=1, source_target_pairs={{0,8},{8,16},{16,24},{24,0},{1,9},{9,17},{17,25},{25,1},{2,10},{10... | collective-permute-start | bytes 786440 | tf_op jit(solution)/shard_map/ppermute | solution.py:329
  7.5 7.4 %collective-permute-start.6 = (s32[1]{0:T(128)}, s32[1]{0:T(128)}, u32[]{:S(2)}, u32[]{:S(2)}) collective-permute-start(s32[1]{0:T(128)} %param.21), channel_id=1, source_target_pairs={{0,8},{8,16},{16,24},{24,0},{1,9},{9,17},{17,25},{25,1},{2,10},{10... | collective-permute-start | bytes 20 | tf_op jit(solution)/shard_map/ppermute | solution.py:329
  9.0 0.8 %copy-start.2 = (bf16[1,128,256]{2,1,0:T(8,128)(2,1)S(1)}, bf16[1,128,256]{2,1,0:T(8,128)(2,1)}, u32[]{:S(2)}) copy-start(bf16[1,128,256]{2,1,0:T(8,128)(2,1)} %param.14) | copy-start | bytes 196612
  9.8 0.7 copy-start.3
  10.5 8.1 %copy-start.7 = (bf16[128,1024]{1,0:T(8,128)(2,1)S(1)}, bf16[128,1024]{1,0:T(8,128)(2,1)}, u32[]{:S(2)}) copy-start(bf16[128,1024]{1,0:T(8,128)(2,1)} %get-tuple-element.61) | copy-start | bytes 786436
  14.9 32.4 %collective-permute-start.7 = (bf16[128,4096]{1,0:T(8,128)(2,1)}, bf16[128,4096]{1,0:T(8,128)(2,1)S(1)}, u32[]{:S(2)}, u32[]{:S(2)}) collective-permute-start(bf16[128,4096]{1,0:T(8,128)(2,1)} %bitcast.32), channel_id=1, source_target_pairs={{0,8},{8,16},{16,24},{24,0},{1,9},{9,17},{17,25},{25,1},{2,10},{10... | collective-permute-start | bytes 3145736 | tf_op jit(solution)/shard_map/ppermute | solution.py:329
  16.3 0.6 copy-start.5
  18.6 15.1 %collective-permute-start.2 = (bf16[128,1024]{1,0:T(8,128)(2,1)S(1)}, bf16[128,1024]{1,0:T(8,128)(2,1)S(1)}, u32[]{:S(2)}, u32[]{:S(2)}) collective-permute-start(bf16[128,1024]{1,0:T(8,128)(2,1)S(1)} %copy-done.7), channel_id=1, source_target_pairs={{0,2},{2,0},{4,6},{6,4},{1,3},{3,1},{5,7},{7,5},{8,10},{10,8},{12,... | collective-permute-start | bytes 786440 | tf_op jit(solution)/shard_map/ppermute | solution.py:436
  20.2 18.0 %collective-permute-start.1 = (bf16[128,1024]{1,0:T(8,128)(2,1)S(1)}, bf16[128,1024]{1,0:T(8,128)(2,1)S(1)}, u32[]{:S(2)}, u32[]{:S(2)}) collective-permute-start(bf16[128,1024]{1,0:T(8,128)(2,1)S(1)} %get-tuple-element.53), channel_id=1, source_target_pairs={{0,4},{2,6},{4,0},{6,2},{1,5},{3,7},{5,1},{7,3},{8,12},{10,14},{12... | collective-permute-start | bytes 786440 | tf_op jit(solution)/shard_map/ppermute | solution.py:429
  22.8 15.4 %copy-start = (bf16[1,128,4096]{2,1,0:T(8,128)(2,1)S(1)}, bf16[1,128,4096]{2,1,0:T(8,128)(2,1)}, u32[]{:S(2)}) copy-start(bf16[1,128,4096]{2,1,0:T(8,128)(2,1)} %param.12) | copy-start | bytes 3145732
  24.9 18.0 %collective-permute-start.8 = (bf16[128,1024]{1,0:T(8,128)(2,1)S(1)}, bf16[128,1024]{1,0:T(8,128)(2,1)S(1)}, u32[]{:S(2)}, u32[]{:S(2)}) collective-permute-start(bf16[128,1024]{1,0:T(8,128)(2,1)S(1)} %collective-permute-done.5.refs_0_.refs_2_), channel_id=1, source_target_pairs={{0,2},{2,0},{4,6},{6,4},{1,3},{3,1},{5,7},{7,5},{8,10},{10,8},{12,... | collective-permute-start | bytes 786440 | tf_op jit(solution)/shard_map/ppermute | solution.py:457
  35.6 11.7 %collective-permute-start.4 = (bf16[128,1024]{1,0:T(8,128)(2,1)S(1)}, bf16[128,1024]{1,0:T(8,128)(2,1)S(1)}, u32[]{:S(2)}, u32[]{:S(2)}) collective-permute-start(bf16[128,1024]{1,0:T(8,128)(2,1)S(1)} %get-tuple-element.69), channel_id=1, source_target_pairs={{0,4},{2,6},{4,0},{6,2},{1,5},{3,7},{5,1},{7,3},{8,12},{10,14},{12... | collective-permute-start | bytes 786440 | tf_op jit(solution)/shard_map/ppermute | solution.py:429
  39.0 16.5 %collective-permute-start.3 = (bf16[128,1024]{1,0:T(8,128)(2,1)S(1)}, bf16[128,1024]{1,0:T(8,128)(2,1)S(1)}, u32[]{:S(2)}, u32[]{:S(2)}) collective-permute-start(bf16[128,1024]{1,0:T(8,128)(2,1)S(1)} %get-tuple-element.68), channel_id=1, source_target_pairs={{0,8},{8,16},{16,24},{24,0},{1,9},{9,17},{17,25},{25,1},{2,10},{10... | collective-permute-start | bytes 786440 | tf_op jit(solution)/shard_map/ppermute | solution.py:329
  40.5 15.0 %collective-permute-start.10 = (bf16[128,1024]{1,0:T(8,128)(2,1)S(1)}, bf16[128,1024]{1,0:T(8,128)(2,1)S(1)}, u32[]{:S(2)}, u32[]{:S(2)}) collective-permute-start(bf16[128,1024]{1,0:T(8,128)(2,1)S(1)} %get-tuple-element.77), channel_id=1, source_target_pairs={{0,2},{2,0},{4,6},{6,4},{1,3},{3,1},{5,7},{7,5},{8,10},{10,8},{12,... | collective-permute-start | bytes 786440 | tf_op jit(solution)/shard_map/ppermute | solution.py:510
  48.0 7.8 %collective-permute-start.9 = (bf16[128,1024]{1,0:T(8,128)(2,1)S(1)}, bf16[128,1024]{1,0:T(8,128)(2,1)S(1)}, u32[]{:S(2)}, u32[]{:S(2)}) collective-permute-start(bf16[128,1024]{1,0:T(8,128)(2,1)S(1)} %get-tuple-element.76), channel_id=1, source_target_pairs={{0,8},{8,16},{16,24},{24,0},{1,9},{9,17},{17,25},{25,1},{2,10},{10... | collective-permute-start | bytes 786440 | tf_op jit(solution)/shard_map/ppermute | solution.py:329
  49.4 10.1 %collective-permute-start.16 = (bf16[128,1024]{1,0:T(8,128)(2,1)S(1)}, bf16[128,1024]{1,0:T(8,128)(2,1)S(1)}, u32[]{:S(2)}, u32[]{:S(2)}) collective-permute-start(bf16[128,1024]{1,0:T(8,128)(2,1)S(1)} %collective-permute-done.5.refs_0_.refs_2_), channel_id=1, source_target_pairs={{0,4},{2,6},{4,0},{6,2},{1,5},{3,7},{5,1},{7,3},{8,12},{10,14},{12... | collective-permute-start | bytes 786440 | tf_op jit(solution)/shard_map/ppermute | solution.py:463
  49.5 12.4 %collective-permute-start.12 = (bf16[128,1024]{1,0:T(8,128)(2,1)S(1)}, bf16[128,1024]{1,0:T(8,128)(2,1)S(1)}, u32[]{:S(2)}, u32[]{:S(2)}) collective-permute-start(bf16[128,1024]{1,0:T(8,128)(2,1)S(1)} %get-tuple-element.83), channel_id=1, source_target_pairs={{0,2},{2,0},{4,6},{6,4},{1,3},{3,1},{5,7},{7,5},{8,10},{10,8},{12,... | collective-permute-start | bytes 786440 | tf_op jit(solution)/shard_map/ppermute | solution.py:510
  56.3 9.3 %collective-permute-start.11 = (bf16[128,1024]{1,0:T(8,128)(2,1)S(1)}, bf16[128,1024]{1,0:T(8,128)(2,1)S(1)}, u32[]{:S(2)}, u32[]{:S(2)}) collective-permute-start(bf16[128,1024]{1,0:T(8,128)(2,1)S(1)} %get-tuple-element.82), channel_id=1, source_target_pairs={{0,8},{8,16},{16,24},{24,0},{1,9},{9,17},{17,25},{25,1},{2,10},{10... | collective-permute-start | bytes 786440 | tf_op jit(solution)/shard_map/ppermute | solution.py:329
  59.5 6.4 %collective-permute-start.17 = (bf16[128,1024]{1,0:T(8,128)(2,1)S(1)}, bf16[128,1024]{1,0:T(8,128)(2,1)S(1)}, u32[]{:S(2)}, u32[]{:S(2)}) collective-permute-start(bf16[128,1024]{1,0:T(8,128)(2,1)S(1)} %collective-permute-done.16.refs_0_.refs_2_), channel_id=1, source_target_pairs={{0,2},{2,0},{4,6},{6,4},{1,3},{3,1},{5,7},{7,5},{8,10},{10,8},{12,... | collective-permute-start | bytes 786440 | tf_op jit(solution)/shard_map/ppermute | solution.py:467
  62.2 8.3 %collective-permute-start.13 = (bf16[128,1024]{1,0:T(8,128)(2,1)S(1)}, bf16[128,1024]{1,0:T(8,128)(2,1)S(1)}, u32[]{:S(2)}, u32[]{:S(2)}) collective-permute-start(bf16[128,1024]{1,0:T(8,128)(2,1)S(1)} %get-tuple-element.85), channel_id=1, source_target_pairs={{0,8},{8,16},{16,24},{24,0},{1,9},{9,17},{17,25},{25,1},{2,10},{10... | collective-permute-start | bytes 786440 | tf_op jit(solution)/shard_map/ppermute | solution.py:329
  64.1 1.2 %collective-permute-start.14 = (f32[8,128]{1,0:T(8,128)S(1)}, f32[8,128]{1,0:T(8,128)S(1)}, u32[]{:S(2)}, u32[]{:S(2)}) collective-permute-start(f32[8,128]{1,0:T(8,128)S(1)} %add_add_fusion), channel_id=1, source_target_pairs={{0,1},{1,0},{2,3},{3,2},{4,5},{5,4},{6,7},{7,6},{8,9},{9,8},{10,11... | collective-permute-start | bytes 12296 | tf_op jit(solution)/shard_map/ppermute | solution.py:543
  65.2 5.3 %copy-start.4 = (f32[4096]{0:T(1024)S(1)}, f32[4096]{0:T(1024)}, u32[]{:S(2)}) copy-start(f32[4096]{0:T(1024)} %param.17) | copy-start | bytes 49156
  65.2 5.3 %collective-permute-start.15 = (f32[8,128]{1,0:T(8,128)S(1)}, f32[8,128]{1,0:T(8,128)S(1)}, u32[]{:S(2)}, u32[]{:S(2)}) collective-permute-start(f32[8,128]{1,0:T(8,128)S(1)} %add.15), channel_id=1, source_target_pairs={{0,8},{8,16},{16,24},{24,0},{1,9},{9,17},{17,25},{25,1},{2,10},{10... | collective-permute-start | bytes 12296 | tf_op jit(solution)/shard_map/ppermute | solution.py:329
